TPU v7x, 512 devices: a whole 4x8x8 slice. The times are simulated.
512 devices in a mesh: fsdp: 32 (over z, y_lo, core), mp: 16 (over y_hi, x).
Axes of the slice: x: 4, y: 8 (y_hi: 4, y_lo: 2; y = y_hi * 2 + y_lo), z: 8, core: 2. Of those that a mesh axis runs over, the one named last changes fastest.
Arguments:
- normed_tokens: bfloat16 [8192, 6144], P('fsdp', 'mp'), may hold values from -6 to 6
- up_weight: bfloat16 [6144, 12288], P('fsdp', 'mp'), may hold values from -0.078125 to 0.078125
- adapter_down: bfloat16 [6144, 64], replicated, may hold values from -0.078125 to 0.078125
- adapter_up: bfloat16 [64, 12288], replicated, may hold values from -0.0546875 to 0.0546875
- act_grad: bfloat16 [8192, 12288], P('fsdp', 'mp'), may hold values from -3 to 3
Outputs:
- normed_grad: bfloat16 [8192, 6144], P('fsdp', 'mp')
- down_grad: bfloat16 [6144, 64], P('mp')
- up_grad: bfloat16 [64, 12288], P(None, 'mp')
All inputs are finite; a program needn't handle non-finite values.
Results may differ from a plain program's by a relative error of at most 0.019.
Values may be sent and summed in bfloat16 or wider, within the bound.
No kernel may reach another device: no remote copies, remote signals or barrier semaphores. Data moves between devices by JAX's collectives and lax.ppermute only.
A program may use at most 64 MiB of HBM per device.

v0:
```python
import jax
import jax.numpy as jnp
from jax import lax
from jax.sharding import PartitionSpec as P

adapter_scale = 2.0


def gelu_slope(preact):
    normal_cdf = 0.5 * (1.0 + jax.scipy.special.erf(preact * 0.7071067811865476))
    density = jnp.exp(-0.5 * preact * preact) * 0.3989422804014327
    return normal_cdf + preact * density


def contract(left, right, left_dim, right_dim):
    return lax.dot_general(
        left, right, (((left_dim,), (right_dim,)), ((), ())), preferred_element_type=jnp.float32
    )


def body(normed_tokens, up_weight, adapter_down, adapter_up, act_grad):
    tok_rows, local_width = normed_tokens.shape
    hidden_cols = up_weight.shape[1]
    model_index = lax.axis_index("mp")
    whole_rows = lax.all_gather(normed_tokens, "mp", axis=1, tiled=True)
    lowrank = jnp.dot(whole_rows, adapter_down, preferred_element_type=jnp.float32).astype(
        jnp.bfloat16
    )
    up_columns = lax.dynamic_slice_in_dim(adapter_up, model_index * hidden_cols, hidden_cols, 1)
    down_rows = lax.dynamic_slice_in_dim(adapter_down, model_index * local_width, local_width, 0)
    gathered = lax.all_gather(up_weight, "fsdp", axis=0, tiled=True)
    frozen_pre = jnp.dot(whole_rows, gathered, preferred_element_type=jnp.float32)
    preact = frozen_pre + adapter_scale * jnp.dot(
        lowrank, up_columns, preferred_element_type=jnp.float32
    )
    slope_grad = (act_grad.astype(jnp.float32) * gelu_slope(preact)).astype(jnp.bfloat16)
    up_local = adapter_scale * contract(lowrank, slope_grad, 0, 0)
    up_grad = lax.psum(up_local, "fsdp").astype(jnp.bfloat16)
    rank_part = adapter_scale * contract(slope_grad, up_columns, 1, 1)
    rank_grad = lax.psum(rank_part, "mp").astype(jnp.bfloat16)
    frozen_term = contract(slope_grad, gathered, 1, 1)
    summed = lax.psum_scatter(
        frozen_term.astype(jnp.bfloat16), "mp", scatter_dimension=1, tiled=True
    ).astype(jnp.float32)
    normed_grad = (summed + contract(rank_grad, down_rows, 1, 1)).astype(jnp.bfloat16)
    down_local = contract(normed_tokens, rank_grad, 0, 0)
    down_grad = lax.psum(down_local, "fsdp").astype(jnp.bfloat16)
    return (normed_grad, down_grad, up_grad)


def solution(mesh):
    placed = (P("fsdp", "mp"), P("fsdp", "mp"), P(), P(), P("fsdp", "mp"))
    return jax.shard_map(
        body,
        mesh=mesh,
        in_specs=placed,
        out_specs=(P("fsdp", "mp"), P("mp", None), P(None, "mp")),
        check_vma=False,
    )
```

profile of v0, /device:TPU:1, one launch (start us, length us, event | category | flops | bytes accessed | tf_op | source)
XLA Modules:
  0.0 386.2 jit_solution(5962823337677233679)
XLA Ops:
  7.2 0.0 copy-start
  7.2 0.0 all-gather.3.cloned.1.call-start
  7.2 0.7 all-gather.3.cloned.1.call-update
  7.9 0.0 all-gather.5.cloned.1.call-start
  8.0 0.7 all-gather.5.cloned.1.call-update
  8.7 0.0 reduce-scatter.4.cloned.1.call-start
  8.7 85.8 %all-gather.3.cloned.1.call-done = bf16[256,6144]{1,0:T(8,128)(2,1)} async-done(((bf16[256,384]{1,0:T(8,128)(2,1)}), bf16[256,6144]{1,0:T(8,128)(2,1)}) %all-gather.3.cloned.1.call-update) | async-done | bytes 3145744 | tf_op jit(solution)/shard_map/all_gather | solution.py:25
  94.5 3.2 convolution_convert_fusion.1
  97.6 74.2 %all-gather.5.cloned.1.call-done = bf16[6144,768]{1,0:T(8,128)(2,1)} async-done(((bf16[192,768]{1,0:T(8,128)(2,1)}), bf16[6144,768]{1,0:T(8,128)(2,1)}) %all-gather.5.cloned.1.call-update) | async-done | bytes 9437200 | tf_op jit(solution)/shard_map/all_gather | solution.py:31
  171.8 7.4 %fusion.16 = f32[256,768]{1,0:T(8,128)S(1)} fusion(bf16[256,6144]{1,0:T(8,128)(2,1)} %all-gather.3.cloned.1.call-done, bf16[6144,768]{1,0:T(8,128)(2,1)} %all-gather.5.cloned.1.call-done), kind=kOutput, calls=%fused_computation.24 | convolution fusion | flops 2415919104 | bytes 13369344 | tf_op jit(solution)/shard_map/dot_general | solution.py:32
  179.2 0.0 copy-done
  179.2 0.0 copy-done.3
  179.2 0.6 fusion.7
  179.8 0.0 copy-done.2
  179.8 4.1 %convolution_convert_fusion = bf16[256,6144]{1,0:T(8,128)(2,1)} fusion(bf16[256,768]{1,0:T(8,128)(2,1)S(1)} %fusion.7, bf16[6144,768]{1,0:T(8,128)(2,1)S(1)} %copy-done.2), kind=kOutput, calls=%fused_computation | convolution fusion | flops 2417491968 | bytes 12976128 | tf_op jit(solution)/shard_map/dot_general | solution.py:16
  183.9 4.7 %copy.8 = bf16[256,6144]{0,1:T(8,128)(2,1)} copy(bf16[256,6144]{1,0:T(8,128)(2,1)} %convolution_convert_fusion) | data formatting | bytes 6291456
  188.6 0.0 reduce-scatter.4.cloned.1.call-update
  188.6 0.3 convolution_multiply_fusion.2
  188.9 69.0 %psum.21 = bf16[256,64]{0,1:T(8,128)(2,1)S(1)} all-reduce(f32[256,64]{0,1:T(8,128)S(1)} %convolution_multiply_fusion.2), channel_id=1, replica_groups=mesh['fsdp'=32,'mp'=16] {'mp'}, use_global_device_ids=true, to_apply=%region_1.0 | all-reduce | flops 16384 | bytes 98304 | tf_op jit(solution)/shard_map/psum | solution.py:40
  257.9 0.2 convolution_bitcast_fusion
  258.0 0.2 convolution_multiply_fusion.1
  258.2 118.6 %all-reduce.2 = (bf16[384,64]{0,1:T(8,128)(2,1)}, bf16[64,768]{1,0:T(8,128)(2,1)}) all-reduce(f32[384,64]{0,1:T(8,128)S(1)} %convolution_bitcast_fusion, f32[64,768]{1,0:T(8,128)S(1)} %convolution_multiply_fusion.1), channel_id=1, replica_groups=mesh['fsdp'=32,'mp'=16] {'fsdp'}, use_global_device_ids=true, to_apply=%region_2.0 | all-reduce | flops 73728 | bytes 442368 | tf_op jit(solution)/shard_map/psum | solution.py:47
  376.9 1.1 copy.9
  378.0 1.7 fusion.1
  (5 shorter events, 0.0 us)
Async XLA Ops:
  7.2 172.0 %copy-start = (bf16[64,12288]{1,0:T(8,128)(2,1)S(1)}, bf16[64,12288]{1,0:T(8,128)(2,1)}, u32[]{:S(2)}) copy-start(bf16[64,12288]{1,0:T(8,128)(2,1)} %param.8) | copy-start | bytes 4718596
  7.2 87.3 %all-gather.3.cloned.1.call-start = ((), (), s32[]{:S(2)}) async-start(), calls=%async_computation.1 | async-start | bytes 3342336 | tf_op jit(solution)/shard_map/all_gather | solution.py:25
  7.9 163.9 %all-gather.5.cloned.1.call-start = ((), (), s32[]{:S(2)}) async-start(), calls=%async_computation.2 | async-start | bytes 9732096 | tf_op jit(solution)/shard_map/all_gather | solution.py:31
  8.7 368.2 %reduce-scatter.4.cloned.1.call-start = ((), (), s32[]{:S(2)}) async-start(), calls=%async_computation.3 | async-start | bytes 3342336
  97.6 81.6 %copy-start.3 = (bf16[256,768]{1,0:T(8,128)(2,1)S(1)}, bf16[256,768]{1,0:T(8,128)(2,1)}, u32[]{:S(2)}) copy-start(bf16[256,768]{1,0:T(8,128)(2,1)} %param.9) | copy-start | bytes 1179652
  171.8 8.0 %copy-start.2 = (bf16[6144,768]{1,0:T(8,128)(2,1)S(1)}, bf16[6144,768]{1,0:T(8,128)(2,1)}, u32[]{:S(2)}) copy-start(bf16[6144,768]{1,0:T(8,128)(2,1)} %all-gather.5.cloned.1.call-done) | copy-start | bytes 28311556
  188.6 69.3 %copy-start.1 = (bf16[256,384]{1,0:T(8,128)(2,1)S(1)}, bf16[256,384]{1,0:T(8,128)(2,1)}, u32[]{:S(2)}) copy-start(bf16[256,384]{1,0:T(8,128)(2,1)} %param.5) | copy-start | bytes 589828
Sparse Core Ops, SparseCore 0:
  11.0 83.4 all-gather.2
  96.6 75.1 all-gather.4
  188.7 94.8 reduce-scatter.3
where the time goes:
time: 387 us; the launch traced here: 386 us
  blocking collectives  188 us (49%)
  waiting for transfers between devices  161 us (42%)
  matrix products  17.5 us (5%)
  between operations  13.8 us (4%)
  local copies, waits for them, and re-layouts  5.76 us (1%)
    psum x1, blocking collectives, body(): down_grad = lax.psum(down_local, 'fsdp').astype(jnp.bfloat16)  119 us
    all_gather x1, waiting for transfers between devices, body(): whole_rows = lax.all_gather(normed_tokens, 'mp', axis=1, tiled=True)  85.8 us
    all_gather x1, waiting for transfers between devices, body(): gathered = lax.all_gather(up_weight, 'fsdp', axis=0, tiled=True)  74.2 us
    psum x1, blocking collectives, body(): rank_grad = lax.psum(rank_part, 'mp').astype(jnp.bfloat16)  69 us
  transfers between devices with their start and end apart: 3, of which 2 were waited for; matrix products, arithmetic and copies ran while one was open for 1% of the time, Pallas kernels for 0%

commit v1 on v0

v1 whole, which is shorter than its diff:
```python
import jax
import jax.numpy as jnp
from jax import lax
from jax.sharding import PartitionSpec as P

adapter_scale = 2.0

Z, YL, C = 8, 2, 2
YH, X = 4, 4


def gelu_slope(preact):
    normal_cdf = 0.5 * (1.0 + jax.scipy.special.erf(preact * 0.7071067811865476))
    density = jnp.exp(-0.5 * preact * preact) * 0.3989422804014327
    return normal_cdf + preact * density


def contract(left, right, left_dim, right_dim):
    return lax.dot_general(
        left, right, (((left_dim,), (right_dim,)), ((), ())), preferred_element_type=jnp.float32
    )


def mp_send(value, step):
    pairs = []
    for m in range(YH * X):
        y, x = step(m // X, m % X)
        pairs.append((m, (y % YH) * X + x % X))
    return lax.ppermute(value, "mp", pairs)


def fsdp_send(value, step):
    pairs = []
    for f in range(Z * YL * C):
        z, y, c = step(f // (YL * C), f // C % YL, f % C)
        pairs.append((f, (z % Z) * YL * C + y * C + c))
    return lax.ppermute(value, "fsdp", pairs)


def y_up(value):
    return mp_send(value, lambda y, x: (y + 1, x))


def y_down(value):
    return mp_send(value, lambda y, x: (y - 1, x))


def x_up(value):
    return mp_send(value, lambda y, x: (y, x + 1))


def x_down(value):
    return mp_send(value, lambda y, x: (y, x - 1))


def ring_gather(value, up, down):
    half = value.shape[0] // 2
    previous, following = up(value), down(value)
    opposite = jnp.concatenate([up(previous[:half]), down(following[half:])], axis=0)
    return [value, following, opposite, previous]


def ring_scatter(parts, up, down):
    half = parts[2].shape[0] // 2
    from_previous = up(parts[2][:half])
    from_next = down(parts[2][half:])
    f32 = jnp.float32
    to_next = jnp.concatenate(
        [(parts[1][:half].astype(f32) + from_previous.astype(f32)).astype(jnp.bfloat16), parts[1][half:]], axis=0
    )
    to_previous = jnp.concatenate(
        [parts[3][:half], (parts[3][half:].astype(f32) + from_next.astype(f32)).astype(jnp.bfloat16)], axis=0
    )
    return parts[0].astype(f32) + up(to_next).astype(f32) + down(to_previous).astype(f32)


def sum_mp(value):
    for step in (
        lambda y, x: (y, x ^ 1),
        lambda y, x: (y, 3 - x),
        lambda y, x: (y ^ 1, x),
        lambda y, x: (3 - y, x),
    ):
        value = value + mp_send(value, step)
    return value


def sum_fsdp(value):
    for step in (
        lambda z, y, c: (z, y, c ^ 1),
        lambda z, y, c: (z, y ^ 1, c),
        lambda z, y, c: (z ^ 1, y, c),
        lambda z, y, c: (z ^ 2, y, c),
        lambda z, y, c: (7 - z, y, c),
    ):
        value = value + fsdp_send(value, step)
    return value


def body(normed_tokens, up_weight, adapter_down, adapter_up, act_grad):
    tok_rows, local_width = normed_tokens.shape
    hidden_cols = up_weight.shape[1]
    model_index = lax.axis_index("mp")
    y_hi, x_at = model_index >> 2, model_index & 3

    gathered = lax.all_gather(up_weight, "fsdp", axis=0, tiled=True)

    along_y = jnp.concatenate(ring_gather(normed_tokens, y_up, y_down), axis=1)
    along_x = ring_gather(along_y, x_up, x_down)
    whole_rows = jnp.zeros((tok_rows, local_width * YH * X), jnp.bfloat16)
    for q in range(X):
        for r in range(YH):
            at = (((y_hi + r) & 3) * X + ((x_at + q) & 3)) * local_width
            block = along_x[q][:, r * local_width : (r + 1) * local_width]
            whole_rows = lax.dynamic_update_slice_in_dim(whole_rows, block, at, 1)

    lowrank = jnp.dot(whole_rows, adapter_down, preferred_element_type=jnp.float32).astype(
        jnp.bfloat16
    )
    up_columns = lax.dynamic_slice_in_dim(adapter_up, model_index * hidden_cols, hidden_cols, 1)
    down_rows = lax.dynamic_slice_in_dim(adapter_down, model_index * local_width, local_width, 0)
    frozen_pre = jnp.dot(whole_rows, gathered, preferred_element_type=jnp.float32)
    preact = frozen_pre + adapter_scale * jnp.dot(
        lowrank, up_columns, preferred_element_type=jnp.float32
    )
    slope_grad = (act_grad.astype(jnp.float32) * gelu_slope(preact)).astype(jnp.bfloat16)

    rank_part = adapter_scale * contract(up_columns, slope_grad, 1, 1)
    rank_grad = sum_mp(rank_part).astype(jnp.bfloat16)
    up_local = adapter_scale * contract(lowrank, slope_grad, 0, 0)
    up_grad = sum_fsdp(up_local).astype(jnp.bfloat16)
    down_local = contract(rank_grad, normed_tokens, 1, 0)
    down_grad = sum_fsdp(down_local).astype(jnp.bfloat16).T

    frozen_term = contract(slope_grad, gathered, 1, 1).astype(jnp.bfloat16)
    by_x = []
    for q in range(X):
        blocks = []
        for r in range(YH):
            at = (((y_hi + r) & 3) * X + ((x_at + q) & 3)) * local_width
            blocks.append(lax.dynamic_slice_in_dim(frozen_term, at, local_width, 1))
        by_x.append(jnp.concatenate(blocks, axis=1))
    over_x = ring_scatter(by_x, x_up, x_down).astype(jnp.bfloat16)
    by_y = [over_x[:, r * local_width : (r + 1) * local_width] for r in range(YH)]
    summed = ring_scatter(by_y, y_up, y_down)
    normed_grad = (summed + contract(rank_grad, down_rows, 0, 1)).astype(jnp.bfloat16)
    return (normed_grad, down_grad, up_grad)


def solution(mesh):
    placed = (P("fsdp", "mp"), P("fsdp", "mp"), P(), P(), P("fsdp", "mp"))
    return jax.shard_map(
        body,
        mesh=mesh,
        in_specs=placed,
        out_specs=(P("fsdp", "mp"), P("mp", None), P(None, "mp")),
        check_vma=False,
    )
```

time: 387 us -> 230 us (0.59)
  the two profiles are of different devices: /device:TPU:1 before, /device:TPU:88 now
where the time goes in v1:
time: 230 us; the launch traced here: 229 us
  starting transfers between devices  98.4 us (43%)
  waiting for transfers between devices  81.6 us (35%)
  matrix products  21.1 us (9%)
  between operations  14.9 us (6%)
  other arithmetic  8.49 us (4%)
  local copies, waits for them, and re-layouts  4.19 us (2%)
    ppermute x20, starting transfers between devices, mp_send(): return lax.ppermute(value, 'mp', pairs)  68.2 us
    ppermute x20, waiting for transfers between devices, mp_send(): return lax.ppermute(value, 'mp', pairs)  55.3 us
    ppermute x10, starting transfers between devices, fsdp_send(): return lax.ppermute(value, 'fsdp', pairs)  30.1 us
    all_gather x1, waiting for transfers between devices, body(): gathered = lax.all_gather(up_weight, 'fsdp', axis=0, tiled=True)  13.7 us
    dot_general x5, matrix products, contract(): lax.dot_general(left, right, (((left_dim,), (right_dim,)), ((), ())), pre...  12.3 us
    ppermute x10, waiting for transfers between devices, fsdp_send(): return lax.ppermute(value, 'fsdp', pairs)  11.9 us
    dot_general x1, matrix products, body(): jnp.dot(whole_rows, gathered, preferred_element_type=jnp.float32)  7.42 us
  transfers between devices with their start and end apart: 31, of which 16 were waited for; matrix products, arithmetic and copies ran while one was open for 10% of the time, Pallas kernels for 0%

profile of v1, /device:TPU:88, one launch (start us, length us, event | category | flops | bytes accessed | tf_op | source)
XLA Modules:
  0.0 228.7 jit_solution(14538030277131198688)
XLA Ops:
  7.9 4.8 %collective-permute-start.1 = (bf16[256,384]{1,0:T(8,128)(2,1)}, bf16[256,384]{1,0:T(8,128)(2,1)S(1)}, u32[]{:S(2)}, u32[]{:S(2)}) collective-permute-start(bf16[256,384]{1,0:T(8,128)(2,1)} %param.5), channel_id=1, source_target_pairs={{0,4},{1,5},{2,6},{3,7},{4,8},{5,9},{6,10},{7,11},{8,12},{9,13},{1... | collective-permute-start | bytes 589832 | tf_op jit(solution)/shard_map/ppermute | solution.py:29
  14.7 7.1 %collective-permute-done.1 = bf16[256,384]{1,0:T(8,128)(2,1)S(1)} collective-permute-done((bf16[256,384]{1,0:T(8,128)(2,1)}, bf16[256,384]{1,0:T(8,128)(2,1)S(1)}, u32[]{:S(2)}, u32[]{:S(2)}) %collective-permute-start.1) | collective-permute-done | bytes 196640 | tf_op jit(solution)/shard_map/ppermute | solution.py:29
  21.8 4.9 %collective-permute-start.2 = (bf16[128,384]{1,0:T(8,128)(2,1)S(1)}, bf16[128,384]{1,0:T(8,128)(2,1)S(1)}, u32[]{:S(2)}, u32[]{:S(2)}) collective-permute-start(bf16[128,384]{1,0:T(8,128)(2,1)S(1)} %slice.125), channel_id=1, source_target_pairs={{0,4},{1,5},{2,6},{3,7},{4,8},{5,9},{6,10},{7,11},{8,12},{9,13},{1... | collective-permute-start | bytes 294920 | tf_op jit(solution)/shard_map/ppermute | solution.py:29
  30.8 5.7 %collective-permute-done.3 = bf16[128,384]{1,0:T(8,128)(2,1)S(1)} collective-permute-done((bf16[128,384]{1,0:T(8,128)(2,1)S(1)}, bf16[128,384]{1,0:T(8,128)(2,1)S(1)}, u32[]{:S(2)}, u32[]{:S(2)}) %collective-permute-start.3) | collective-permute-done | bytes 98336 | tf_op jit(solution)/shard_map/ppermute | solution.py:29
  41.9 3.7 %collective-permute-start.4 = (bf16[256,1536]{1,0:T(8,128)(2,1)}, bf16[256,1536]{1,0:T(8,128)(2,1)S(1)}, u32[]{:S(2)}, u32[]{:S(2)}) collective-permute-start(bf16[256,1536]{1,0:T(8,128)(2,1)} %pad_maximum_fusion), channel_id=1, source_target_pairs={{0,3},{1,0},{2,1},{3,2},{4,7},{5,4},{6,5},{7,6},{8,11},{9,8},{10,9... | collective-permute-start | bytes 2359304 | tf_op jit(solution)/shard_map/ppermute | solution.py:29
  46.7 14.0 %collective-permute-done.5 = bf16[256,1536]{1,0:T(8,128)(2,1)S(1)} collective-permute-done((bf16[256,1536]{1,0:T(8,128)(2,1)}, bf16[256,1536]{1,0:T(8,128)(2,1)S(1)}, u32[]{:S(2)}, u32[]{:S(2)}) %collective-permute-start.5) | collective-permute-done | bytes 786464 | tf_op jit(solution)/shard_map/ppermute | solution.py:29
  63.0 5.0 %collective-permute-start.7 = (bf16[128,1536]{1,0:T(8,128)(2,1)S(1)}, bf16[128,1536]{1,0:T(8,128)(2,1)S(1)}, u32[]{:S(2)}, u32[]{:S(2)}) collective-permute-start(bf16[128,1536]{1,0:T(8,128)(2,1)S(1)} %slice.132), channel_id=1, source_target_pairs={{0,3},{1,0},{2,1},{3,2},{4,7},{5,4},{6,5},{7,6},{8,11},{9,8},{10,9... | collective-permute-start | bytes 1179656 | tf_op jit(solution)/shard_map/ppermute | solution.py:29
  68.2 5.2 %collective-permute-done.6 = bf16[128,1536]{1,0:T(8,128)(2,1)S(1)} collective-permute-done((bf16[128,1536]{1,0:T(8,128)(2,1)S(1)}, bf16[128,1536]{1,0:T(8,128)(2,1)S(1)}, u32[]{:S(2)}, u32[]{:S(2)}) %collective-permute-start.6) | collective-permute-done | bytes 393248 | tf_op jit(solution)/shard_map/ppermute | solution.py:29
  78.3 13.7 %all-gather.2.cloned.1.call-done = bf16[6144,768]{1,0:T(8,128)(2,1)} async-done(((bf16[192,768]{1,0:T(8,128)(2,1)}), bf16[6144,768]{1,0:T(8,128)(2,1)}) %all-gather.2.cloned.1.call-update) | async-done | bytes 9437200 | tf_op jit(solution)/shard_map/all_gather | solution.py:106
  92.1 7.4 %fusion.5 = bf16[256,768]{1,0:T(8,128)(2,1)S(1)} fusion(f32[256,768]{1,0:T(8,128)S(1)} %convolution_multiply_fusion, bf16[256,6144]{1,0:T(8,128)(2,1)} %copy-done.1, bf16[6144,768]{1,0:T(8,128)(2,1)} %all-gather.2.cloned.1.call-done, bf16[256,768]{1,0:T(8,128)(2,1)S(1)} %copy-done.8), kind=kOutput, calls=%fused_computation.13 | convolution fusion | flops 2418278400 | bytes 14155776 | tf_op jit(solution)/shard_map/dot_general | solution.py:122
  102.1 3.7 %collective-permute-start.16 = (f32[64,256]{1,0:T(8,128)S(1)}, f32[64,256]{1,0:T(8,128)S(1)}, u32[]{:S(2)}, u32[]{:S(2)}) collective-permute-start(f32[64,256]{1,0:T(8,128)S(1)} %convolution_multiply_fusion.2), channel_id=1, source_target_pairs={{0,1},{1,0},{2,3},{3,2},{4,5},{5,4},{6,7},{7,6},{8,9},{9,8},{10,11... | collective-permute-start | bytes 196616 | tf_op jit(solution)/shard_map/ppermute | solution.py:29
  105.8 10.0 %convolution_convert_fusion = bf16[256,6144]{1,0:T(8,128)(2,1)S(1)} fusion(bf16[256,768]{1,0:T(8,128)(2,1)S(1)} %fusion.5, bf16[6144,768]{1,0:T(8,128)(2,1)} %all-gather.2.cloned.1.call-done), kind=kOutput, calls=%fused_computation | convolution fusion | flops 2417491968 | bytes 12976128 | tf_op jit(solution)/shard_map/dot_general | solution.py:19
  118.7 4.9 %collective-permute-start.17 = (f32[64,256]{1,0:T(8,128)S(1)}, f32[64,256]{1,0:T(8,128)S(1)}, u32[]{:S(2)}, u32[]{:S(2)}) collective-permute-start(f32[64,256]{1,0:T(8,128)S(1)} %add.326), channel_id=1, source_target_pairs={{0,3},{1,2},{2,1},{3,0},{4,7},{5,6},{6,5},{7,4},{8,11},{9,10},{10,... | collective-permute-start | bytes 196616 | tf_op jit(solution)/shard_map/ppermute | solution.py:29
  125.9 6.2 %collective-permute-done.17 = f32[64,256]{1,0:T(8,128)S(1)} collective-permute-done((f32[64,256]{1,0:T(8,128)S(1)}, f32[64,256]{1,0:T(8,128)S(1)}, u32[]{:S(2)}, u32[]{:S(2)}) %collective-permute-start.17) | collective-permute-done | bytes 65568 | tf_op jit(solution)/shard_map/ppermute | solution.py:29
  134.1 5.3 %collective-permute-done.18 = f32[64,256]{1,0:T(8,128)S(1)} collective-permute-done((f32[64,256]{1,0:T(8,128)S(1)}, f32[64,256]{1,0:T(8,128)S(1)}, u32[]{:S(2)}, u32[]{:S(2)}) %collective-permute-start.18) | collective-permute-done | bytes 65568 | tf_op jit(solution)/shard_map/ppermute | solution.py:29
  139.4 4.1 %collective-permute-start.19 = (f32[64,256]{1,0:T(8,128)S(1)}, f32[64,256]{1,0:T(8,128)S(1)}, u32[]{:S(2)}, u32[]{:S(2)}) collective-permute-start(f32[64,256]{1,0:T(8,128)S(1)} %add.328), channel_id=1, source_target_pairs={{0,12},{1,13},{2,14},{3,15},{4,8},{5,9},{6,10},{7,11},{8,4},{9,5},... | collective-permute-start | bytes 196616 | tf_op jit(solution)/shard_map/ppermute | solution.py:29
  150.3 5.1 %collective-permute-start.11 = (bf16[256,1536]{1,0:T(8,128)(2,1)}, bf16[256,1536]{1,0:T(8,128)(2,1)}, u32[]{:S(2)}, u32[]{:S(2)}) collective-permute-start(bf16[256,1536]{1,0:T(8,128)(2,1)} %pad_maximum_fusion.5), channel_id=1, source_target_pairs={{0,3},{1,0},{2,1},{3,2},{4,7},{5,4},{6,5},{7,6},{8,11},{9,8},{10,9... | collective-permute-start | bytes 2359304 | tf_op jit(solution)/shard_map/ppermute | solution.py:29
  167.5 4.6 %collective-permute-done.22 = f32[64,384]{1,0:T(8,128)S(1)} collective-permute-done((f32[64,384]{1,0:T(8,128)S(1)}, f32[64,384]{1,0:T(8,128)S(1)}, u32[]{:S(2)}, u32[]{:S(2)}) %collective-permute-start.22) | collective-permute-done | bytes 98336 | tf_op jit(solution)/shard_map/ppermute | solution.py:37
  172.1 3.6 %collective-permute-start.23 = (f32[64,384]{1,0:T(8,128)S(1)}, f32[64,384]{1,0:T(8,128)}, u32[]{:S(2)}, u32[]{:S(2)}) collective-permute-start(f32[64,384]{1,0:T(8,128)S(1)} %add.334), channel_id=1, source_target_pairs={{0,128},{16,144},{32,160},{48,176},{64,192},{80,208},{96,224},{112... | collective-permute-start | bytes 294920 | tf_op jit(solution)/shard_map/ppermute | solution.py:37
  179.8 4.4 %collective-permute-done.23 = f32[64,384]{1,0:T(8,128)} collective-permute-done((f32[64,384]{1,0:T(8,128)S(1)}, f32[64,384]{1,0:T(8,128)}, u32[]{:S(2)}, u32[]{:S(2)}) %collective-permute-start.23) | collective-permute-done | bytes 98336 | tf_op jit(solution)/shard_map/ppermute | solution.py:37
  188.8 4.6 %collective-permute-start.12 = (bf16[128,384]{1,0:T(8,128)(2,1)S(1)}, bf16[128,384]{1,0:T(8,128)(2,1)S(1)}, u32[]{:S(2)}, u32[]{:S(2)}) collective-permute-start(bf16[128,384]{1,0:T(8,128)(2,1)S(1)} %get-tuple-element.21), channel_id=1, source_target_pairs={{0,4},{1,5},{2,6},{3,7},{4,8},{5,9},{6,10},{7,11},{8,12},{9,13},{1... | collective-permute-start | bytes 294920 | tf_op jit(solution)/shard_map/ppermute | solution.py:29
  196.2 6.9 %collective-permute-start.29 = (f32[64,768]{1,0:T(8,128)S(1)}, f32[64,768]{1,0:T(8,128)S(1)}, u32[]{:S(2)}, u32[]{:S(2)}) collective-permute-start(f32[64,768]{1,0:T(8,128)S(1)} %add.340), channel_id=1, source_target_pairs={{0,448},{16,464},{32,480},{48,496},{64,384},{80,400},{96,416},{112... | collective-permute-start | bytes 589832 | tf_op jit(solution)/shard_map/ppermute | solution.py:37
  203.2 5.8 %collective-permute-start.13 = (bf16[256,384]{1,0:T(8,128)(2,1)S(1)}, bf16[256,384]{1,0:T(8,128)(2,1)S(1)}, u32[]{:S(2)}, u32[]{:S(2)}) collective-permute-start(bf16[256,384]{1,0:T(8,128)(2,1)S(1)} %pad_maximum_fusion.6), channel_id=1, source_target_pairs={{0,4},{1,5},{2,6},{3,7},{4,8},{5,9},{6,10},{7,11},{8,12},{9,13},{1... | collective-permute-start | bytes 589832 | tf_op jit(solution)/shard_map/ppermute | solution.py:29
  212.5 7.6 %collective-permute-done.15 = bf16[256,384]{1,0:T(8,128)(2,1)S(1)} collective-permute-done((bf16[256,384]{1,0:T(8,128)(2,1)S(1)}, bf16[256,384]{1,0:T(8,128)(2,1)S(1)}, u32[]{:S(2)}, u32[]{:S(2)}) %collective-permute-start.15) | collective-permute-done | bytes 196640 | tf_op jit(solution)/shard_map/ppermute | solution.py:29
  (121 shorter events, 65.7 us)
Async XLA Ops:
  7.2 84.9 %all-gather.2.cloned.1.call-start = ((), (), s32[]{:S(2)}) async-start(), calls=%async_computation | async-start | bytes 9732096 | tf_op jit(solution)/shard_map/all_gather | solution.py:106
  7.9 13.8 %collective-permute-start.1 = (bf16[256,384]{1,0:T(8,128)(2,1)}, bf16[256,384]{1,0:T(8,128)(2,1)S(1)}, u32[]{:S(2)}, u32[]{:S(2)}) collective-permute-start(bf16[256,384]{1,0:T(8,128)(2,1)} %param.5), channel_id=1, source_target_pairs={{0,4},{1,5},{2,6},{3,7},{4,8},{5,9},{6,10},{7,11},{8,12},{9,13},{1... | collective-permute-start | bytes 589832 | tf_op jit(solution)/shard_map/ppermute | solution.py:29
  12.7 14.7 %collective-permute-start = (bf16[256,384]{1,0:T(8,128)(2,1)}, bf16[256,384]{1,0:T(8,128)(2,1)S(1)}, u32[]{:S(2)}, u32[]{:S(2)}) collective-permute-start(bf16[256,384]{1,0:T(8,128)(2,1)} %param.5), channel_id=1, source_target_pairs={{0,12},{1,13},{2,14},{3,15},{4,0},{5,1},{6,2},{7,3},{8,4},{9,5},{1... | collective-permute-start | bytes 589832 | tf_op jit(solution)/shard_map/ppermute | solution.py:29
  38.5 22.2 %collective-permute-start.5 = (bf16[256,1536]{1,0:T(8,128)(2,1)}, bf16[256,1536]{1,0:T(8,128)(2,1)S(1)}, u32[]{:S(2)}, u32[]{:S(2)}) collective-permute-start(bf16[256,1536]{1,0:T(8,128)(2,1)} %pad_maximum_fusion), channel_id=1, source_target_pairs={{0,1},{1,2},{2,3},{3,0},{4,5},{5,6},{6,7},{7,4},{8,9},{9,10},{10,1... | collective-permute-start | bytes 2359304 | tf_op jit(solution)/shard_map/ppermute | solution.py:29
  41.9 21.0 %collective-permute-start.4 = (bf16[256,1536]{1,0:T(8,128)(2,1)}, bf16[256,1536]{1,0:T(8,128)(2,1)S(1)}, u32[]{:S(2)}, u32[]{:S(2)}) collective-permute-start(bf16[256,1536]{1,0:T(8,128)(2,1)} %pad_maximum_fusion), channel_id=1, source_target_pairs={{0,3},{1,0},{2,1},{3,2},{4,7},{5,4},{6,5},{7,6},{8,11},{9,8},{10,9... | collective-permute-start | bytes 2359304 | tf_op jit(solution)/shard_map/ppermute | solution.py:29
  60.8 12.7 %collective-permute-start.6 = (bf16[128,1536]{1,0:T(8,128)(2,1)S(1)}, bf16[128,1536]{1,0:T(8,128)(2,1)S(1)}, u32[]{:S(2)}, u32[]{:S(2)}) collective-permute-start(bf16[128,1536]{1,0:T(8,128)(2,1)S(1)} %slice.131), channel_id=1, source_target_pairs={{0,1},{1,2},{2,3},{3,0},{4,5},{5,6},{6,7},{7,4},{8,9},{9,10},{10,1... | collective-permute-start | bytes 1179656 | tf_op jit(solution)/shard_map/ppermute | solution.py:29
  63.0 11.8 %collective-permute-start.7 = (bf16[128,1536]{1,0:T(8,128)(2,1)S(1)}, bf16[128,1536]{1,0:T(8,128)(2,1)S(1)}, u32[]{:S(2)}, u32[]{:S(2)}) collective-permute-start(bf16[128,1536]{1,0:T(8,128)(2,1)S(1)} %slice.132), channel_id=1, source_target_pairs={{0,3},{1,0},{2,1},{3,2},{4,7},{5,4},{6,5},{7,6},{8,11},{9,8},{10,9... | collective-permute-start | bytes 1179656 | tf_op jit(solution)/shard_map/ppermute | solution.py:29
  100.0 43.6 %collective-permute-start.25 = (f32[64,768]{1,0:T(8,128)S(1)}, f32[64,768]{1,0:T(8,128)S(1)}, u32[]{:S(2)}, u32[]{:S(2)}) collective-permute-start(f32[64,768]{1,0:T(8,128)S(1)} %convolution_multiply_fusion.1), channel_id=1, source_target_pairs={{0,16},{16,0},{32,48},{48,32},{64,80},{80,64},{96,112},{112,96},{1... | collective-permute-start | bytes 589832 | tf_op jit(solution)/shard_map/ppermute | solution.py:37
  102.1 16.6 %collective-permute-start.16 = (f32[64,256]{1,0:T(8,128)S(1)}, f32[64,256]{1,0:T(8,128)S(1)}, u32[]{:S(2)}, u32[]{:S(2)}) collective-permute-start(f32[64,256]{1,0:T(8,128)S(1)} %convolution_multiply_fusion.2), channel_id=1, source_target_pairs={{0,1},{1,0},{2,3},{3,2},{4,5},{5,4},{6,7},{7,6},{8,9},{9,8},{10,11... | collective-permute-start | bytes 196616 | tf_op jit(solution)/shard_map/ppermute | solution.py:29
  116.5 30.5 %collective-permute-start.8 = (bf16[128,1536]{1,0:T(8,128)(2,1)S(1)}, bf16[128,1536]{1,0:T(8,128)(2,1)S(1)}, u32[]{:S(2)}, u32[]{:S(2)}) collective-permute-start(bf16[128,1536]{1,0:T(8,128)(2,1)S(1)} %get-tuple-element.25), channel_id=1, source_target_pairs={{0,1},{1,2},{2,3},{3,0},{4,5},{5,6},{6,7},{7,4},{8,9},{9,10},{10,1... | collective-permute-start | bytes 1179656 | tf_op jit(solution)/shard_map/ppermute | solution.py:29
  118.7 13.3 %collective-permute-start.17 = (f32[64,256]{1,0:T(8,128)S(1)}, f32[64,256]{1,0:T(8,128)S(1)}, u32[]{:S(2)}, u32[]{:S(2)}) collective-permute-start(f32[64,256]{1,0:T(8,128)S(1)} %add.326), channel_id=1, source_target_pairs={{0,3},{1,2},{2,1},{3,0},{4,7},{5,6},{6,5},{7,4},{8,11},{9,10},{10,... | collective-permute-start | bytes 196616 | tf_op jit(solution)/shard_map/ppermute | solution.py:29
  123.7 25.5 %collective-permute-start.10 = (bf16[128,1536]{1,0:T(8,128)(2,1)S(1)}, bf16[128,1536]{1,0:T(8,128)(2,1)S(1)}, u32[]{:S(2)}, u32[]{:S(2)}) collective-permute-start(bf16[128,1536]{1,0:T(8,128)(2,1)S(1)} %get-tuple-element.26), channel_id=1, source_target_pairs={{0,3},{1,0},{2,1},{3,2},{4,7},{5,4},{6,5},{7,6},{8,11},{9,8},{10,9... | collective-permute-start | bytes 1179656 | tf_op jit(solution)/shard_map/ppermute | solution.py:29
  139.4 16.0 %collective-permute-start.19 = (f32[64,256]{1,0:T(8,128)S(1)}, f32[64,256]{1,0:T(8,128)S(1)}, u32[]{:S(2)}, u32[]{:S(2)}) collective-permute-start(f32[64,256]{1,0:T(8,128)S(1)} %add.328), channel_id=1, source_target_pairs={{0,12},{1,13},{2,14},{3,15},{4,8},{5,9},{6,10},{7,11},{8,4},{9,5},... | collective-permute-start | bytes 196616 | tf_op jit(solution)/shard_map/ppermute | solution.py:29
  143.5 17.6 %collective-permute-start.26 = (f32[64,768]{1,0:T(8,128)S(1)}, f32[64,768]{1,0:T(8,128)S(1)}, u32[]{:S(2)}, u32[]{:S(2)}) collective-permute-start(f32[64,768]{1,0:T(8,128)S(1)} %add.337), channel_id=1, source_target_pairs={{0,32},{16,48},{32,0},{48,16},{64,96},{80,112},{96,64},{112,80},{1... | collective-permute-start | bytes 589832 | tf_op jit(solution)/shard_map/ppermute | solution.py:37
  147.2 39.8 %collective-permute-start.9 = (bf16[256,1536]{1,0:T(8,128)(2,1)S(1)}, bf16[256,1536]{1,0:T(8,128)(2,1)}, u32[]{:S(2)}, u32[]{:S(2)}) collective-permute-start(bf16[256,1536]{1,0:T(8,128)(2,1)S(1)} %pad_maximum_fusion.3), channel_id=1, source_target_pairs={{0,1},{1,2},{2,3},{3,0},{4,5},{5,6},{6,7},{7,4},{8,9},{9,10},{10,1... | collective-permute-start | bytes 2359304 | tf_op jit(solution)/shard_map/ppermute | solution.py:29
  150.3 36.8 %collective-permute-start.11 = (bf16[256,1536]{1,0:T(8,128)(2,1)}, bf16[256,1536]{1,0:T(8,128)(2,1)}, u32[]{:S(2)}, u32[]{:S(2)}) collective-permute-start(bf16[256,1536]{1,0:T(8,128)(2,1)} %pad_maximum_fusion.5), channel_id=1, source_target_pairs={{0,3},{1,0},{2,1},{3,2},{4,7},{5,4},{6,5},{7,6},{8,11},{9,8},{10,9... | collective-permute-start | bytes 2359304 | tf_op jit(solution)/shard_map/ppermute | solution.py:29
  161.2 14.5 %collective-permute-start.27 = (f32[64,768]{1,0:T(8,128)S(1)}, f32[64,768]{1,0:T(8,128)}, u32[]{:S(2)}, u32[]{:S(2)}) collective-permute-start(f32[64,768]{1,0:T(8,128)S(1)} %add.338), channel_id=1, source_target_pairs={{0,64},{16,80},{32,96},{48,112},{64,0},{80,16},{96,32},{112,48},{1... | collective-permute-start | bytes 589832 | tf_op jit(solution)/shard_map/ppermute | solution.py:37
  172.1 12.1 %collective-permute-start.23 = (f32[64,384]{1,0:T(8,128)S(1)}, f32[64,384]{1,0:T(8,128)}, u32[]{:S(2)}, u32[]{:S(2)}) collective-permute-start(f32[64,384]{1,0:T(8,128)S(1)} %add.334), channel_id=1, source_target_pairs={{0,128},{16,144},{32,160},{48,176},{64,192},{80,208},{96,224},{112... | collective-permute-start | bytes 294920 | tf_op jit(solution)/shard_map/ppermute | solution.py:37
  176.6 19.5 %collective-permute-start.28 = (f32[64,768]{1,0:T(8,128)S(1)}, f32[64,768]{1,0:T(8,128)S(1)}, u32[]{:S(2)}, u32[]{:S(2)}) collective-permute-start(f32[64,768]{1,0:T(8,128)S(1)} %add.339), channel_id=1, source_target_pairs={{0,128},{16,144},{32,160},{48,176},{64,192},{80,208},{96,224},{112... | collective-permute-start | bytes 589832 | tf_op jit(solution)/shard_map/ppermute | solution.py:37
  185.1 10.5 %collective-permute-start.24 = (f32[64,384]{1,0:T(8,128)S(1)}, f32[64,384]{1,0:T(8,128)S(1)}, u32[]{:S(2)}, u32[]{:S(2)}) collective-permute-start(f32[64,384]{1,0:T(8,128)S(1)} %add.335), channel_id=1, source_target_pairs={{0,448},{16,464},{32,480},{48,496},{64,384},{80,400},{96,416},{112... | collective-permute-start | bytes 294920 | tf_op jit(solution)/shard_map/ppermute | solution.py:37
  188.8 14.3 %collective-permute-start.12 = (bf16[128,384]{1,0:T(8,128)(2,1)S(1)}, bf16[128,384]{1,0:T(8,128)(2,1)S(1)}, u32[]{:S(2)}, u32[]{:S(2)}) collective-permute-start(bf16[128,384]{1,0:T(8,128)(2,1)S(1)} %get-tuple-element.21), channel_id=1, source_target_pairs={{0,4},{1,5},{2,6},{3,7},{4,8},{5,9},{6,10},{7,11},{8,12},{9,13},{1... | collective-permute-start | bytes 294920 | tf_op jit(solution)/shard_map/ppermute | solution.py:29
  193.4 9.7 %collective-permute-start.14 = (bf16[128,384]{1,0:T(8,128)(2,1)S(1)}, bf16[128,384]{1,0:T(8,128)(2,1)S(1)}, u32[]{:S(2)}, u32[]{:S(2)}) collective-permute-start(bf16[128,384]{1,0:T(8,128)(2,1)S(1)} %get-tuple-element.22), channel_id=1, source_target_pairs={{0,12},{1,13},{2,14},{3,15},{4,0},{5,1},{6,2},{7,3},{8,4},{9,5},{1... | collective-permute-start | bytes 294920 | tf_op jit(solution)/shard_map/ppermute | solution.py:29
  196.2 14.8 %collective-permute-start.29 = (f32[64,768]{1,0:T(8,128)S(1)}, f32[64,768]{1,0:T(8,128)S(1)}, u32[]{:S(2)}, u32[]{:S(2)}) collective-permute-start(f32[64,768]{1,0:T(8,128)S(1)} %add.340), channel_id=1, source_target_pairs={{0,448},{16,464},{32,480},{48,496},{64,384},{80,400},{96,416},{112... | collective-permute-start | bytes 589832 | tf_op jit(solution)/shard_map/ppermute | solution.py:37
  209.1 11.0 %collective-permute-start.15 = (bf16[256,384]{1,0:T(8,128)(2,1)S(1)}, bf16[256,384]{1,0:T(8,128)(2,1)S(1)}, u32[]{:S(2)}, u32[]{:S(2)}) collective-permute-start(bf16[256,384]{1,0:T(8,128)(2,1)S(1)} %pad_maximum_fusion.7), channel_id=1, source_target_pairs={{0,12},{1,13},{2,14},{3,15},{4,0},{5,1},{6,2},{7,3},{8,4},{9,5},{1... | collective-permute-start | bytes 589832 | tf_op jit(solution)/shard_map/ppermute | solution.py:29
  (16 other events, 212.0 us)
Sparse Core Ops, SparseCore 0:
  10.2 81.8 all-gather.1

commit v2 on v0

v2 whole, which is shorter than its diff:
```python
import functools

import jax
import jax.numpy as jnp
from jax import lax
from jax.experimental import pallas as pl
from jax.experimental.pallas import tpu as pltpu
from jax.sharding import PartitionSpec as P

adapter_scale = 2.0
f32, bf16 = jnp.float32, jnp.bfloat16

Z, YL, C = 8, 2, 2
YH, X = 4, 4


def gelu_slope(preact):
    normal_cdf = 0.5 * (1.0 + lax.erf(preact * 0.7071067811865476))
    density = jnp.exp(-0.5 * preact * preact) * 0.3989422804014327
    return normal_cdf + preact * density


def contract(left, right, left_dim, right_dim):
    return lax.dot_general(
        left, right, (((left_dim,), (right_dim,)), ((), ())), preferred_element_type=f32
    )


def send(value, step):
    pairs = []
    for device in range(Z * YL * C * YH * X):
        f, m = device // (YH * X), device % (YH * X)
        z, yl, c, yh, x = step(f // (YL * C), f // C % YL, f % C, m // X, m % X)
        pairs.append((device, ((z * YL + yl) * C + c) * YH * X + yh * X + x))
    return lax.ppermute(value, ("fsdp", "mp"), pairs)


def first(c):
    return 1 if c else 3


def second(c):
    return 3 if c else 1


y_first = functools.partial(send, step=lambda z, yl, c, yh, x: (z, yl, c, yh ^ first(c), x))
y_second = functools.partial(send, step=lambda z, yl, c, yh, x: (z, yl, c, yh ^ second(c), x))
x_first = functools.partial(send, step=lambda z, yl, c, yh, x: (z, yl, c, yh, x ^ first(c)))
x_second = functools.partial(send, step=lambda z, yl, c, yh, x: (z, yl, c, yh, x ^ second(c)))


def block_copy(table, w, held, sems, p):
    width = w.shape[0] // 16
    source = w.at[pl.ds(pl.multiple_of(table[p] * width, width), width)]
    return pltpu.make_async_copy(source, held.at[pl.ds(p * width, width)], sems.at[p])


def main_kernel(table, xa, xb, w, down_t, up, act, slope_out, rank_out, up_out, away, held, acc, low, sems):
    width = w.shape[0] // 16
    wide = 2 * width
    for p in range(16):
        block_copy(table, w, held, sems, p).start()

    acc[...] = jnp.zeros_like(acc)
    low[...] = jnp.zeros_like(low)

    def gather_half(x_ref, base):
        def step(k, carry):
            at = pl.multiple_of(k * wide, wide)
            p = base + 2 * k
            block_copy(table, w, held, sems, p).wait()
            block_copy(table, w, held, sems, p + 1).wait()
            x = x_ref[:, pl.ds(at, wide)]
            rows = pl.ds(pl.multiple_of(p * width, wide), wide)
            acc[...] += jnp.dot(x, held[rows], preferred_element_type=f32)
            for half in range(2):
                there = pl.ds(pl.multiple_of(table[p + half] * width, width), width)
                low[...] += contract(down_t[:, there], x[:, half * width : (half + 1) * width], 1, 1)
            return carry

        lax.fori_loop(0, 4, step, 0)

    gather_half(xa, 0)
    gather_half(xb, 8)

    low_t = low[...]
    lowrank_t, lowrank = low_t.astype(bf16), low_t.T.astype(bf16)
    preact = acc[...] + adapter_scale * jnp.dot(lowrank, up[...], preferred_element_type=f32)
    slope = (act[...].astype(f32) * gelu_slope(preact)).astype(bf16)
    slope_out[...] = slope
    rank_out[...] = adapter_scale * contract(up[...], slope, 1, 1)
    up_out[...] = adapter_scale * jnp.dot(lowrank_t, slope, preferred_element_type=f32)

    def term(k, carry):
        at = pl.multiple_of(k * wide, wide)
        rows = pl.ds(pl.multiple_of(8 * width + k * wide, wide), wide)
        away[:, pl.ds(at, wide)] = contract(slope_out[...], held[rows], 1, 1).astype(bf16)
        return carry

    lax.fori_loop(0, 4, term, 0)


VMEM = pl.BlockSpec(memory_space=pltpu.VMEM)
SMEM = pl.BlockSpec(memory_space=pltpu.SMEM)
HBM = pl.BlockSpec(memory_space=pltpu.HBM)


def forward(table, xa, xb, w, down_t, up, act):
    rows, rank, hidden = xa.shape[0], down_t.shape[0], w.shape[1]
    return pl.pallas_call(
        main_kernel,
        out_shape=(
            jax.ShapeDtypeStruct((rows, hidden), bf16),
            jax.ShapeDtypeStruct((rank, rows), f32),
            jax.ShapeDtypeStruct((rank, hidden), f32),
            jax.ShapeDtypeStruct(xa.shape, bf16),
        ),
        in_specs=[SMEM, VMEM, VMEM, HBM, VMEM, VMEM, VMEM],
        out_specs=(VMEM, VMEM, VMEM, VMEM),
        scratch_shapes=[
            pltpu.VMEM(w.shape, bf16),
            pltpu.VMEM((rows, hidden), f32),
            pltpu.VMEM((rank, rows), f32),
            pltpu.SemaphoreType.DMA((16,)),
        ],
        compiler_params=pltpu.CompilerParams(vmem_limit_bytes=56 * 2**20),
        cost_estimate=pl.CostEstimate(
            flops=3 * rows * w.shape[0] * hidden, bytes_accessed=14 * 2**20, transcendentals=0
        ),
        name="forward",
    )(table, xa, xb, w, down_t, up, act)


def kept_kernel(table, slope, w, out, held, sems):
    width = w.shape[0] // 16
    wide = 2 * width
    for p in range(8):
        block_copy(table, w, held, sems, p).start()

    def term(k, carry):
        block_copy(table, w, held, sems, 2 * k).wait()
        block_copy(table, w, held, sems, 2 * k + 1).wait()
        at = pl.multiple_of(k * wide, wide)
        out[:, pl.ds(at, wide)] = contract(slope[...], held[pl.ds(at, wide)], 1, 1).astype(bf16)
        return carry

    lax.fori_loop(0, 4, term, 0)


def kept_half(table, slope, w):
    rows, hidden = slope.shape
    half = w.shape[0] // 2
    return pl.pallas_call(
        kept_kernel,
        out_shape=jax.ShapeDtypeStruct((rows, half), bf16),
        in_specs=[SMEM, VMEM, HBM],
        out_specs=VMEM,
        scratch_shapes=[pltpu.VMEM((half, hidden), bf16), pltpu.SemaphoreType.DMA((8,))],
        compiler_params=pltpu.CompilerParams(vmem_limit_bytes=56 * 2**20),
        cost_estimate=pl.CostEstimate(
            flops=2 * rows * half * hidden, bytes_accessed=7 * 2**20, transcendentals=0
        ),
        name="kept_half",
    )(table, slope, w)


def widen(value):
    return value.astype(f32)


def pair_sum(value, *meetings):
    for meet in meetings:
        value = value + meet(value)
    return value


def rounded_sum(value, meet):
    rounded = value.astype(bf16)
    return widen(rounded) + widen(send(rounded, meet))


def body(normed_tokens, up_weight, adapter_down, adapter_up, act_grad):
    width = normed_tokens.shape[1]
    hidden = up_weight.shape[1]
    model_index = lax.axis_index("mp")
    core = lax.axis_index("fsdp") & 1
    y_hi, x_at = model_index >> 2, model_index & 3
    one, two = 3 - 2 * core, 1 + 2 * core

    step = [0 * core, one, two, 0 * core + 2]
    table = jnp.stack([((y_hi ^ step[r]) << 2) | (x_at ^ step[q]) for q in range(4) for r in range(4)])

    gathered = lax.all_gather(up_weight, "fsdp", axis=0, tiled=True)

    pair = jnp.concatenate([normed_tokens, y_first(normed_tokens)], axis=1)
    column = jnp.concatenate([pair, y_second(pair)], axis=1)
    near = jnp.concatenate([column, x_first(column)], axis=1)
    far = x_second(near)

    up_columns = lax.dynamic_slice_in_dim(adapter_up, model_index * hidden, hidden, 1)
    slope_grad, rank_part, up_local, away = forward(
        table, near, far, gathered, adapter_down.T, up_columns, act_grad
    )

    over_x = x_second(away)
    kept = kept_half(table, slope_grad, gathered)
    rank_sum = pair_sum(rank_part, y_first, y_second)
    over_x, kept, rank_sum = lax.optimization_barrier((over_x, kept, rank_sum))

    half = 4 * width
    to_next = (widen(kept[:, half:]) + widen(over_x[:, half:])).astype(bf16)
    over_next = x_first(to_next)
    rank_sum = pair_sum(rank_sum, x_first, x_second)
    over_next, rank_sum = lax.optimization_barrier((over_next, rank_sum))

    rank_grad = rank_sum.astype(bf16)
    own = widen(kept[:, :half]) + widen(over_x[:, :half]) + widen(over_next)
    own, to_y = own[:, : 2 * width], own[:, 2 * width :].astype(bf16)
    over_y = y_second(to_y)
    down_local = jnp.dot(rank_grad, normed_tokens, preferred_element_type=f32)
    grads = jnp.concatenate([up_local, down_local], axis=1)
    grads = rounded_sum(grads, lambda z, yl, c, yh, x: (z ^ 1, yl, c, yh, x))
    grads = rounded_sum(grads, lambda z, yl, c, yh, x: (z ^ 3, yl, c, yh, x))
    over_y, grads = lax.optimization_barrier((over_y, grads))

    own = own + widen(over_y)
    own, to_y = own[:, :width], own[:, width:].astype(bf16)
    over_y = y_first(to_y)
    grads = rounded_sum(grads, lambda z, yl, c, yh, x: (z ^ 7, yl, c, yh, x))
    grads = rounded_sum(grads, lambda z, yl, c, yh, x: (z, yl ^ 1, c, yh, x))
    grads = rounded_sum(grads, lambda z, yl, c, yh, x: (z, yl, c ^ 1, yh, x))
    summed = own + widen(over_y)
    up_grad, down_grad = grads[:, :hidden].astype(bf16), grads[:, hidden:].astype(bf16).T

    down_rows = lax.dynamic_slice_in_dim(adapter_down, model_index * width, width, 0)
    normed_grad = (summed + contract(rank_grad, down_rows, 0, 1)).astype(bf16)
    return (normed_grad, down_grad, up_grad)


def solution(mesh):
    placed = (P("fsdp", "mp"), P("fsdp", "mp"), P(), P(), P("fsdp", "mp"))
    return jax.shard_map(
        body,
        mesh=mesh,
        in_specs=placed,
        out_specs=(P("fsdp", "mp"), P("mp", None), P(None, "mp")),
        check_vma=False,
    )
```

time: 387 us -> 218 us (0.56)
  the two profiles are of different devices: /device:TPU:1 before, /device:TPU:6 now
where the time goes in v2:
time: 218 us; the launch traced here: 215 us
  waiting for transfers between devices  113 us (52%)
  starting transfers between devices  58.6 us (27%)
  Pallas kernels  17.7 us (8%)
  between operations  14.4 us (7%)
  other arithmetic  5.81 us (3%)
  local copies, waits for them, and re-layouts  3.58 us (2%)
    ppermute x17, waiting for transfers between devices, send(): return lax.ppermute(value, ('fsdp', 'mp'), pairs)  97.3 us
    ppermute x17, starting transfers between devices, send(): return lax.ppermute(value, ('fsdp', 'mp'), pairs)  58.5 us
    all_gather x1, waiting for transfers between devices, body(): gathered = lax.all_gather(up_weight, 'fsdp', axis=0, tiled=True)  15.3 us
    pallas_call x1, Pallas kernels, forward(): pl.pallas_call(main_kernel, out_shape=(jax.ShapeDtypeStruct((rows, hidden...  12.2 us
    pallas_call x1, Pallas kernels, kept_half(): pl.pallas_call(kept_kernel, out_shape=jax.ShapeDtypeStruct((rows, half),...  5.51 us
  transfers between devices with their start and end apart: 18, of which 15 were waited for; matrix products, arithmetic and copies ran while one was open for 4% of the time, Pallas kernels for 3%

profile of v2, /device:TPU:6, one launch (start us, length us, event | category | flops | bytes accessed | tf_op | source)
XLA Modules:
  0.0 215.2 jit_solution(10969724215390006099)
XLA Ops:
  7.9 6.2 %collective-permute-start = (bf16[256,384]{1,0:T(8,128)(2,1)}, bf16[256,384]{1,0:T(8,128)(2,1)S(1)}, u32[]{:S(2)}, u32[]{:S(2)}) collective-permute-start(bf16[256,384]{1,0:T(8,128)(2,1)} %param.5), channel_id=1, source_target_pairs={{0,12},{1,13},{2,14},{3,15},{4,8},{5,9},{6,10},{7,11},{8,4},{9,5},... | collective-permute-start | bytes 589832 | tf_op jit(solution)/shard_map/ppermute | solution.py:35
  14.1 5.6 %collective-permute-done = bf16[256,384]{1,0:T(8,128)(2,1)S(1)} collective-permute-done((bf16[256,384]{1,0:T(8,128)(2,1)}, bf16[256,384]{1,0:T(8,128)(2,1)S(1)}, u32[]{:S(2)}, u32[]{:S(2)}) %collective-permute-start) | collective-permute-done | bytes 196640 | tf_op jit(solution)/shard_map/ppermute | solution.py:35
  20.7 4.7 %collective-permute-start.1 = (bf16[256,768]{1,0:T(8,128)(2,1)S(1)}, bf16[256,768]{1,0:T(8,128)(2,1)S(1)}, u32[]{:S(2)}, u32[]{:S(2)}) collective-permute-start(bf16[256,768]{1,0:T(8,128)(2,1)S(1)} %pad_maximum_fusion.1), channel_id=1, source_target_pairs={{0,4},{1,5},{2,6},{3,7},{4,0},{5,1},{6,2},{7,3},{8,12},{9,13},{10,... | collective-permute-start | bytes 1179656 | tf_op jit(solution)/shard_map/ppermute | solution.py:35
  25.4 13.8 %collective-permute-done.1 = bf16[256,768]{1,0:T(8,128)(2,1)S(1)} collective-permute-done((bf16[256,768]{1,0:T(8,128)(2,1)S(1)}, bf16[256,768]{1,0:T(8,128)(2,1)S(1)}, u32[]{:S(2)}, u32[]{:S(2)}) %collective-permute-start.1) | collective-permute-done | bytes 393248 | tf_op jit(solution)/shard_map/ppermute | solution.py:35
  40.1 4.6 %collective-permute-start.2 = (bf16[256,1536]{1,0:T(8,128)(2,1)S(1)}, bf16[256,1536]{1,0:T(8,128)(2,1)S(1)}, u32[]{:S(2)}, u32[]{:S(2)}) collective-permute-start(bf16[256,1536]{1,0:T(8,128)(2,1)S(1)} %pad_maximum_fusion), channel_id=1, source_target_pairs={{0,3},{1,2},{2,1},{3,0},{4,7},{5,6},{6,5},{7,4},{8,11},{9,10},{10,... | collective-permute-start | bytes 2359304 | tf_op jit(solution)/shard_map/ppermute | solution.py:35
  44.9 14.5 %collective-permute-done.2 = bf16[256,1536]{1,0:T(8,128)(2,1)S(1)} collective-permute-done((bf16[256,1536]{1,0:T(8,128)(2,1)S(1)}, bf16[256,1536]{1,0:T(8,128)(2,1)S(1)}, u32[]{:S(2)}, u32[]{:S(2)}) %collective-permute-start.2) | collective-permute-done | bytes 786464 | tf_op jit(solution)/shard_map/ppermute | solution.py:35
  62.7 19.2 %collective-permute-done.3.xb = bf16[256,3072]{1,0:T(8,128)(2,1)} collective-permute-done((bf16[256,3072]{1,0:T(8,128)(2,1)S(1)}, bf16[256,3072]{1,0:T(8,128)(2,1)}, u32[]{:S(2)}, u32[]{:S(2)}) %collective-permute-start.3) | collective-permute-done | bytes 1572896 | tf_op jit(solution)/shard_map/ppermute | solution.py:35
  81.9 15.3 %all-gather.2.cloned.1.call-done.w = bf16[6144,768]{1,0:T(8,128)(2,1)} async-done(((bf16[192,768]{1,0:T(8,128)(2,1)}), bf16[6144,768]{1,0:T(8,128)(2,1)}) %all-gather.2.cloned.1.call-update) | async-done | bytes 9437200 | tf_op jit(solution)/shard_map/all_gather | solution.py:193
  97.2 12.2 %forward.1 = (bf16[256,768]{1,0:T(8,128)(2,1)}, f32[64,256]{1,0:T(8,128)}, f32[64,768]{1,0:T(8,128)}, bf16[256,3072]{1,0:T(8,128)(2,1)}) custom-call(s32[16]{0:T(128)} %stack.67.table, bf16[256,3072]{1,0:T(8,128)(2,1)} %copy-done.3, bf16[256,3072]{1,0:T(8,128)(2,1)} %collective-permute-done.3.xb, bf16[6144,768]{1,0:T(8,128)(2,1)} %all-gather.2.cloned.1.call-done.w, ...), custom_call_target="tpu_custom_call" | custom-call | flops 3623878656 | bytes 14680064 | tf_op jit(solution)/shard_map/forward/pallas_call | solution.py:110
  109.4 2.6 %collective-permute-start.4 = (bf16[256,3072]{1,0:T(8,128)(2,1)}, bf16[256,3072]{1,0:T(8,128)(2,1)S(1)}, u32[]{:S(2)}, u32[]{:S(2)}) collective-permute-start(bf16[256,3072]{1,0:T(8,128)(2,1)} %get-tuple-element.14), channel_id=1, source_target_pairs={{0,1},{1,0},{2,3},{3,2},{4,5},{5,4},{6,7},{7,6},{8,9},{9,8},{10,11... | collective-permute-start | bytes 4718600 | tf_op jit(solution)/shard_map/ppermute | solution.py:35
  112.0 4.0 %collective-permute-start.5 = (f32[64,256]{1,0:T(8,128)}, f32[64,256]{1,0:T(8,128)S(1)}, u32[]{:S(2)}, u32[]{:S(2)}) collective-permute-start(f32[64,256]{1,0:T(8,128)} %get-tuple-element.16), channel_id=1, source_target_pairs={{0,12},{1,13},{2,14},{3,15},{4,8},{5,9},{6,10},{7,11},{8,4},{9,5},... | collective-permute-start | bytes 196616 | tf_op jit(solution)/shard_map/ppermute | solution.py:35
  115.9 4.6 %collective-permute-done.5 = f32[64,256]{1,0:T(8,128)S(1)} collective-permute-done((f32[64,256]{1,0:T(8,128)}, f32[64,256]{1,0:T(8,128)S(1)}, u32[]{:S(2)}, u32[]{:S(2)}) %collective-permute-start.5) | collective-permute-done | bytes 65568 | tf_op jit(solution)/shard_map/ppermute | solution.py:35
  121.4 4.3 %collective-permute-start.6 = (f32[64,256]{1,0:T(8,128)S(1)}, f32[64,256]{1,0:T(8,128)S(1)}, u32[]{:S(2)}, u32[]{:S(2)}) collective-permute-start(f32[64,256]{1,0:T(8,128)S(1)} %add.56), channel_id=1, source_target_pairs={{0,4},{1,5},{2,6},{3,7},{4,0},{5,1},{6,2},{7,3},{8,12},{9,13},{10,... | collective-permute-start | bytes 196616 | tf_op jit(solution)/shard_map/ppermute | solution.py:35
  125.7 5.5 %kept_half.1 = bf16[256,3072]{1,0:T(8,128)(2,1)} custom-call(s32[16]{0:T(128)} %stack.67.table, bf16[256,768]{1,0:T(8,128)(2,1)} %get-tuple-element.15.slope, bf16[6144,768]{1,0:T(8,128)(2,1)} %all-gather.2.cloned.1.call-done.w), custom_call_target="tpu_custom_call" | custom-call | flops 1207959552 | bytes 7340032 | tf_op jit(solution)/shard_map/kept_half/pallas_call | solution.py:153
  135.4 5.0 %collective-permute-start.8 = (f32[64,256]{1,0:T(8,128)S(1)}, f32[64,256]{1,0:T(8,128)S(1)}, u32[]{:S(2)}, u32[]{:S(2)}) collective-permute-start(f32[64,256]{1,0:T(8,128)S(1)} %add.57), channel_id=1, source_target_pairs={{0,3},{1,2},{2,1},{3,0},{4,7},{5,6},{6,5},{7,4},{8,11},{9,10},{10,... | collective-permute-start | bytes 196616 | tf_op jit(solution)/shard_map/ppermute | solution.py:35
  140.3 8.7 %collective-permute-done.8 = f32[64,256]{1,0:T(8,128)S(1)} collective-permute-done((f32[64,256]{1,0:T(8,128)S(1)}, f32[64,256]{1,0:T(8,128)S(1)}, u32[]{:S(2)}, u32[]{:S(2)}) %collective-permute-start.8) | collective-permute-done | bytes 65568 | tf_op jit(solution)/shard_map/ppermute | solution.py:35
  151.0 4.2 %collective-permute-done.9 = f32[64,256]{1,0:T(8,128)S(1)} collective-permute-done((f32[64,256]{1,0:T(8,128)S(1)}, f32[64,256]{1,0:T(8,128)S(1)}, u32[]{:S(2)}, u32[]{:S(2)}) %collective-permute-start.9) | collective-permute-done | bytes 65568 | tf_op jit(solution)/shard_map/ppermute | solution.py:35
  155.4 2.4 %collective-permute-start.11 = (bf16[64,1152]{1,0:T(8,128)(2,1)S(1)}, bf16[64,1152]{1,0:T(8,128)(2,1)S(1)}, u32[]{:S(2)}, u32[]{:S(2)}) collective-permute-start(bf16[64,1152]{1,0:T(8,128)(2,1)S(1)} %pad_maximum_fusion.2), channel_id=1, source_target_pairs={{0,64},{1,65},{2,66},{3,67},{4,68},{5,69},{6,70},{7,71},{8,72},{9,... | collective-permute-start | bytes 442376 | tf_op jit(solution)/shard_map/ppermute | solution.py:35
  157.8 4.6 %collective-permute-done.11 = bf16[64,1152]{1,0:T(8,128)(2,1)S(1)} collective-permute-done((bf16[64,1152]{1,0:T(8,128)(2,1)S(1)}, bf16[64,1152]{1,0:T(8,128)(2,1)S(1)}, u32[]{:S(2)}, u32[]{:S(2)}) %collective-permute-start.11) | collective-permute-done | bytes 147488 | tf_op jit(solution)/shard_map/ppermute | solution.py:35
  162.5 3.9 %collective-permute-start.12 = (bf16[64,1152]{1,0:T(8,128)(2,1)S(1)}, bf16[64,1152]{1,0:T(8,128)(2,1)S(1)}, u32[]{:S(2)}, u32[]{:S(2)}) collective-permute-start(bf16[64,1152]{1,0:T(8,128)(2,1)S(1)} %add_convert_fusion.4), channel_id=1, source_target_pairs={{0,192},{1,193},{2,194},{3,195},{4,196},{5,197},{6,198},{7,199},{8... | collective-permute-start | bytes 442376 | tf_op jit(solution)/shard_map/ppermute | solution.py:35
  166.9 3.5 %collective-permute-start.10 = (bf16[256,768]{1,0:T(8,128)(2,1)S(1)}, bf16[256,768]{1,0:T(8,128)(2,1)S(1)}, u32[]{:S(2)}, u32[]{:S(2)}) collective-permute-start(bf16[256,768]{1,0:T(8,128)(2,1)S(1)} %slice.63), channel_id=1, source_target_pairs={{0,4},{1,5},{2,6},{3,7},{4,0},{5,1},{6,2},{7,3},{8,12},{9,13},{10,... | collective-permute-start | bytes 1179656 | tf_op jit(solution)/shard_map/ppermute | solution.py:35
  171.4 10.3 %collective-permute-done.10 = bf16[256,768]{1,0:T(8,128)(2,1)S(1)} collective-permute-done((bf16[256,768]{1,0:T(8,128)(2,1)S(1)}, bf16[256,768]{1,0:T(8,128)(2,1)S(1)}, u32[]{:S(2)}, u32[]{:S(2)}) %collective-permute-start.10) | collective-permute-done | bytes 393248 | tf_op jit(solution)/shard_map/ppermute | solution.py:35
  184.7 7.5 %collective-permute-done.14 = bf16[64,1152]{1,0:T(8,128)(2,1)S(1)} collective-permute-done((bf16[64,1152]{1,0:T(8,128)(2,1)S(1)}, bf16[64,1152]{1,0:T(8,128)(2,1)S(1)}, u32[]{:S(2)}, u32[]{:S(2)}) %collective-permute-start.14) | collective-permute-done | bytes 147488 | tf_op jit(solution)/shard_map/ppermute | solution.py:35
  195.5 5.0 %collective-permute-start.13 = (bf16[256,384]{1,0:T(8,128)(2,1)S(1)}, bf16[256,384]{1,0:T(8,128)(2,1)S(1)}, u32[]{:S(2)}, u32[]{:S(2)}) collective-permute-start(bf16[256,384]{1,0:T(8,128)(2,1)S(1)} %slice.64), channel_id=1, source_target_pairs={{0,12},{1,13},{2,14},{3,15},{4,8},{5,9},{6,10},{7,11},{8,4},{9,5},... | collective-permute-start | bytes 589832 | tf_op jit(solution)/shard_map/ppermute | solution.py:35
  (55 shorter events, 28.6 us)
Async XLA Ops:
  7.2 54.9 %copy-start = (bf16[64,12288]{1,0:T(8,128)(2,1)S(1)}, bf16[64,12288]{1,0:T(8,128)(2,1)}, u32[]{:S(2)}) copy-start(bf16[64,12288]{1,0:T(8,128)(2,1)} %param.8) | copy-start | bytes 4718596
  7.2 37.6 %copy-start.2 = (bf16[256,384]{1,0:T(8,128)(2,1)S(1)}, bf16[256,384]{1,0:T(8,128)(2,1)}, u32[]{:S(2)}) copy-start(bf16[256,384]{1,0:T(8,128)(2,1)} %param.5) | copy-start | bytes 589828
  7.2 90.0 %all-gather.2.cloned.1.call-start = ((), (), s32[]{:S(2)}) async-start(), calls=%async_computation | async-start | bytes 9732096 | tf_op jit(solution)/shard_map/all_gather | solution.py:193
  7.9 11.8 %collective-permute-start = (bf16[256,384]{1,0:T(8,128)(2,1)}, bf16[256,384]{1,0:T(8,128)(2,1)S(1)}, u32[]{:S(2)}, u32[]{:S(2)}) collective-permute-start(bf16[256,384]{1,0:T(8,128)(2,1)} %param.5), channel_id=1, source_target_pairs={{0,12},{1,13},{2,14},{3,15},{4,8},{5,9},{6,10},{7,11},{8,4},{9,5},... | collective-permute-start | bytes 589832 | tf_op jit(solution)/shard_map/ppermute | solution.py:35
  20.7 18.5 %collective-permute-start.1 = (bf16[256,768]{1,0:T(8,128)(2,1)S(1)}, bf16[256,768]{1,0:T(8,128)(2,1)S(1)}, u32[]{:S(2)}, u32[]{:S(2)}) collective-permute-start(bf16[256,768]{1,0:T(8,128)(2,1)S(1)} %pad_maximum_fusion.1), channel_id=1, source_target_pairs={{0,4},{1,5},{2,6},{3,7},{4,0},{5,1},{6,2},{7,3},{8,12},{9,13},{10,... | collective-permute-start | bytes 1179656 | tf_op jit(solution)/shard_map/ppermute | solution.py:35
  40.1 19.3 %collective-permute-start.2 = (bf16[256,1536]{1,0:T(8,128)(2,1)S(1)}, bf16[256,1536]{1,0:T(8,128)(2,1)S(1)}, u32[]{:S(2)}, u32[]{:S(2)}) collective-permute-start(bf16[256,1536]{1,0:T(8,128)(2,1)S(1)} %pad_maximum_fusion), channel_id=1, source_target_pairs={{0,3},{1,2},{2,1},{3,0},{4,7},{5,6},{6,5},{7,4},{8,11},{9,10},{10,... | collective-permute-start | bytes 2359304 | tf_op jit(solution)/shard_map/ppermute | solution.py:35
  59.5 37.7 %copy-start.3 = (bf16[256,3072]{1,0:T(8,128)(2,1)}, bf16[256,3072]{1,0:T(8,128)(2,1)S(1)}, u32[]{:S(2)}) copy-start(bf16[256,3072]{1,0:T(8,128)(2,1)S(1)} %constant_dynamic-update-slice_fusion.xa) | copy-start | bytes 4718596
  59.5 22.4 %collective-permute-start.3 = (bf16[256,3072]{1,0:T(8,128)(2,1)S(1)}, bf16[256,3072]{1,0:T(8,128)(2,1)}, u32[]{:S(2)}, u32[]{:S(2)}) collective-permute-start(bf16[256,3072]{1,0:T(8,128)(2,1)S(1)} %constant_dynamic-update-slice_fusion.xa), channel_id=1, source_target_pairs={{0,1},{1,0},{2,3},{3,2},{4,5},{5,4},{6,7},{7,6},{8,9},{9,8},{10,11... | collective-permute-start | bytes 4718600 | tf_op jit(solution)/shard_map/ppermute | solution.py:35
  109.4 22.5 %collective-permute-start.4 = (bf16[256,3072]{1,0:T(8,128)(2,1)}, bf16[256,3072]{1,0:T(8,128)(2,1)S(1)}, u32[]{:S(2)}, u32[]{:S(2)}) collective-permute-start(bf16[256,3072]{1,0:T(8,128)(2,1)} %get-tuple-element.14), channel_id=1, source_target_pairs={{0,1},{1,0},{2,3},{3,2},{4,5},{5,4},{6,7},{7,6},{8,9},{9,8},{10,11... | collective-permute-start | bytes 4718600 | tf_op jit(solution)/shard_map/ppermute | solution.py:35
  112.0 8.6 %collective-permute-start.5 = (f32[64,256]{1,0:T(8,128)}, f32[64,256]{1,0:T(8,128)S(1)}, u32[]{:S(2)}, u32[]{:S(2)}) collective-permute-start(f32[64,256]{1,0:T(8,128)} %get-tuple-element.16), channel_id=1, source_target_pairs={{0,12},{1,13},{2,14},{3,15},{4,8},{5,9},{6,10},{7,11},{8,4},{9,5},... | collective-permute-start | bytes 196616 | tf_op jit(solution)/shard_map/ppermute | solution.py:35
  121.4 9.8 %collective-permute-start.6 = (f32[64,256]{1,0:T(8,128)S(1)}, f32[64,256]{1,0:T(8,128)S(1)}, u32[]{:S(2)}, u32[]{:S(2)}) collective-permute-start(f32[64,256]{1,0:T(8,128)S(1)} %add.56), channel_id=1, source_target_pairs={{0,4},{1,5},{2,6},{3,7},{4,0},{5,1},{6,2},{7,3},{8,12},{9,13},{10,... | collective-permute-start | bytes 196616 | tf_op jit(solution)/shard_map/ppermute | solution.py:35
  131.2 19.8 %copy-start.5 = (f32[64,768]{1,0:T(8,128)S(1)}, f32[64,768]{1,0:T(8,128)}, u32[]{:S(2)}) copy-start(f32[64,768]{1,0:T(8,128)} %get-tuple-element.21) | copy-start | bytes 589828
  131.3 35.2 %copy-start.1 = (bf16[256,3072]{1,0:T(8,128)(2,1)S(1)}, bf16[256,3072]{1,0:T(8,128)(2,1)}, u32[]{:S(2)}) copy-start(bf16[256,3072]{1,0:T(8,128)(2,1)} %kept_half.1) | copy-start | bytes 4718596
  133.2 22.0 %collective-permute-start.7 = (bf16[256,1536]{1,0:T(8,128)(2,1)S(1)}, bf16[256,1536]{1,0:T(8,128)(2,1)S(1)}, u32[]{:S(2)}, u32[]{:S(2)}) collective-permute-start(bf16[256,1536]{1,0:T(8,128)(2,1)S(1)} %add_convert_fusion), channel_id=1, source_target_pairs={{0,3},{1,2},{2,1},{3,0},{4,7},{5,6},{6,5},{7,4},{8,11},{9,10},{10,... | collective-permute-start | bytes 2359304 | tf_op jit(solution)/shard_map/ppermute | solution.py:35
  135.4 13.7 %collective-permute-start.8 = (f32[64,256]{1,0:T(8,128)S(1)}, f32[64,256]{1,0:T(8,128)S(1)}, u32[]{:S(2)}, u32[]{:S(2)}) collective-permute-start(f32[64,256]{1,0:T(8,128)S(1)} %add.57), channel_id=1, source_target_pairs={{0,3},{1,2},{2,1},{3,0},{4,7},{5,6},{6,5},{7,4},{8,11},{9,10},{10,... | collective-permute-start | bytes 196616 | tf_op jit(solution)/shard_map/ppermute | solution.py:35
  149.1 6.2 %collective-permute-start.9 = (f32[64,256]{1,0:T(8,128)S(1)}, f32[64,256]{1,0:T(8,128)S(1)}, u32[]{:S(2)}, u32[]{:S(2)}) collective-permute-start(f32[64,256]{1,0:T(8,128)S(1)} %add.60), channel_id=1, source_target_pairs={{0,1},{1,0},{2,3},{3,2},{4,5},{5,4},{6,7},{7,6},{8,9},{9,8},{10,11... | collective-permute-start | bytes 196616 | tf_op jit(solution)/shard_map/ppermute | solution.py:35
  155.4 7.0 %collective-permute-start.11 = (bf16[64,1152]{1,0:T(8,128)(2,1)S(1)}, bf16[64,1152]{1,0:T(8,128)(2,1)S(1)}, u32[]{:S(2)}, u32[]{:S(2)}) collective-permute-start(bf16[64,1152]{1,0:T(8,128)(2,1)S(1)} %pad_maximum_fusion.2), channel_id=1, source_target_pairs={{0,64},{1,65},{2,66},{3,67},{4,68},{5,69},{6,70},{7,71},{8,72},{9,... | collective-permute-start | bytes 442376 | tf_op jit(solution)/shard_map/ppermute | solution.py:35
  162.5 8.8 %collective-permute-start.12 = (bf16[64,1152]{1,0:T(8,128)(2,1)S(1)}, bf16[64,1152]{1,0:T(8,128)(2,1)S(1)}, u32[]{:S(2)}, u32[]{:S(2)}) collective-permute-start(bf16[64,1152]{1,0:T(8,128)(2,1)S(1)} %add_convert_fusion.4), channel_id=1, source_target_pairs={{0,192},{1,193},{2,194},{3,195},{4,196},{5,197},{6,198},{7,199},{8... | collective-permute-start | bytes 442376 | tf_op jit(solution)/shard_map/ppermute | solution.py:35
  166.9 14.8 %collective-permute-start.10 = (bf16[256,768]{1,0:T(8,128)(2,1)S(1)}, bf16[256,768]{1,0:T(8,128)(2,1)S(1)}, u32[]{:S(2)}, u32[]{:S(2)}) collective-permute-start(bf16[256,768]{1,0:T(8,128)(2,1)S(1)} %slice.63), channel_id=1, source_target_pairs={{0,4},{1,5},{2,6},{3,7},{4,0},{5,1},{6,2},{7,3},{8,12},{9,13},{10,... | collective-permute-start | bytes 1179656 | tf_op jit(solution)/shard_map/ppermute | solution.py:35
  181.6 0.7 copy-start.4
  182.4 9.8 %collective-permute-start.14 = (bf16[64,1152]{1,0:T(8,128)(2,1)S(1)}, bf16[64,1152]{1,0:T(8,128)(2,1)S(1)}, u32[]{:S(2)}, u32[]{:S(2)}) collective-permute-start(bf16[64,1152]{1,0:T(8,128)(2,1)S(1)} %convert_add_fusion.1), channel_id=1, source_target_pairs={{0,448},{1,449},{2,450},{3,451},{4,452},{5,453},{6,454},{7,455},{8... | collective-permute-start | bytes 442376 | tf_op jit(solution)/shard_map/ppermute | solution.py:35
  192.2 9.1 %collective-permute-start.15 = (bf16[64,1152]{1,0:T(8,128)(2,1)S(1)}, bf16[64,1152]{1,0:T(8,128)(2,1)S(1)}, u32[]{:S(2)}, u32[]{:S(2)}) collective-permute-start(bf16[64,1152]{1,0:T(8,128)(2,1)S(1)} %add_convert_fusion.3), channel_id=1, source_target_pairs={{0,32},{1,33},{2,34},{3,35},{4,36},{5,37},{6,38},{7,39},{8,40},{9,... | collective-permute-start | bytes 442376 | tf_op jit(solution)/shard_map/ppermute | solution.py:35
  195.5 9.8 %collective-permute-start.13 = (bf16[256,384]{1,0:T(8,128)(2,1)S(1)}, bf16[256,384]{1,0:T(8,128)(2,1)S(1)}, u32[]{:S(2)}, u32[]{:S(2)}) collective-permute-start(bf16[256,384]{1,0:T(8,128)(2,1)S(1)} %slice.64), channel_id=1, source_target_pairs={{0,12},{1,13},{2,14},{3,15},{4,8},{5,9},{6,10},{7,11},{8,4},{9,5},... | collective-permute-start | bytes 589832 | tf_op jit(solution)/shard_map/ppermute | solution.py:35
  201.4 5.7 %collective-permute-start.16 = (bf16[64,1152]{1,0:T(8,128)(2,1)S(1)}, bf16[64,1152]{1,0:T(8,128)(2,1)S(1)}, u32[]{:S(2)}, u32[]{:S(2)}) collective-permute-start(bf16[64,1152]{1,0:T(8,128)(2,1)S(1)} %add_convert_fusion.2), channel_id=1, source_target_pairs={{0,16},{1,17},{2,18},{3,19},{4,20},{5,21},{6,22},{7,23},{8,24},{9,... | collective-permute-start | bytes 442376 | tf_op jit(solution)/shard_map/ppermute | solution.py:35
Sparse Core Ops, SparseCore 0:
  10.2 86.9 all-gather.1

commit v3 on v2

--- a/solution.py
+++ b/solution.py
@@ -55,49 +55,41 @@
     return pltpu.make_async_copy(source, held.at[pl.ds(p * width, width)], sems.at[p])
 
 
-def main_kernel(table, xa, xb, w, down_t, up, act, slope_out, rank_out, up_out, away, held, acc, low, sems):
+def lowrank_kernel(table, xa, xb, down_t, up, low_out, term_out):
+    width = xa.shape[1] // 8
+    low = jnp.zeros(low_out.shape, f32)
+    for p in range(16):
+        there = pl.ds(pl.multiple_of(table[p] * width, width), width)
+        x_ref = xa if p < 8 else xb
+        x = x_ref[:, p % 8 * width : (p % 8 + 1) * width]
+        low += contract(down_t[:, there], x, 1, 1)
+    low_out[...] = low.astype(bf16)
+    lowrank = low.T.astype(bf16)
+    term_out[...] = adapter_scale * jnp.dot(lowrank, up[...], preferred_element_type=f32)
+
+
+def main_kernel(table, xa, xb, w, low_t, term, up, act, slope_out, rank_out, up_out, away, held, acc, sems):
     width = w.shape[0] // 16
     wide = 2 * width
     for p in range(16):
         block_copy(table, w, held, sems, p).start()
 
-    acc[...] = jnp.zeros_like(acc)
-    low[...] = jnp.zeros_like(low)
-
-    def gather_half(x_ref, base):
-        def step(k, carry):
-            at = pl.multiple_of(k * wide, wide)
-            p = base + 2 * k
-            block_copy(table, w, held, sems, p).wait()
-            block_copy(table, w, held, sems, p + 1).wait()
-            x = x_ref[:, pl.ds(at, wide)]
-            rows = pl.ds(pl.multiple_of(p * width, wide), wide)
-            acc[...] += jnp.dot(x, held[rows], preferred_element_type=f32)
-            for half in range(2):
-                there = pl.ds(pl.multiple_of(table[p + half] * width, width), width)
-                low[...] += contract(down_t[:, there], x[:, half * width : (half + 1) * width], 1, 1)
-            return carry
-
-        lax.fori_loop(0, 4, step, 0)
-
-    gather_half(xa, 0)
-    gather_half(xb, 8)
-
-    low_t = low[...]
-    lowrank_t, lowrank = low_t.astype(bf16), low_t.T.astype(bf16)
-    preact = acc[...] + adapter_scale * jnp.dot(lowrank, up[...], preferred_element_type=f32)
-    slope = (act[...].astype(f32) * gelu_slope(preact)).astype(bf16)
+    acc[...] = term[...]
+    for k in range(8):
+        block_copy(table, w, held, sems, 2 * k).wait()
+        block_copy(table, w, held, sems, 2 * k + 1).wait()
+        x_ref = xa if k < 4 else xb
+        x = x_ref[:, k % 4 * wide : (k % 4 + 1) * wide]
+        acc[...] += jnp.dot(x, held[k * wide : (k + 1) * wide], preferred_element_type=f32)
+
+    slope = (act[...].astype(f32) * gelu_slope(acc[...])).astype(bf16)
     slope_out[...] = slope
-    rank_out[...] = adapter_scale * contract(up[...], slope, 1, 1)
-    up_out[...] = adapter_scale * jnp.dot(lowrank_t, slope, preferred_element_type=f32)
-
-    def term(k, carry):
-        at = pl.multiple_of(k * wide, wide)
-        rows = pl.ds(pl.multiple_of(8 * width + k * wide, wide), wide)
-        away[:, pl.ds(at, wide)] = contract(slope_out[...], held[rows], 1, 1).astype(bf16)
-        return carry
-
-    lax.fori_loop(0, 4, term, 0)
+    rank_out[...] = (adapter_scale * contract(up[...], slope, 1, 1)).astype(bf16)
+    up_out[...] = (adapter_scale * jnp.dot(low_t[...], slope, preferred_element_type=f32)).astype(bf16)
+
+    for k in range(4):
+        rows = held[(4 + k) * wide : (5 + k) * wide]
+        away[:, k * wide : (k + 1) * wide] = contract(slope, rows, 1, 1).astype(bf16)
 
 
 VMEM = pl.BlockSpec(memory_space=pltpu.VMEM)
@@ -105,22 +97,39 @@
 HBM = pl.BlockSpec(memory_space=pltpu.HBM)
 
 
-def forward(table, xa, xb, w, down_t, up, act):
-    rows, rank, hidden = xa.shape[0], down_t.shape[0], w.shape[1]
+def lowrank_terms(table, xa, xb, down_t, up):
+    rows, rank, hidden = xa.shape[0], up.shape[0], up.shape[1]
+    return pl.pallas_call(
+        lowrank_kernel,
+        out_shape=(
+            jax.ShapeDtypeStruct((rank, rows), bf16),
+            jax.ShapeDtypeStruct((rows, hidden), f32),
+        ),
+        in_specs=[SMEM, VMEM, VMEM, VMEM, VMEM],
+        out_specs=(VMEM, VMEM),
+        compiler_params=pltpu.CompilerParams(vmem_limit_bytes=56 * 2**20),
+        cost_estimate=pl.CostEstimate(
+            flops=2 * rows * rank * 16 * xa.shape[1], bytes_accessed=5 * 2**20, transcendentals=0
+        ),
+        name="lowrank_terms",
+    )(table, xa, xb, down_t, up)
+
+
+def forward(table, xa, xb, w, low_t, term, up, act):
+    rows, rank, hidden = xa.shape[0], up.shape[0], w.shape[1]
     return pl.pallas_call(
         main_kernel,
         out_shape=(
             jax.ShapeDtypeStruct((rows, hidden), bf16),
-            jax.ShapeDtypeStruct((rank, rows), f32),
-            jax.ShapeDtypeStruct((rank, hidden), f32),
+            jax.ShapeDtypeStruct((rank, rows), bf16),
+            jax.ShapeDtypeStruct((rank, hidden), bf16),
             jax.ShapeDtypeStruct(xa.shape, bf16),
         ),
-        in_specs=[SMEM, VMEM, VMEM, HBM, VMEM, VMEM, VMEM],
+        in_specs=[SMEM, VMEM, VMEM, HBM, VMEM, VMEM, VMEM, VMEM],
         out_specs=(VMEM, VMEM, VMEM, VMEM),
         scratch_shapes=[
             pltpu.VMEM(w.shape, bf16),
             pltpu.VMEM((rows, hidden), f32),
-            pltpu.VMEM((rank, rows), f32),
             pltpu.SemaphoreType.DMA((16,)),
         ],
         compiler_params=pltpu.CompilerParams(vmem_limit_bytes=56 * 2**20),
@@ -128,7 +137,7 @@
             flops=3 * rows * w.shape[0] * hidden, bytes_accessed=14 * 2**20, transcendentals=0
         ),
         name="forward",
-    )(table, xa, xb, w, down_t, up, act)
+    )(table, xa, xb, w, low_t, term, up, act)
 
 
 def kept_kernel(table, slope, w, out, held, sems):
@@ -168,15 +177,13 @@
     return value.astype(f32)
 
 
-def pair_sum(value, *meetings):
-    for meet in meetings:
-        value = value + meet(value)
-    return value
-
-
-def rounded_sum(value, meet):
-    rounded = value.astype(bf16)
-    return widen(rounded) + widen(send(rounded, meet))
+def exchange(value, axis):
+    return lax.all_to_all(value, axis, 0, 0, tiled=True)
+
+
+def gather_small(value, axis, count):
+    copies = jnp.broadcast_to(value[None], (count, *value.shape))
+    return exchange(copies.reshape(-1, value.shape[1]), axis)
 
 
 def body(normed_tokens, up_weight, adapter_down, adapter_up, act_grad):
@@ -198,39 +205,41 @@
     far = x_second(near)
 
     up_columns = lax.dynamic_slice_in_dim(adapter_up, model_index * hidden, hidden, 1)
+    low_t, low_term = lowrank_terms(table, near, far, adapter_down.T, up_columns)
     slope_grad, rank_part, up_local, away = forward(
-        table, near, far, gathered, adapter_down.T, up_columns, act_grad
+        table, near, far, gathered, low_t, low_term, up_columns, act_grad
     )
 
     over_x = x_second(away)
     kept = kept_half(table, slope_grad, gathered)
-    rank_sum = pair_sum(rank_part, y_first, y_second)
-    over_x, kept, rank_sum = lax.optimization_barrier((over_x, kept, rank_sum))
+    rank_parts = gather_small(rank_part, "mp", YH * X)
+    over_x, kept, rank_parts = lax.optimization_barrier((over_x, kept, rank_parts))
 
     half = 4 * width
     to_next = (widen(kept[:, half:]) + widen(over_x[:, half:])).astype(bf16)
     over_next = x_first(to_next)
-    rank_sum = pair_sum(rank_sum, x_first, x_second)
-    over_next, rank_sum = lax.optimization_barrier((over_next, rank_sum))
-
-    rank_grad = rank_sum.astype(bf16)
+    rank = rank_part.shape[0]
+    rank_grad = jnp.sum(widen(rank_parts).reshape(YH * X, rank, -1), axis=0).astype(bf16)
+    down_local = jnp.dot(rank_grad, normed_tokens, preferred_element_type=f32).astype(bf16)
+    shares = jnp.concatenate(
+        [up_local[:, :width], up_local[:, width:], down_local, jnp.zeros_like(down_local)], axis=0
+    )
+    shares = exchange(shares, "fsdp")
+    over_next, shares = lax.optimization_barrier((over_next, shares))
+
     own = widen(kept[:, :half]) + widen(over_x[:, :half]) + widen(over_next)
     own, to_y = own[:, : 2 * width], own[:, 2 * width :].astype(bf16)
     over_y = y_second(to_y)
-    down_local = jnp.dot(rank_grad, normed_tokens, preferred_element_type=f32)
-    grads = jnp.concatenate([up_local, down_local], axis=1)
-    grads = rounded_sum(grads, lambda z, yl, c, yh, x: (z ^ 1, yl, c, yh, x))
-    grads = rounded_sum(grads, lambda z, yl, c, yh, x: (z ^ 3, yl, c, yh, x))
+    members = Z * YL * C
+    share = jnp.sum(widen(shares).reshape(members, -1, width), axis=0).astype(bf16)
+    grads = gather_small(share, "fsdp", members)
     over_y, grads = lax.optimization_barrier((over_y, grads))
 
     own = own + widen(over_y)
     own, to_y = own[:, :width], own[:, width:].astype(bf16)
-    over_y = y_first(to_y)
-    grads = rounded_sum(grads, lambda z, yl, c, yh, x: (z ^ 7, yl, c, yh, x))
-    grads = rounded_sum(grads, lambda z, yl, c, yh, x: (z, yl ^ 1, c, yh, x))
-    grads = rounded_sum(grads, lambda z, yl, c, yh, x: (z, yl, c ^ 1, yh, x))
-    summed = own + widen(over_y)
-    up_grad, down_grad = grads[:, :hidden].astype(bf16), grads[:, hidden:].astype(bf16).T
+    summed = own + widen(y_first(to_y))
+    up_grad = jnp.concatenate([grads[:rank], grads[rank : 2 * rank]], axis=1)
+    down_grad = grads[2 * rank : 3 * rank].T
 
     down_rows = lax.dynamic_slice_in_dim(adapter_down, model_index * width, width, 0)
     normed_grad = (summed + contract(rank_grad, down_rows, 0, 1)).astype(bf16)

time: 218 us -> 202 us (0.927)
  waiting for transfers between devices: 113 us -> 92.2 us
  blocking collectives: 0 us -> 16.2 us
  starting transfers between devices: 58.6 us -> 43.4 us
  Pallas kernels: 17.7 us -> 21 us
    ppermute x17 -> x8, waiting for transfers between devices: 97.3 us -> 59.6 us  [send(): return lax.ppermute(value, ('fsdp', 'mp'), pairs)]
    ppermute x17 -> x8, starting transfers between devices: 58.5 us -> 31.7 us  [send(): return lax.ppermute(value, ('fsdp', 'mp'), pairs)]
    all_to_all x0 -> x2, waiting for transfers between devices: none -> 21.3 us  [exchange(): return lax.all_to_all(value, axis, 0, 0, tiled=True)]
    all_to_all x0 -> x1, blocking collectives: none -> 16.2 us  [exchange(): return lax.all_to_all(value, axis, 0, 0, tiled=True)]
    all_to_all x0 -> x2, starting transfers between devices: none -> 11.7 us  [exchange(): return lax.all_to_all(value, axis, 0, 0, tiled=True)]
    all_gather x1, waiting for transfers between devices: 15.3 us -> 10.6 us  [body(): gathered = lax.all_gather(up_weight, 'fsdp', axis=0, tiled=True)]
    pallas_call x0 -> x1, Pallas kernels: none -> 4.62 us  [lowrank_terms(): pl.pallas_call(lowrank_kernel, out_shape=(jax.ShapeDtypeStruct((rank, row...]
    broadcast_in_dim x0 -> x3, local copies, waits for them, and re-layouts: none -> 2.32 us  [the longest x2 2.31 us: gather_small(): copies = jnp.broadcast_to(value[None], (count, *value.shape))]
  transfers between devices with their start and end apart: 18 -> 11, of which waited for: 15 -> 8; matrix products, arithmetic and copies ran while one was open for 4% -> 4% of each run, Pallas kernels for 3% -> 5%
where the time goes in v3:
time: 202 us; the launch traced here: 201 us
  waiting for transfers between devices  92.2 us (46%)
  starting transfers between devices  43.4 us (21%)
  Pallas kernels  21 us (10%)
  blocking collectives  16.2 us (8%)
  between operations  14.3 us (7%)
  other arithmetic  6.99 us (3%)
  local copies, waits for them, and re-layouts  5.38 us (3%)
    ppermute x8, waiting for transfers between devices, send(): return lax.ppermute(value, ('fsdp', 'mp'), pairs)  59.6 us
    ppermute x8, starting transfers between devices, send(): return lax.ppermute(value, ('fsdp', 'mp'), pairs)  31.7 us
    all_to_all x2, waiting for transfers between devices, exchange(): return lax.all_to_all(value, axis, 0, 0, tiled=True)  21.3 us
    all_to_all x1, blocking collectives, exchange(): return lax.all_to_all(value, axis, 0, 0, tiled=True)  16.2 us
    all_to_all x2, starting transfers between devices, exchange(): return lax.all_to_all(value, axis, 0, 0, tiled=True)  11.7 us
    pallas_call x1, Pallas kernels, forward(): pl.pallas_call(main_kernel, out_shape=(jax.ShapeDtypeStruct((rows, hidden...  10.9 us
    all_gather x1, waiting for transfers between devices, body(): gathered = lax.all_gather(up_weight, 'fsdp', axis=0, tiled=True)  10.6 us
    pallas_call x1, Pallas kernels, kept_half(): pl.pallas_call(kept_kernel, out_shape=jax.ShapeDtypeStruct((rows, half),...  5.55 us
  transfers between devices with their start and end apart: 11, of which 8 were waited for; matrix products, arithmetic and copies ran while one was open for 4% of the time, Pallas kernels for 5%

profile of v3, /device:TPU:6, one launch (start us, length us, event | category | flops | bytes accessed | tf_op | source)
XLA Modules:
  0.0 201.4 jit_solution(1860708224659675773)
XLA Ops:
  7.9 6.2 %collective-permute-start = (bf16[256,384]{1,0:T(8,128)(2,1)}, bf16[256,384]{1,0:T(8,128)(2,1)S(1)}, u32[]{:S(2)}, u32[]{:S(2)}) collective-permute-start(bf16[256,384]{1,0:T(8,128)(2,1)} %param.5), channel_id=1, source_target_pairs={{0,12},{1,13},{2,14},{3,15},{4,8},{5,9},{6,10},{7,11},{8,4},{9,5},... | collective-permute-start | bytes 589832 | tf_op jit(solution)/shard_map/ppermute | solution.py:35
  14.1 5.6 %collective-permute-done = bf16[256,384]{1,0:T(8,128)(2,1)S(1)} collective-permute-done((bf16[256,384]{1,0:T(8,128)(2,1)}, bf16[256,384]{1,0:T(8,128)(2,1)S(1)}, u32[]{:S(2)}, u32[]{:S(2)}) %collective-permute-start) | collective-permute-done | bytes 196640 | tf_op jit(solution)/shard_map/ppermute | solution.py:35
  20.7 4.7 %collective-permute-start.1 = (bf16[256,768]{1,0:T(8,128)(2,1)S(1)}, bf16[256,768]{1,0:T(8,128)(2,1)S(1)}, u32[]{:S(2)}, u32[]{:S(2)}) collective-permute-start(bf16[256,768]{1,0:T(8,128)(2,1)S(1)} %pad_maximum_fusion.1), channel_id=1, source_target_pairs={{0,4},{1,5},{2,6},{3,7},{4,0},{5,1},{6,2},{7,3},{8,12},{9,13},{10,... | collective-permute-start | bytes 1179656 | tf_op jit(solution)/shard_map/ppermute | solution.py:35
  25.4 13.8 %collective-permute-done.1 = bf16[256,768]{1,0:T(8,128)(2,1)S(1)} collective-permute-done((bf16[256,768]{1,0:T(8,128)(2,1)S(1)}, bf16[256,768]{1,0:T(8,128)(2,1)S(1)}, u32[]{:S(2)}, u32[]{:S(2)}) %collective-permute-start.1) | collective-permute-done | bytes 393248 | tf_op jit(solution)/shard_map/ppermute | solution.py:35
  40.1 4.6 %collective-permute-start.2 = (bf16[256,1536]{1,0:T(8,128)(2,1)S(1)}, bf16[256,1536]{1,0:T(8,128)(2,1)S(1)}, u32[]{:S(2)}, u32[]{:S(2)}) collective-permute-start(bf16[256,1536]{1,0:T(8,128)(2,1)S(1)} %pad_maximum_fusion), channel_id=1, source_target_pairs={{0,3},{1,2},{2,1},{3,0},{4,7},{5,6},{6,5},{7,4},{8,11},{9,10},{10,... | collective-permute-start | bytes 2359304 | tf_op jit(solution)/shard_map/ppermute | solution.py:35
  44.9 14.5 %collective-permute-done.2 = bf16[256,1536]{1,0:T(8,128)(2,1)S(1)} collective-permute-done((bf16[256,1536]{1,0:T(8,128)(2,1)S(1)}, bf16[256,1536]{1,0:T(8,128)(2,1)S(1)}, u32[]{:S(2)}, u32[]{:S(2)}) %collective-permute-start.2) | collective-permute-done | bytes 786464 | tf_op jit(solution)/shard_map/ppermute | solution.py:35
  59.5 1.9 collective-permute-start.3
  62.8 19.2 %collective-permute-done.3.xb = bf16[256,3072]{1,0:T(8,128)(2,1)} collective-permute-done((bf16[256,3072]{1,0:T(8,128)(2,1)S(1)}, bf16[256,3072]{1,0:T(8,128)(2,1)}, u32[]{:S(2)}, u32[]{:S(2)}) %collective-permute-start.3) | collective-permute-done | bytes 1572896 | tf_op jit(solution)/shard_map/ppermute | solution.py:35
  81.9 4.6 %lowrank_terms.1 = (bf16[64,256]{1,0:T(8,128)(2,1)}, f32[256,768]{1,0:T(8,128)}) custom-call(s32[16]{0:T(128)} %stack.67.table, bf16[256,3072]{1,0:T(8,128)(2,1)} %copy-done.3, bf16[256,3072]{1,0:T(8,128)(2,1)} %collective-permute-done.3.xb, bf16[64,6144]{1,0:T(8,128)(2,1)} %bitcast.32, bf16[64,768]{1,0:T(8,128)(2,1)} %constant_dynamic-slice_fusion.up), custom_call_target="tpu_custom_call" | custom-call | flops 1610612736 | bytes 5242880 | tf_op jit(solution)/shard_map/lowrank_terms/pallas_call | solution.py:102
  86.5 10.6 %all-gather.2.cloned.1.call-done.w = bf16[6144,768]{1,0:T(8,128)(2,1)} async-done(((bf16[192,768]{1,0:T(8,128)(2,1)}), bf16[6144,768]{1,0:T(8,128)(2,1)}) %all-gather.2.cloned.1.call-update) | async-done | bytes 9437200 | tf_op jit(solution)/shard_map/all_gather | solution.py:200
  97.2 10.9 %forward.1 = (bf16[256,768]{1,0:T(8,128)(2,1)}, bf16[64,256]{1,0:T(8,128)(2,1)}, bf16[64,768]{1,0:T(8,128)(2,1)}, bf16[256,3072]{1,0:T(8,128)(2,1)}) custom-call(s32[16]{0:T(128)} %stack.67.table, bf16[256,3072]{1,0:T(8,128)(2,1)} %copy-done.3, bf16[256,3072]{1,0:T(8,128)(2,1)} %collective-permute-done.3.xb, ...), custom_call_target="tpu_custom_call" | custom-call | flops 3623878656 | bytes 14680064 | tf_op jit(solution)/shard_map/forward/pallas_call | solution.py:120
  108.1 2.6 %collective-permute-start.4 = (bf16[256,3072]{1,0:T(8,128)(2,1)}, bf16[256,3072]{1,0:T(8,128)(2,1)}, u32[]{:S(2)}, u32[]{:S(2)}) collective-permute-start(bf16[256,3072]{1,0:T(8,128)(2,1)} %get-tuple-element.18), channel_id=1, source_target_pairs={{0,1},{1,0},{2,3},{3,2},{4,5},{5,4},{6,7},{7,6},{8,9},{9,8},{10,11... | collective-permute-start | bytes 4718600 | tf_op jit(solution)/shard_map/ppermute | solution.py:35
  112.3 7.8 %all-to-all-start = ((bf16[16,64,256]{2,1,0:T(8,128)(2,1)}), bf16[16,64,256]{2,1,0:T(8,128)(2,1)S(1)}, u32[]{:S(2)}, u32[]{:S(2)}) async-start(bf16[16,64,256]{2,1,0:T(8,128)(2,1)} %broadcast_in_dim.6), calls=%async_computation | async-start | bytes 1048576 | tf_op jit(solution)/shard_map/all_to_all | solution.py:181
  120.2 5.5 %kept_half.1 = bf16[256,3072]{1,0:T(8,128)(2,1)} custom-call(s32[16]{0:T(128)} %stack.67.table, bf16[256,768]{1,0:T(8,128)(2,1)} %get-tuple-element.19.slope, bf16[6144,768]{1,0:T(8,128)(2,1)} %all-gather.2.cloned.1.call-done.w), custom_call_target="tpu_custom_call" | custom-call | flops 1207959552 | bytes 7340032 | tf_op jit(solution)/shard_map/kept_half/pallas_call | solution.py:162
  125.8 10.5 %all-to-all-done = bf16[16,64,256]{2,1,0:T(8,128)(2,1)S(1)} async-done(((bf16[16,64,256]{2,1,0:T(8,128)(2,1)}), bf16[16,64,256]{2,1,0:T(8,128)(2,1)S(1)}, u32[]{:S(2)}, u32[]{:S(2)}) %all-to-all-start) | async-done | bytes 524320 | tf_op jit(solution)/shard_map/all_to_all | solution.py:181
  136.3 1.7 add_convert_fusion
  138.0 4.2 %collective-permute-start.5 = (bf16[256,1536]{1,0:T(8,128)(2,1)S(1)}, bf16[256,1536]{1,0:T(8,128)(2,1)S(1)}, u32[]{:S(2)}, u32[]{:S(2)}) collective-permute-start(bf16[256,1536]{1,0:T(8,128)(2,1)S(1)} %add_convert_fusion), channel_id=1, source_target_pairs={{0,3},{1,2},{2,1},{3,0},{4,7},{5,6},{6,5},{7,4},{8,11},{9,10},{10,... | collective-permute-start | bytes 2359304 | tf_op jit(solution)/shard_map/ppermute | solution.py:35
  142.5 16.2 %all_to_all.30 = bf16[32,8,384]{2,1,0:T(8,128)(2,1)S(1)} all-to-all(bf16[32,8,384]{2,1,0:T(8,128)(2,1)S(1)} %maximum_bitcast_fusion), channel_id=1, replica_groups=mesh['fsdp'=32,'mp'=16] {'fsdp'}, dimensions={0} | all-to-all | bytes 393216 | tf_op jit(solution)/shard_map/all_to_all | solution.py:181
  160.9 3.6 %collective-permute-start.6 = (bf16[256,768]{1,0:T(8,128)(2,1)}, bf16[256,768]{1,0:T(8,128)(2,1)}, u32[]{:S(2)}, u32[]{:S(2)}) collective-permute-start(bf16[256,768]{1,0:T(8,128)(2,1)} %slice.71), channel_id=1, source_target_pairs={{0,4},{1,5},{2,6},{3,7},{4,0},{5,1},{6,2},{7,3},{8,12},{9,13},{10,... | collective-permute-start | bytes 1179656 | tf_op jit(solution)/shard_map/ppermute | solution.py:35
  165.3 3.9 %all-to-all-start.2 = ((bf16[32,8,384]{2,1,0:T(8,128)(2,1)}), bf16[32,8,384]{2,1,0:T(8,128)(2,1)S(1)}, u32[]{:S(2)}, u32[]{:S(2)}) async-start(bf16[32,8,384]{2,1,0:T(8,128)(2,1)} %broadcast_in_dim.8), calls=%async_computation.2 | async-start | bytes 393216 | tf_op jit(solution)/shard_map/all_to_all | solution.py:181
  169.2 10.8 %all-to-all-done.2 = bf16[32,8,384]{2,1,0:T(8,128)(2,1)S(1)} async-done(((bf16[32,8,384]{2,1,0:T(8,128)(2,1)}), bf16[32,8,384]{2,1,0:T(8,128)(2,1)S(1)}, u32[]{:S(2)}, u32[]{:S(2)}) %all-to-all-start.2) | async-done | bytes 196640 | tf_op jit(solution)/shard_map/all_to_all | solution.py:181
  181.1 3.8 %collective-permute-start.7 = (bf16[256,384]{1,0:T(8,128)(2,1)S(1)}, bf16[256,384]{1,0:T(8,128)(2,1)S(1)}, u32[]{:S(2)}, u32[]{:S(2)}) collective-permute-start(bf16[256,384]{1,0:T(8,128)(2,1)S(1)} %slice.72), channel_id=1, source_target_pairs={{0,12},{1,13},{2,14},{3,15},{4,8},{5,9},{6,10},{7,11},{8,4},{9,5},... | collective-permute-start | bytes 589832 | tf_op jit(solution)/shard_map/ppermute | solution.py:35
  186.2 6.6 %collective-permute-done.7 = bf16[256,384]{1,0:T(8,128)(2,1)S(1)} collective-permute-done((bf16[256,384]{1,0:T(8,128)(2,1)S(1)}, bf16[256,384]{1,0:T(8,128)(2,1)S(1)}, u32[]{:S(2)}, u32[]{:S(2)}) %collective-permute-start.7) | collective-permute-done | bytes 196640 | tf_op jit(solution)/shard_map/ppermute | solution.py:35
  192.8 1.7 fusion.1
  (38 shorter events, 11.6 us)
Async XLA Ops:
  7.2 54.9 %copy-start = (bf16[64,12288]{1,0:T(8,128)(2,1)S(1)}, bf16[64,12288]{1,0:T(8,128)(2,1)}, u32[]{:S(2)}) copy-start(bf16[64,12288]{1,0:T(8,128)(2,1)} %param.8) | copy-start | bytes 4718596
  7.2 37.6 %copy-start.2 = (bf16[256,384]{1,0:T(8,128)(2,1)S(1)}, bf16[256,384]{1,0:T(8,128)(2,1)}, u32[]{:S(2)}) copy-start(bf16[256,384]{1,0:T(8,128)(2,1)} %param.5) | copy-start | bytes 589828
  7.2 90.0 %all-gather.2.cloned.1.call-start = ((), (), s32[]{:S(2)}) async-start(), calls=%async_computation.3 | async-start | bytes 9732096 | tf_op jit(solution)/shard_map/all_gather | solution.py:200
  7.9 11.8 %collective-permute-start = (bf16[256,384]{1,0:T(8,128)(2,1)}, bf16[256,384]{1,0:T(8,128)(2,1)S(1)}, u32[]{:S(2)}, u32[]{:S(2)}) collective-permute-start(bf16[256,384]{1,0:T(8,128)(2,1)} %param.5), channel_id=1, source_target_pairs={{0,12},{1,13},{2,14},{3,15},{4,8},{5,9},{6,10},{7,11},{8,4},{9,5},... | collective-permute-start | bytes 589832 | tf_op jit(solution)/shard_map/ppermute | solution.py:35
  20.7 18.5 %collective-permute-start.1 = (bf16[256,768]{1,0:T(8,128)(2,1)S(1)}, bf16[256,768]{1,0:T(8,128)(2,1)S(1)}, u32[]{:S(2)}, u32[]{:S(2)}) collective-permute-start(bf16[256,768]{1,0:T(8,128)(2,1)S(1)} %pad_maximum_fusion.1), channel_id=1, source_target_pairs={{0,4},{1,5},{2,6},{3,7},{4,0},{5,1},{6,2},{7,3},{8,12},{9,13},{10,... | collective-permute-start | bytes 1179656 | tf_op jit(solution)/shard_map/ppermute | solution.py:35
  40.1 19.3 %collective-permute-start.2 = (bf16[256,1536]{1,0:T(8,128)(2,1)S(1)}, bf16[256,1536]{1,0:T(8,128)(2,1)S(1)}, u32[]{:S(2)}, u32[]{:S(2)}) collective-permute-start(bf16[256,1536]{1,0:T(8,128)(2,1)S(1)} %pad_maximum_fusion), channel_id=1, source_target_pairs={{0,3},{1,2},{2,1},{3,0},{4,7},{5,6},{6,5},{7,4},{8,11},{9,10},{10,... | collective-permute-start | bytes 2359304 | tf_op jit(solution)/shard_map/ppermute | solution.py:35
  59.5 22.4 %copy-start.3 = (bf16[256,3072]{1,0:T(8,128)(2,1)}, bf16[256,3072]{1,0:T(8,128)(2,1)S(1)}, u32[]{:S(2)}) copy-start(bf16[256,3072]{1,0:T(8,128)(2,1)S(1)} %constant_dynamic-update-slice_fusion.xa) | copy-start | bytes 4718596
  59.5 22.4 %collective-permute-start.3 = (bf16[256,3072]{1,0:T(8,128)(2,1)S(1)}, bf16[256,3072]{1,0:T(8,128)(2,1)}, u32[]{:S(2)}, u32[]{:S(2)}) collective-permute-start(bf16[256,3072]{1,0:T(8,128)(2,1)S(1)} %constant_dynamic-update-slice_fusion.xa), channel_id=1, source_target_pairs={{0,1},{1,0},{2,3},{3,2},{4,5},{5,4},{6,7},{7,6},{8,9},{9,8},{10,11... | collective-permute-start | bytes 4718600 | tf_op jit(solution)/shard_map/ppermute | solution.py:35
  108.1 28.1 %collective-permute-start.4 = (bf16[256,3072]{1,0:T(8,128)(2,1)}, bf16[256,3072]{1,0:T(8,128)(2,1)}, u32[]{:S(2)}, u32[]{:S(2)}) collective-permute-start(bf16[256,3072]{1,0:T(8,128)(2,1)} %get-tuple-element.18), channel_id=1, source_target_pairs={{0,1},{1,0},{2,3},{3,2},{4,5},{5,4},{6,7},{7,6},{8,9},{9,8},{10,11... | collective-permute-start | bytes 4718600 | tf_op jit(solution)/shard_map/ppermute | solution.py:35
  112.3 23.9 %all-to-all-start = ((bf16[16,64,256]{2,1,0:T(8,128)(2,1)}), bf16[16,64,256]{2,1,0:T(8,128)(2,1)S(1)}, u32[]{:S(2)}, u32[]{:S(2)}) async-start(bf16[16,64,256]{2,1,0:T(8,128)(2,1)} %broadcast_in_dim.6), calls=%async_computation | async-start | bytes 1048576 | tf_op jit(solution)/shard_map/all_to_all | solution.py:181
  120.2 5.6 %copy-start.4 = (bf16[64,768]{1,0:T(8,128)(2,1)S(1)}, bf16[64,768]{1,0:T(8,128)(2,1)}, u32[]{:S(2)}) copy-start(bf16[64,768]{1,0:T(8,128)(2,1)} %get-tuple-element.23) | copy-start | bytes 294916
  136.3 22.4 %copy-start.1 = (bf16[256,3072]{1,0:T(8,128)(2,1)S(1)}, bf16[256,3072]{1,0:T(8,128)(2,1)}, u32[]{:S(2)}) copy-start(bf16[256,3072]{1,0:T(8,128)(2,1)} %kept_half.1) | copy-start | bytes 4718596
  138.0 20.7 %collective-permute-start.5 = (bf16[256,1536]{1,0:T(8,128)(2,1)S(1)}, bf16[256,1536]{1,0:T(8,128)(2,1)S(1)}, u32[]{:S(2)}, u32[]{:S(2)}) collective-permute-start(bf16[256,1536]{1,0:T(8,128)(2,1)S(1)} %add_convert_fusion), channel_id=1, source_target_pairs={{0,3},{1,2},{2,1},{3,0},{4,7},{5,6},{6,5},{7,4},{8,11},{9,10},{10,... | collective-permute-start | bytes 2359304 | tf_op jit(solution)/shard_map/ppermute | solution.py:35
  160.9 19.1 %collective-permute-start.6 = (bf16[256,768]{1,0:T(8,128)(2,1)}, bf16[256,768]{1,0:T(8,128)(2,1)}, u32[]{:S(2)}, u32[]{:S(2)}) collective-permute-start(bf16[256,768]{1,0:T(8,128)(2,1)} %slice.71), channel_id=1, source_target_pairs={{0,4},{1,5},{2,6},{3,7},{4,0},{5,1},{6,2},{7,3},{8,12},{9,13},{10,... | collective-permute-start | bytes 1179656 | tf_op jit(solution)/shard_map/ppermute | solution.py:35
  165.3 14.7 %all-to-all-start.2 = ((bf16[32,8,384]{2,1,0:T(8,128)(2,1)}), bf16[32,8,384]{2,1,0:T(8,128)(2,1)S(1)}, u32[]{:S(2)}, u32[]{:S(2)}) async-start(bf16[32,8,384]{2,1,0:T(8,128)(2,1)} %broadcast_in_dim.8), calls=%async_computation.2 | async-start | bytes 393216 | tf_op jit(solution)/shard_map/all_to_all | solution.py:181
  181.1 11.7 %collective-permute-start.7 = (bf16[256,384]{1,0:T(8,128)(2,1)S(1)}, bf16[256,384]{1,0:T(8,128)(2,1)S(1)}, u32[]{:S(2)}, u32[]{:S(2)}) collective-permute-start(bf16[256,384]{1,0:T(8,128)(2,1)S(1)} %slice.72), channel_id=1, source_target_pairs={{0,12},{1,13},{2,14},{3,15},{4,8},{5,9},{6,10},{7,11},{8,4},{9,5},... | collective-permute-start | bytes 589832 | tf_op jit(solution)/shard_map/ppermute | solution.py:35
Sparse Core Ops, SparseCore 0:
  10.2 86.9 all-gather.1

commit v4 on v3

--- a/solution.py
+++ b/solution.py
@@ -35,6 +35,9 @@
     return lax.ppermute(value, ("fsdp", "mp"), pairs)
 
 
+PLANES = [[(z * YL + y) * C + c for z in range(Z) for c in range(C)] for y in range(YL)]
+
+
 def first(c):
     return 1 if c else 3
 
@@ -45,14 +48,30 @@
 
 y_first = functools.partial(send, step=lambda z, yl, c, yh, x: (z, yl, c, yh ^ first(c), x))
 y_second = functools.partial(send, step=lambda z, yl, c, yh, x: (z, yl, c, yh ^ second(c), x))
+other_plane = functools.partial(send, step=lambda z, yl, c, yh, x: (z, yl ^ 1, c, yh, x))
 x_first = functools.partial(send, step=lambda z, yl, c, yh, x: (z, yl, c, yh, x ^ first(c)))
 x_second = functools.partial(send, step=lambda z, yl, c, yh, x: (z, yl, c, yh, x ^ second(c)))
 
 
-def block_copy(table, w, held, sems, p):
-    width = w.shape[0] // 16
-    source = w.at[pl.ds(pl.multiple_of(table[p] * width, width), width)]
-    return pltpu.make_async_copy(source, held.at[pl.ds(p * width, width)], sems.at[p])
+def row_copies(lies, w, held, sems, p):
+    rows = w.shape[0] // 32
+    copies = []
+    for run in (2 * p, 2 * p + 1):
+        source = w.at[pl.ds(pl.multiple_of(lies[run] * rows, rows), rows)]
+        copies.append(pltpu.make_async_copy(source, held.at[pl.ds(run * rows, rows)], sems.at[run]))
+    return copies
+
+
+def start_blocks(lies, w, held, sems, count):
+    for p in range(count):
+        for copy in row_copies(lies, w, held, sems, p):
+            copy.start()
+
+
+def await_blocks(lies, w, held, sems, first_block):
+    for p in (first_block, first_block + 1):
+        for copy in row_copies(lies, w, held, sems, p):
+            copy.wait()
 
 
 def lowrank_kernel(table, xa, xb, down_t, up, low_out, term_out):
@@ -68,16 +87,14 @@
     term_out[...] = adapter_scale * jnp.dot(lowrank, up[...], preferred_element_type=f32)
 
 
-def main_kernel(table, xa, xb, w, low_t, term, up, act, slope_out, rank_out, up_out, away, held, acc, sems):
+def main_kernel(lies, xa, xb, w, low_t, term, up, act, slope_out, rank_out, up_out, away, held, acc, sems):
     width = w.shape[0] // 16
     wide = 2 * width
-    for p in range(16):
-        block_copy(table, w, held, sems, p).start()
+    start_blocks(lies, w, held, sems, 16)
 
     acc[...] = term[...]
     for k in range(8):
-        block_copy(table, w, held, sems, 2 * k).wait()
-        block_copy(table, w, held, sems, 2 * k + 1).wait()
+        await_blocks(lies, w, held, sems, 2 * k)
         x_ref = xa if k < 4 else xb
         x = x_ref[:, k % 4 * wide : (k % 4 + 1) * wide]
         acc[...] += jnp.dot(x, held[k * wide : (k + 1) * wide], preferred_element_type=f32)
@@ -115,7 +132,7 @@
     )(table, xa, xb, down_t, up)
 
 
-def forward(table, xa, xb, w, low_t, term, up, act):
+def forward(lies, xa, xb, w, low_t, term, up, act):
     rows, rank, hidden = xa.shape[0], up.shape[0], w.shape[1]
     return pl.pallas_call(
         main_kernel,
@@ -130,33 +147,27 @@
         scratch_shapes=[
             pltpu.VMEM(w.shape, bf16),
             pltpu.VMEM((rows, hidden), f32),
-            pltpu.SemaphoreType.DMA((16,)),
+            pltpu.SemaphoreType.DMA((32,)),
         ],
         compiler_params=pltpu.CompilerParams(vmem_limit_bytes=56 * 2**20),
         cost_estimate=pl.CostEstimate(
             flops=3 * rows * w.shape[0] * hidden, bytes_accessed=14 * 2**20, transcendentals=0
         ),
         name="forward",
-    )(table, xa, xb, w, low_t, term, up, act)
-
-
-def kept_kernel(table, slope, w, out, held, sems):
+    )(lies, xa, xb, w, low_t, term, up, act)
+
+
+def kept_kernel(lies, slope, w, out, held, sems):
     width = w.shape[0] // 16
     wide = 2 * width
-    for p in range(8):
-        block_copy(table, w, held, sems, p).start()
-
-    def term(k, carry):
-        block_copy(table, w, held, sems, 2 * k).wait()
-        block_copy(table, w, held, sems, 2 * k + 1).wait()
-        at = pl.multiple_of(k * wide, wide)
-        out[:, pl.ds(at, wide)] = contract(slope[...], held[pl.ds(at, wide)], 1, 1).astype(bf16)
-        return carry
-
-    lax.fori_loop(0, 4, term, 0)
-
-
-def kept_half(table, slope, w):
+    start_blocks(lies, w, held, sems, 8)
+    for k in range(4):
+        await_blocks(lies, w, held, sems, 2 * k)
+        rows = held[k * wide : (k + 1) * wide]
+        out[:, k * wide : (k + 1) * wide] = contract(slope[...], rows, 1, 1).astype(bf16)
+
+
+def kept_half(lies, slope, w):
     rows, hidden = slope.shape
     half = w.shape[0] // 2
     return pl.pallas_call(
@@ -164,13 +175,13 @@
         out_shape=jax.ShapeDtypeStruct((rows, half), bf16),
         in_specs=[SMEM, VMEM, HBM],
         out_specs=VMEM,
-        scratch_shapes=[pltpu.VMEM((half, hidden), bf16), pltpu.SemaphoreType.DMA((8,))],
+        scratch_shapes=[pltpu.VMEM((half, hidden), bf16), pltpu.SemaphoreType.DMA((16,))],
         compiler_params=pltpu.CompilerParams(vmem_limit_bytes=56 * 2**20),
         cost_estimate=pl.CostEstimate(
             flops=2 * rows * half * hidden, bytes_accessed=7 * 2**20, transcendentals=0
         ),
         name="kept_half",
-    )(table, slope, w)
+    )(lies, slope, w)
 
 
 def widen(value):
@@ -184,6 +195,10 @@
 def gather_small(value, axis, count):
     copies = jnp.broadcast_to(value[None], (count, *value.shape))
     return exchange(copies.reshape(-1, value.shape[1]), axis)
+
+
+def add_parts(parts, count):
+    return jnp.sum(widen(parts).reshape(count, -1, parts.shape[1]), axis=0).astype(bf16)
 
 
 def body(normed_tokens, up_weight, adapter_down, adapter_up, act_grad):
@@ -197,7 +212,10 @@
     step = [0 * core, one, two, 0 * core + 2]
     table = jnp.stack([((y_hi ^ step[r]) << 2) | (x_at ^ step[q]) for q in range(4) for r in range(4)])
 
-    gathered = lax.all_gather(up_weight, "fsdp", axis=0, tiled=True)
+    plane = (lax.axis_index("fsdp") >> 1) & 1
+    both = jnp.concatenate([up_weight, other_plane(up_weight)], axis=0)
+    gathered = lax.all_gather(both, "fsdp", axis=0, tiled=True, axis_index_groups=PLANES)
+    lies = jnp.stack([(table >> 1) * 4 + ((table & 1) ^ plane) + 2 * c for c in range(C)], axis=1).reshape(-1)
 
     pair = jnp.concatenate([normed_tokens, y_first(normed_tokens)], axis=1)
     column = jnp.concatenate([pair, y_second(pair)], axis=1)
@@ -207,42 +225,41 @@
     up_columns = lax.dynamic_slice_in_dim(adapter_up, model_index * hidden, hidden, 1)
     low_t, low_term = lowrank_terms(table, near, far, adapter_down.T, up_columns)
     slope_grad, rank_part, up_local, away = forward(
-        table, near, far, gathered, low_t, low_term, up_columns, act_grad
+        lies, near, far, gathered, low_t, low_term, up_columns, act_grad
     )
 
     over_x = x_second(away)
-    kept = kept_half(table, slope_grad, gathered)
     rank_parts = gather_small(rank_part, "mp", YH * X)
-    over_x, kept, rank_parts = lax.optimization_barrier((over_x, kept, rank_parts))
-
+    kept = kept_half(lies, slope_grad, gathered)
     half = 4 * width
     to_next = (widen(kept[:, half:]) + widen(over_x[:, half:])).astype(bf16)
     over_next = x_first(to_next)
-    rank = rank_part.shape[0]
-    rank_grad = jnp.sum(widen(rank_parts).reshape(YH * X, rank, -1), axis=0).astype(bf16)
+    rank_parts, _ = lax.optimization_barrier((rank_parts, to_next))
+    rank_grad = add_parts(rank_parts, YH * X)
+    rank = rank_grad.shape[0]
     down_local = jnp.dot(rank_grad, normed_tokens, preferred_element_type=f32).astype(bf16)
     shares = jnp.concatenate(
         [up_local[:, :width], up_local[:, width:], down_local, jnp.zeros_like(down_local)], axis=0
     )
     shares = exchange(shares, "fsdp")
-    over_next, shares = lax.optimization_barrier((over_next, shares))
 
     own = widen(kept[:, :half]) + widen(over_x[:, :half]) + widen(over_next)
     own, to_y = own[:, : 2 * width], own[:, 2 * width :].astype(bf16)
     over_y = y_second(to_y)
+    shares, _ = lax.optimization_barrier((shares, to_y))
     members = Z * YL * C
-    share = jnp.sum(widen(shares).reshape(members, -1, width), axis=0).astype(bf16)
+    share, over_y = lax.optimization_barrier((add_parts(shares, members), over_y))
     grads = gather_small(share, "fsdp", members)
-    over_y, grads = lax.optimization_barrier((over_y, grads))
 
     own = own + widen(over_y)
     own, to_y = own[:, :width], own[:, width:].astype(bf16)
-    summed = own + widen(y_first(to_y))
+    over_last = y_first(to_y)
+    down_rows = lax.dynamic_slice_in_dim(adapter_down, model_index * width, width, 0)
+    own = own + contract(rank_grad, down_rows, 0, 1)
+    own, over_last = lax.optimization_barrier((own, over_last))
+    normed_grad = (own + widen(over_last)).astype(bf16)
     up_grad = jnp.concatenate([grads[:rank], grads[rank : 2 * rank]], axis=1)
     down_grad = grads[2 * rank : 3 * rank].T
-
-    down_rows = lax.dynamic_slice_in_dim(adapter_down, model_index * width, width, 0)
-    normed_grad = (summed + contract(rank_grad, down_rows, 0, 1)).astype(bf16)
     return (normed_grad, down_grad, up_grad)
 
 

time: 202 us -> 197 us (0.975); the launches traced: 201 us -> 194 us
  starting transfers between devices: 43.4 us -> 69.8 us
  waiting for transfers between devices: 92.2 us -> 69.6 us
  blocking collectives: 16.2 us -> 0 us
  other arithmetic: 6.99 us -> 10.6 us
    all_to_all x2 -> x3, waiting for transfers between devices: 21.3 us -> 2.51 us  [exchange(): return lax.all_to_all(value, axis, 0, 0, tiled=True)]
    all_to_all x2 -> x3, starting transfers between devices: 11.7 us -> 28.7 us  [exchange(): return lax.all_to_all(value, axis, 0, 0, tiled=True)]
    all_to_all x1 -> x0, blocking collectives: 16.2 us -> none  [exchange(): return lax.all_to_all(value, axis, 0, 0, tiled=True)]
    ppermute x8 -> x9, starting transfers between devices: 31.7 us -> 41.1 us  [send(): return lax.ppermute(value, ('fsdp', 'mp'), pairs)]
    all_gather x1, waiting for transfers between devices: 10.6 us -> 1.31 us  [body(): lax.all_gather(both, 'fsdp', axis=0, tiled=True, axis_index_groups=PLANES)]
    ppermute x8 -> x9, waiting for transfers between devices: 59.6 us -> 65.7 us  [send(): return lax.ppermute(value, ('fsdp', 'mp'), pairs)]
  transfers between devices with their start and end apart: 11 -> 13, of which waited for: 8 -> 10; matrix products, arithmetic and copies ran while one was open for 4% -> 7% of each run, Pallas kernels for 5% -> 5%
where the time goes in v4:
time: 197 us; the launch traced here: 194 us
  starting transfers between devices  69.8 us (35%)
  waiting for transfers between devices  69.6 us (35%)
  Pallas kernels  21.6 us (11%)
  between operations  14.4 us (7%)
  other arithmetic  10.6 us (5%)
  local copies, waits for them, and re-layouts  6.54 us (3%)
    ppermute x9, waiting for transfers between devices, send(): return lax.ppermute(value, ('fsdp', 'mp'), pairs)  65.7 us
    ppermute x9, starting transfers between devices, send(): return lax.ppermute(value, ('fsdp', 'mp'), pairs)  41.1 us
    all_to_all x3, starting transfers between devices, exchange(): return lax.all_to_all(value, axis, 0, 0, tiled=True)  28.7 us
    pallas_call x1, Pallas kernels, forward(): pl.pallas_call(main_kernel, out_shape=(jax.ShapeDtypeStruct((rows, hidden...  11 us
    pallas_call x1, Pallas kernels, kept_half(): pl.pallas_call(kept_kernel, out_shape=jax.ShapeDtypeStruct((rows, half),...  5.99 us
    pallas_call x1, Pallas kernels, lowrank_terms(): pl.pallas_call(lowrank_kernel, out_shape=(jax.ShapeDtypeStruct((rank, row...  4.6 us
  transfers between devices with their start and end apart: 13, of which 10 were waited for; matrix products, arithmetic and copies ran while one was open for 7% of the time, Pallas kernels for 5%

profile of v4, /device:TPU:6, one launch (start us, length us, event | category | flops | bytes accessed | tf_op | source)
XLA Modules:
  0.0 193.8 jit_solution(9197034643885483931)
XLA Ops:
  7.2 3.6 %collective-permute-start.4 = (bf16[192,768]{1,0:T(8,128)(2,1)}, bf16[192,768]{1,0:T(8,128)(2,1)S(1)}, u32[]{:S(2)}, u32[]{:S(2)}) collective-permute-start(bf16[192,768]{1,0:T(8,128)(2,1)} %param.6), channel_id=1, source_target_pairs={{0,32},{1,33},{2,34},{3,35},{4,36},{5,37},{6,38},{7,39},{8,40},{9,... | collective-permute-start | bytes 884744 | tf_op jit(solution)/shard_map/ppermute | solution.py:35
  10.9 7.4 %collective-permute-done.4 = bf16[192,768]{1,0:T(8,128)(2,1)S(1)} collective-permute-done((bf16[192,768]{1,0:T(8,128)(2,1)}, bf16[192,768]{1,0:T(8,128)(2,1)S(1)}, u32[]{:S(2)}, u32[]{:S(2)}) %collective-permute-start.4) | collective-permute-done | bytes 294944 | tf_op jit(solution)/shard_map/ppermute | solution.py:35
  20.1 6.2 %collective-permute-start = (bf16[256,384]{1,0:T(8,128)(2,1)S(1)}, bf16[256,384]{1,0:T(8,128)(2,1)S(1)}, u32[]{:S(2)}, u32[]{:S(2)}) collective-permute-start(bf16[256,384]{1,0:T(8,128)(2,1)S(1)} %copy-done.3), channel_id=1, source_target_pairs={{0,12},{1,13},{2,14},{3,15},{4,8},{5,9},{6,10},{7,11},{8,4},{9,5},... | collective-permute-start | bytes 589832 | tf_op jit(solution)/shard_map/ppermute | solution.py:35
  26.3 5.3 %collective-permute-done = bf16[256,384]{1,0:T(8,128)(2,1)S(1)} collective-permute-done((bf16[256,384]{1,0:T(8,128)(2,1)S(1)}, bf16[256,384]{1,0:T(8,128)(2,1)S(1)}, u32[]{:S(2)}, u32[]{:S(2)}) %collective-permute-start) | collective-permute-done | bytes 196640 | tf_op jit(solution)/shard_map/ppermute | solution.py:35
  31.6 4.1 %collective-permute-start.1 = (bf16[256,768]{1,0:T(8,128)(2,1)S(1)}, bf16[256,768]{1,0:T(8,128)(2,1)S(1)}, u32[]{:S(2)}, u32[]{:S(2)}) collective-permute-start(bf16[256,768]{1,0:T(8,128)(2,1)S(1)} %pad_maximum_fusion.2), channel_id=1, source_target_pairs={{0,4},{1,5},{2,6},{3,7},{4,0},{5,1},{6,2},{7,3},{8,12},{9,13},{10,... | collective-permute-start | bytes 1179656 | tf_op jit(solution)/shard_map/ppermute | solution.py:35
  35.7 9.8 %collective-permute-done.1 = bf16[256,768]{1,0:T(8,128)(2,1)S(1)} collective-permute-done((bf16[256,768]{1,0:T(8,128)(2,1)S(1)}, bf16[256,768]{1,0:T(8,128)(2,1)S(1)}, u32[]{:S(2)}, u32[]{:S(2)}) %collective-permute-start.1) | collective-permute-done | bytes 393248 | tf_op jit(solution)/shard_map/ppermute | solution.py:35
  45.6 4.3 %collective-permute-start.2 = (bf16[256,1536]{1,0:T(8,128)(2,1)S(1)}, bf16[256,1536]{1,0:T(8,128)(2,1)S(1)}, u32[]{:S(2)}, u32[]{:S(2)}) collective-permute-start(bf16[256,1536]{1,0:T(8,128)(2,1)S(1)} %pad_maximum_fusion), channel_id=1, source_target_pairs={{0,3},{1,2},{2,1},{3,0},{4,7},{5,6},{6,5},{7,4},{8,11},{9,10},{10,... | collective-permute-start | bytes 2359304 | tf_op jit(solution)/shard_map/ppermute | solution.py:35
  50.1 10.6 %collective-permute-done.2 = bf16[256,1536]{1,0:T(8,128)(2,1)S(1)} collective-permute-done((bf16[256,1536]{1,0:T(8,128)(2,1)S(1)}, bf16[256,1536]{1,0:T(8,128)(2,1)S(1)}, u32[]{:S(2)}, u32[]{:S(2)}) %collective-permute-start.2) | collective-permute-done | bytes 786464 | tf_op jit(solution)/shard_map/ppermute | solution.py:35
  64.9 18.4 %collective-permute-done.3.xb = bf16[256,3072]{1,0:T(8,128)(2,1)} collective-permute-done((bf16[256,3072]{1,0:T(8,128)(2,1)S(1)}, bf16[256,3072]{1,0:T(8,128)(2,1)}, u32[]{:S(2)}, u32[]{:S(2)}) %collective-permute-start.3) | collective-permute-done | bytes 1572896 | tf_op jit(solution)/shard_map/ppermute | solution.py:35
  83.2 4.6 %lowrank_terms.1 = (bf16[64,256]{1,0:T(8,128)(2,1)}, f32[256,768]{1,0:T(8,128)}) custom-call(s32[16]{0:T(128)} %stack.124.table, bf16[256,3072]{1,0:T(8,128)(2,1)} %copy-done.4, bf16[256,3072]{1,0:T(8,128)(2,1)} %collective-permute-done.3.xb, bf16[64,6144]{1,0:T(8,128)(2,1)} %bitcast.52, bf16[64,768]{1,0:T(8,128)(2,1)} %constant_dynamic-slice_fusion.up), custom_call_target="tpu_custom_call" | custom-call | flops 1610612736 | bytes 5242880 | tf_op jit(solution)/shard_map/lowrank_terms/pallas_call | solution.py:119
  89.1 11.0 %forward.1 = (bf16[256,768]{1,0:T(8,128)(2,1)}, bf16[64,256]{1,0:T(8,128)(2,1)}, bf16[64,768]{1,0:T(8,128)(2,1)}, bf16[256,3072]{1,0:T(8,128)(2,1)}) custom-call(s32[32]{0:T(128)} %reshape.694.lies, bf16[256,3072]{1,0:T(8,128)(2,1)} %copy-done.4, bf16[256,3072]{1,0:T(8,128)(2,1)} %collective-permute-done.3.xb, ...), custom_call_target="tpu_custom_call" | custom-call | flops 3623878656 | bytes 14680064 | tf_op jit(solution)/shard_map/forward/pallas_call | solution.py:137
  100.2 2.8 %collective-permute-start.5 = (bf16[256,3072]{1,0:T(8,128)(2,1)}, bf16[256,3072]{1,0:T(8,128)(2,1)}, u32[]{:S(2)}, u32[]{:S(2)}) collective-permute-start(bf16[256,3072]{1,0:T(8,128)(2,1)} %get-tuple-element.18), channel_id=1, source_target_pairs={{0,1},{1,0},{2,3},{3,2},{4,5},{5,4},{6,7},{7,6},{8,9},{9,8},{10,11... | collective-permute-start | bytes 4718600 | tf_op jit(solution)/shard_map/ppermute | solution.py:35
  104.6 10.0 %all-to-all-start = ((bf16[16,64,256]{2,1,0:T(8,128)(2,1)}), bf16[16,64,256]{2,1,0:T(8,128)(2,1)}, u32[]{:S(2)}, u32[]{:S(2)}) async-start(bf16[16,64,256]{2,1,0:T(8,128)(2,1)} %broadcast_in_dim.6), calls=%async_computation | async-start | bytes 1048576 | tf_op jit(solution)/shard_map/all_to_all | solution.py:192
  114.6 6.0 %kept_half.1 = bf16[256,3072]{1,0:T(8,128)(2,1)} custom-call(s32[32]{0:T(128)} %reshape.694.lies, bf16[256,768]{1,0:T(8,128)(2,1)} %get-tuple-element.17.slope, bf16[6144,768]{1,0:T(8,128)(2,1)} %all-gather.2.cloned.1.call-done.w), custom_call_target="tpu_custom_call" | custom-call | flops 1207959552 | bytes 7340032 | tf_op jit(solution)/shard_map/kept_half/pallas_call | solution.py:173
  120.6 4.1 %collective-permute-done.5 = bf16[256,3072]{1,0:T(8,128)(2,1)} collective-permute-done((bf16[256,3072]{1,0:T(8,128)(2,1)}, bf16[256,3072]{1,0:T(8,128)(2,1)}, u32[]{:S(2)}, u32[]{:S(2)}) %collective-permute-start.5) | collective-permute-done | bytes 1572896 | tf_op jit(solution)/shard_map/ppermute | solution.py:35
  124.7 2.5 %add_convert_fusion = bf16[256,1536]{1,0:T(8,128)(2,1)} fusion(bf16[256,3072]{1,0:T(8,128)(2,1)} %collective-permute-done.5, bf16[256,3072]{1,0:T(8,128)(2,1)} %kept_half.1), kind=kLoop, calls=%fused_computation.1 | loop fusion | flops 1572864 | bytes 2359296 | tf_op jit(solution)/shard_map/convert_element_type | solution.py:235
  127.2 6.7 %collective-permute-start.6 = (bf16[256,1536]{1,0:T(8,128)(2,1)}, bf16[256,1536]{1,0:T(8,128)(2,1)}, u32[]{:S(2)}, u32[]{:S(2)}) collective-permute-start(bf16[256,1536]{1,0:T(8,128)(2,1)} %add_convert_fusion), channel_id=1, source_target_pairs={{0,3},{1,2},{2,1},{3,0},{4,7},{5,6},{6,5},{7,4},{8,11},{9,10},{10,... | collective-permute-start | bytes 2359304 | tf_op jit(solution)/shard_map/ppermute | solution.py:35
  136.1 9.2 %all-to-all-start.1 = ((bf16[32,8,384]{2,1,0:T(8,128)(2,1)}), bf16[32,8,384]{2,1,0:T(8,128)(2,1)S(1)}, u32[]{:S(2)}, u32[]{:S(2)}) async-start(bf16[32,8,384]{2,1,0:T(8,128)(2,1)} %maximum_bitcast_fusion), calls=%async_computation.1 | async-start | bytes 393216 | tf_op jit(solution)/shard_map/all_to_all | solution.py:192
  148.3 5.5 %collective-permute-start.7 = (bf16[256,768]{1,0:T(8,128)(2,1)S(1)}, bf16[256,768]{1,0:T(8,128)(2,1)S(1)}, u32[]{:S(2)}, u32[]{:S(2)}) collective-permute-start(bf16[256,768]{1,0:T(8,128)(2,1)S(1)} %slice.88), channel_id=1, source_target_pairs={{0,4},{1,5},{2,6},{3,7},{4,0},{5,1},{6,2},{7,3},{8,12},{9,13},{10,... | collective-permute-start | bytes 1179656 | tf_op jit(solution)/shard_map/ppermute | solution.py:35
  153.7 2.5 %all-to-all-done.1 = bf16[32,8,384]{2,1,0:T(8,128)(2,1)S(1)} async-done(((bf16[32,8,384]{2,1,0:T(8,128)(2,1)}), bf16[32,8,384]{2,1,0:T(8,128)(2,1)S(1)}, u32[]{:S(2)}, u32[]{:S(2)}) %all-to-all-start.1) | async-done | bytes 196640 | tf_op jit(solution)/shard_map/all_to_all | solution.py:192
  156.3 7.4 %collective-permute-done.7 = bf16[256,768]{1,0:T(8,128)(2,1)S(1)} collective-permute-done((bf16[256,768]{1,0:T(8,128)(2,1)S(1)}, bf16[256,768]{1,0:T(8,128)(2,1)S(1)}, u32[]{:S(2)}, u32[]{:S(2)}) %collective-permute-start.7) | collective-permute-done | bytes 393248 | tf_op jit(solution)/shard_map/ppermute | solution.py:35
  164.4 9.5 %all-to-all-start.2 = ((bf16[32,8,384]{2,1,0:T(8,128)(2,1)}), bf16[32,8,384]{2,1,0:T(8,128)(2,1)S(1)}, u32[]{:S(2)}, u32[]{:S(2)}) async-start(bf16[32,8,384]{2,1,0:T(8,128)(2,1)} %broadcast_in_dim.8), calls=%async_computation.2 | async-start | bytes 393216 | tf_op jit(solution)/shard_map/all_to_all | solution.py:192
  175.1 6.0 %collective-permute-start.8 = (bf16[256,384]{1,0:T(8,128)(2,1)S(1)}, bf16[256,384]{1,0:T(8,128)(2,1)S(1)}, u32[]{:S(2)}, u32[]{:S(2)}) collective-permute-start(bf16[256,384]{1,0:T(8,128)(2,1)S(1)} %slice.89), channel_id=1, source_target_pairs={{0,12},{1,13},{2,14},{3,15},{4,8},{5,9},{6,10},{7,11},{8,4},{9,5},... | collective-permute-start | bytes 589832 | tf_op jit(solution)/shard_map/ppermute | solution.py:35
  182.2 2.7 %collective-permute-done.8 = bf16[256,384]{1,0:T(8,128)(2,1)S(1)} collective-permute-done((bf16[256,384]{1,0:T(8,128)(2,1)S(1)}, bf16[256,384]{1,0:T(8,128)(2,1)S(1)}, u32[]{:S(2)}, u32[]{:S(2)}) %collective-permute-start.8) | collective-permute-done | bytes 196640 | tf_op jit(solution)/shard_map/ppermute | solution.py:35
  (50 shorter events, 19.2 us)
Async XLA Ops:
  7.2 57.0 %copy-start = (bf16[64,12288]{1,0:T(8,128)(2,1)S(1)}, bf16[64,12288]{1,0:T(8,128)(2,1)}, u32[]{:S(2)}) copy-start(bf16[64,12288]{1,0:T(8,128)(2,1)} %param.8) | copy-start | bytes 4718596
  7.2 12.9 %copy-start.3 = (bf16[256,384]{1,0:T(8,128)(2,1)S(1)}, bf16[256,384]{1,0:T(8,128)(2,1)}, u32[]{:S(2)}) copy-start(bf16[256,384]{1,0:T(8,128)(2,1)} %param.5) | copy-start | bytes 589828
  7.2 81.9 %all-gather.2.cloned.1.call-start = ((), (), s32[]{:S(2)}) async-start(), calls=%async_computation.3 | async-start | bytes 10027008 | tf_op jit(solution)/shard_map/all_gather | solution.py:217
  7.2 11.0 %collective-permute-start.4 = (bf16[192,768]{1,0:T(8,128)(2,1)}, bf16[192,768]{1,0:T(8,128)(2,1)S(1)}, u32[]{:S(2)}, u32[]{:S(2)}) collective-permute-start(bf16[192,768]{1,0:T(8,128)(2,1)} %param.6), channel_id=1, source_target_pairs={{0,32},{1,33},{2,34},{3,35},{4,36},{5,37},{6,38},{7,39},{8,40},{9,... | collective-permute-start | bytes 884744 | tf_op jit(solution)/shard_map/ppermute | solution.py:35
  20.1 11.4 %collective-permute-start = (bf16[256,384]{1,0:T(8,128)(2,1)S(1)}, bf16[256,384]{1,0:T(8,128)(2,1)S(1)}, u32[]{:S(2)}, u32[]{:S(2)}) collective-permute-start(bf16[256,384]{1,0:T(8,128)(2,1)S(1)} %copy-done.3), channel_id=1, source_target_pairs={{0,12},{1,13},{2,14},{3,15},{4,8},{5,9},{6,10},{7,11},{8,4},{9,5},... | collective-permute-start | bytes 589832 | tf_op jit(solution)/shard_map/ppermute | solution.py:35
  31.6 13.9 %collective-permute-start.1 = (bf16[256,768]{1,0:T(8,128)(2,1)S(1)}, bf16[256,768]{1,0:T(8,128)(2,1)S(1)}, u32[]{:S(2)}, u32[]{:S(2)}) collective-permute-start(bf16[256,768]{1,0:T(8,128)(2,1)S(1)} %pad_maximum_fusion.2), channel_id=1, source_target_pairs={{0,4},{1,5},{2,6},{3,7},{4,0},{5,1},{6,2},{7,3},{8,12},{9,13},{10,... | collective-permute-start | bytes 1179656 | tf_op jit(solution)/shard_map/ppermute | solution.py:35
  45.6 15.1 %collective-permute-start.2 = (bf16[256,1536]{1,0:T(8,128)(2,1)S(1)}, bf16[256,1536]{1,0:T(8,128)(2,1)S(1)}, u32[]{:S(2)}, u32[]{:S(2)}) collective-permute-start(bf16[256,1536]{1,0:T(8,128)(2,1)S(1)} %pad_maximum_fusion), channel_id=1, source_target_pairs={{0,3},{1,2},{2,1},{3,0},{4,7},{5,6},{6,5},{7,4},{8,11},{9,10},{10,... | collective-permute-start | bytes 2359304 | tf_op jit(solution)/shard_map/ppermute | solution.py:35
  60.8 22.4 %copy-start.4 = (bf16[256,3072]{1,0:T(8,128)(2,1)}, bf16[256,3072]{1,0:T(8,128)(2,1)S(1)}, u32[]{:S(2)}) copy-start(bf16[256,3072]{1,0:T(8,128)(2,1)S(1)} %constant_dynamic-update-slice_fusion.xa) | copy-start | bytes 4718596
  60.8 22.4 %collective-permute-start.3 = (bf16[256,3072]{1,0:T(8,128)(2,1)S(1)}, bf16[256,3072]{1,0:T(8,128)(2,1)}, u32[]{:S(2)}, u32[]{:S(2)}) collective-permute-start(bf16[256,3072]{1,0:T(8,128)(2,1)S(1)} %constant_dynamic-update-slice_fusion.xa), channel_id=1, source_target_pairs={{0,1},{1,0},{2,3},{3,2},{4,5},{5,4},{6,7},{7,6},{8,9},{9,8},{10,11... | collective-permute-start | bytes 4718600 | tf_op jit(solution)/shard_map/ppermute | solution.py:35
  100.2 24.5 %collective-permute-start.5 = (bf16[256,3072]{1,0:T(8,128)(2,1)}, bf16[256,3072]{1,0:T(8,128)(2,1)}, u32[]{:S(2)}, u32[]{:S(2)}) collective-permute-start(bf16[256,3072]{1,0:T(8,128)(2,1)} %get-tuple-element.18), channel_id=1, source_target_pairs={{0,1},{1,0},{2,3},{3,2},{4,5},{5,4},{6,7},{7,6},{8,9},{9,8},{10,11... | collective-permute-start | bytes 4718600 | tf_op jit(solution)/shard_map/ppermute | solution.py:35
  104.6 29.5 %all-to-all-start = ((bf16[16,64,256]{2,1,0:T(8,128)(2,1)}), bf16[16,64,256]{2,1,0:T(8,128)(2,1)}, u32[]{:S(2)}, u32[]{:S(2)}) async-start(bf16[16,64,256]{2,1,0:T(8,128)(2,1)} %broadcast_in_dim.6), calls=%async_computation | async-start | bytes 1048576 | tf_op jit(solution)/shard_map/all_to_all | solution.py:192
  120.6 13.4 %copy-start.5 = (bf16[64,768]{1,0:T(8,128)(2,1)S(1)}, bf16[64,768]{1,0:T(8,128)(2,1)}, u32[]{:S(2)}) copy-start(bf16[64,768]{1,0:T(8,128)(2,1)} %get-tuple-element.19) | copy-start | bytes 294916
  120.6 24.8 %copy-start.1 = (bf16[256,3072]{1,0:T(8,128)(2,1)S(1)}, bf16[256,3072]{1,0:T(8,128)(2,1)}, u32[]{:S(2)}) copy-start(bf16[256,3072]{1,0:T(8,128)(2,1)} %kept_half.1) | copy-start | bytes 4718596
  127.2 18.2 %collective-permute-start.6 = (bf16[256,1536]{1,0:T(8,128)(2,1)}, bf16[256,1536]{1,0:T(8,128)(2,1)}, u32[]{:S(2)}, u32[]{:S(2)}) collective-permute-start(bf16[256,1536]{1,0:T(8,128)(2,1)} %add_convert_fusion), channel_id=1, source_target_pairs={{0,3},{1,2},{2,1},{3,0},{4,7},{5,6},{6,5},{7,4},{8,11},{9,10},{10,... | collective-permute-start | bytes 2359304 | tf_op jit(solution)/shard_map/ppermute | solution.py:35
  136.1 20.1 %all-to-all-start.1 = ((bf16[32,8,384]{2,1,0:T(8,128)(2,1)}), bf16[32,8,384]{2,1,0:T(8,128)(2,1)S(1)}, u32[]{:S(2)}, u32[]{:S(2)}) async-start(bf16[32,8,384]{2,1,0:T(8,128)(2,1)} %maximum_bitcast_fusion), calls=%async_computation.1 | async-start | bytes 393216 | tf_op jit(solution)/shard_map/all_to_all | solution.py:192
  147.0 1.2 copy-start.2
  148.3 15.5 %collective-permute-start.7 = (bf16[256,768]{1,0:T(8,128)(2,1)S(1)}, bf16[256,768]{1,0:T(8,128)(2,1)S(1)}, u32[]{:S(2)}, u32[]{:S(2)}) collective-permute-start(bf16[256,768]{1,0:T(8,128)(2,1)S(1)} %slice.88), channel_id=1, source_target_pairs={{0,4},{1,5},{2,6},{3,7},{4,0},{5,1},{6,2},{7,3},{8,12},{9,13},{10,... | collective-permute-start | bytes 1179656 | tf_op jit(solution)/shard_map/ppermute | solution.py:35
  164.4 21.2 %all-to-all-start.2 = ((bf16[32,8,384]{2,1,0:T(8,128)(2,1)}), bf16[32,8,384]{2,1,0:T(8,128)(2,1)S(1)}, u32[]{:S(2)}, u32[]{:S(2)}) async-start(bf16[32,8,384]{2,1,0:T(8,128)(2,1)} %broadcast_in_dim.8), calls=%async_computation.2 | async-start | bytes 393216 | tf_op jit(solution)/shard_map/all_to_all | solution.py:192
  175.1 9.8 %collective-permute-start.8 = (bf16[256,384]{1,0:T(8,128)(2,1)S(1)}, bf16[256,384]{1,0:T(8,128)(2,1)S(1)}, u32[]{:S(2)}, u32[]{:S(2)}) collective-permute-start(bf16[256,384]{1,0:T(8,128)(2,1)S(1)} %slice.89), channel_id=1, source_target_pairs={{0,12},{1,13},{2,14},{3,15},{4,8},{5,9},{6,10},{7,11},{8,4},{9,5},... | collective-permute-start | bytes 589832 | tf_op jit(solution)/shard_map/ppermute | solution.py:35
Sparse Core Ops, SparseCore 0:
  20.2 68.8 all-gather.1

commit v5 on v4

v5 whole, which is shorter than its diff:
```python
import functools

import jax
import jax.numpy as jnp
from jax import lax
from jax.experimental import pallas as pl
from jax.experimental.pallas import tpu as pltpu
from jax.sharding import PartitionSpec as P

adapter_scale = 2.0
f32, bf16 = jnp.float32, jnp.bfloat16

Z, YL, C = 8, 2, 2
YH, X = 4, 4


def gelu_slope(preact):
    normal_cdf = 0.5 * (1.0 + lax.erf(preact * 0.7071067811865476))
    density = jnp.exp(-0.5 * preact * preact) * 0.3989422804014327
    return normal_cdf + preact * density


def contract(left, right, left_dim, right_dim):
    return lax.dot_general(
        left, right, (((left_dim,), (right_dim,)), ((), ())), preferred_element_type=f32
    )


def send(value, step):
    pairs = []
    for device in range(Z * YL * C * YH * X):
        f, m = device // (YH * X), device % (YH * X)
        z, yl, c, yh, x = step(f // (YL * C), f // C % YL, f % C, m // X, m % X)
        pairs.append((device, ((z * YL + yl) * C + c) * YH * X + yh * X + x))
    return lax.ppermute(value, ("fsdp", "mp"), pairs)


PAIRS = [[z * YL * C + y * C + c for y in range(YL)] for z in range(Z) for c in range(C)]
PLANES = [[(z * YL + y) * C + c for z in range(Z) for c in range(C)] for y in range(YL)]


def first(c):
    return 1 if c else 3


def second(c):
    return 3 if c else 1


y_first = functools.partial(send, step=lambda z, yl, c, yh, x: (z, yl, c, yh ^ first(c), x))
y_second = functools.partial(send, step=lambda z, yl, c, yh, x: (z, yl, c, yh ^ second(c), x))
x_first = functools.partial(send, step=lambda z, yl, c, yh, x: (z, yl, c, yh, x ^ first(c)))
x_second = functools.partial(send, step=lambda z, yl, c, yh, x: (z, yl, c, yh, x ^ second(c)))


def row_copies(lies, w, held, sems, p):
    rows = w.shape[0] // 32
    copies = []
    for run in (2 * p, 2 * p + 1):
        source = w.at[pl.ds(pl.multiple_of(lies[run] * rows, rows), rows)]
        copies.append(pltpu.make_async_copy(source, held.at[pl.ds(run * rows, rows)], sems.at[run]))
    return copies


def start_blocks(lies, w, held, sems, count):
    for p in range(count):
        for copy in row_copies(lies, w, held, sems, p):
            copy.start()


def await_blocks(lies, w, held, sems, first_block):
    for p in (first_block, first_block + 1):
        for copy in row_copies(lies, w, held, sems, p):
            copy.wait()


def lowrank_sum(table, x_ref, down_t, base, low):
    width = x_ref.shape[1] // 8
    for p in range(8):
        there = pl.ds(pl.multiple_of(table[base + p] * width, width), width)
        low += contract(down_t[:, there], x_ref[:, p * width : (p + 1) * width], 1, 1)
    return low


def near_kernel(table, xa, down_t, low_out):
    low_out[...] = lowrank_sum(table, xa, down_t, 0, jnp.zeros(low_out.shape, f32))


def main_kernel(lies, table, xa, xb, w, low_near, down_t, up, act, slope_out, rank_out, up_out, held, acc, sems):
    rank = up.shape[0]
    wide = w.shape[0] // 8
    start_blocks(lies, w, held, sems, 16)

    low_t = lowrank_sum(table, xb, down_t, 8, low_near[...])
    lowrank_t, lowrank = low_t.astype(bf16), low_t.T.astype(bf16)
    acc[...] = adapter_scale * jnp.dot(lowrank, up[...], preferred_element_type=f32)
    for k in range(8):
        await_blocks(lies, w, held, sems, 2 * k)
        x_ref = xa if k < 4 else xb
        x = x_ref[:, k % 4 * wide : (k % 4 + 1) * wide]
        acc[...] += jnp.dot(x, held[k * wide : (k + 1) * wide], preferred_element_type=f32)

    slope = (act[...].astype(f32) * gelu_slope(acc[...])).astype(bf16)
    slope_out[...] = slope
    part = (adapter_scale * contract(up[...], slope, 1, 1)).astype(bf16)
    for copy in range(YH * X):
        rank_out[copy * rank : (copy + 1) * rank] = part
    up_out[...] = (adapter_scale * jnp.dot(lowrank_t, slope, preferred_element_type=f32)).astype(bf16)


VMEM = pl.BlockSpec(memory_space=pltpu.VMEM)
SMEM = pl.BlockSpec(memory_space=pltpu.SMEM)
HBM = pl.BlockSpec(memory_space=pltpu.HBM)


def near_lowrank(table, xa, down_t):
    rows, rank = xa.shape[0], down_t.shape[0]
    return pl.pallas_call(
        near_kernel,
        out_shape=jax.ShapeDtypeStruct((rank, rows), f32),
        in_specs=[SMEM, VMEM, VMEM],
        out_specs=VMEM,
        compiler_params=pltpu.CompilerParams(vmem_limit_bytes=56 * 2**20),
        cost_estimate=pl.CostEstimate(
            flops=2 * rows * rank * xa.shape[1], bytes_accessed=3 * 2**20, transcendentals=0
        ),
        name="near_lowrank",
    )(table, xa, down_t)


def forward(lies, table, xa, xb, w, low_near, down_t, up, act):
    rows, rank, hidden = xa.shape[0], up.shape[0], w.shape[1]
    return pl.pallas_call(
        main_kernel,
        out_shape=(
            jax.ShapeDtypeStruct((rows, hidden), bf16),
            jax.ShapeDtypeStruct((YH * X * rank, rows), bf16),
            jax.ShapeDtypeStruct((rank, hidden), bf16),
        ),
        in_specs=[SMEM, SMEM, VMEM, VMEM, HBM, VMEM, VMEM, VMEM, VMEM],
        out_specs=(VMEM, VMEM, VMEM),
        scratch_shapes=[
            pltpu.VMEM(w.shape, bf16),
            pltpu.VMEM((rows, hidden), f32),
            pltpu.SemaphoreType.DMA((32,)),
        ],
        compiler_params=pltpu.CompilerParams(vmem_limit_bytes=56 * 2**20),
        cost_estimate=pl.CostEstimate(
            flops=2 * rows * w.shape[0] * hidden, bytes_accessed=14 * 2**20, transcendentals=0
        ),
        name="forward",
    )(lies, table, xa, xb, w, low_near, down_t, up, act)


def frozen_kernel(lies, slope, w, kept, away, held, sems):
    wide = w.shape[0] // 8
    start_blocks(lies, w, held, sems, 16)
    for k in range(8):
        await_blocks(lies, w, held, sems, 2 * k)
        out = kept if k < 4 else away
        product = contract(slope[...], held[k * wide : (k + 1) * wide], 1, 1)
        out[:, k % 4 * wide : (k % 4 + 1) * wide] = product.astype(bf16)


def frozen_terms(lies, slope, w):
    rows, hidden = slope.shape
    half = jax.ShapeDtypeStruct((rows, w.shape[0] // 2), bf16)
    return pl.pallas_call(
        frozen_kernel,
        out_shape=(half, half),
        in_specs=[SMEM, VMEM, HBM],
        out_specs=(VMEM, VMEM),
        scratch_shapes=[pltpu.VMEM(w.shape, bf16), pltpu.SemaphoreType.DMA((32,))],
        compiler_params=pltpu.CompilerParams(vmem_limit_bytes=56 * 2**20),
        cost_estimate=pl.CostEstimate(
            flops=2 * rows * w.shape[0] * hidden, bytes_accessed=13 * 2**20, transcendentals=0
        ),
        name="frozen_terms",
    )(lies, slope, w)


def widen(value):
    return value.astype(f32)


def exchange(value, axis):
    return lax.all_to_all(value, axis, 0, 0, tiled=True)


def gather_small(value, axis, count):
    copies = jnp.broadcast_to(value[None], (count, *value.shape))
    return exchange(copies.reshape(-1, value.shape[1]), axis)


def add_parts(parts, count):
    return jnp.sum(widen(parts).reshape(count, -1, parts.shape[1]), axis=0).astype(bf16)


def body(normed_tokens, up_weight, adapter_down, adapter_up, act_grad):
    width = normed_tokens.shape[1]
    hidden = up_weight.shape[1]
    model_index = lax.axis_index("mp")
    core = lax.axis_index("fsdp") & 1
    y_hi, x_at = model_index >> 2, model_index & 3
    one, two = 3 - 2 * core, 1 + 2 * core

    step = [0 * core, one, two, 0 * core + 2]
    table = jnp.stack([((y_hi ^ step[r]) << 2) | (x_at ^ step[q]) for q in range(4) for r in range(4)])

    both = lax.all_gather(up_weight, "fsdp", axis=0, tiled=True, axis_index_groups=PAIRS)
    gathered = lax.all_gather(both, "fsdp", axis=0, tiled=True, axis_index_groups=PLANES)
    lies = jnp.stack([(table >> 1) * 4 + (table & 1) + 2 * c for c in range(C)], axis=1).reshape(-1)

    pair = jnp.concatenate([normed_tokens, y_first(normed_tokens)], axis=1)
    column = jnp.concatenate([pair, y_second(pair)], axis=1)
    near = jnp.concatenate([column, x_first(column)], axis=1)
    far = x_second(near)
    down_t = adapter_down.T
    low_near = near_lowrank(table, near, down_t)

    up_columns = lax.dynamic_slice_in_dim(adapter_up, model_index * hidden, hidden, 1)
    slope_grad, rank_shares, up_local = forward(
        lies, table, near, far, gathered, low_near, down_t, up_columns, act_grad
    )

    rank_parts = exchange(rank_shares, "mp")
    kept, away = frozen_terms(lies, slope_grad, gathered)
    over_x = x_second(away)
    rank_parts, _ = lax.optimization_barrier((rank_parts, away))
    rank_grad = add_parts(rank_parts, YH * X)
    rank = rank_grad.shape[0]
    down_local = jnp.dot(rank_grad, normed_tokens, preferred_element_type=f32).astype(bf16)
    shares = jnp.concatenate(
        [up_local[:, :width], up_local[:, width:], down_local, jnp.zeros_like(down_local)], axis=0
    )
    shares = exchange(shares, "fsdp")

    half = 4 * width
    to_next = (widen(kept[:, half:]) + widen(over_x[:, half:])).astype(bf16)
    over_next = x_first(to_next)
    shares, _ = lax.optimization_barrier((shares, to_next))
    members = Z * YL * C
    grads = gather_small(add_parts(shares, members), "fsdp", members)

    own = widen(kept[:, :half]) + widen(over_x[:, :half]) + widen(over_next)
    own, to_y = own[:, : 2 * width], own[:, 2 * width :].astype(bf16)
    over_y = y_second(to_y)

    own = own + widen(over_y)
    own, to_y = own[:, :width], own[:, width:].astype(bf16)
    over_last = y_first(to_y)
    down_rows = lax.dynamic_slice_in_dim(adapter_down, model_index * width, width, 0)
    own = own + contract(rank_grad, down_rows, 0, 1)
    own, over_last = lax.optimization_barrier((own, over_last))
    normed_grad = (own + widen(over_last)).astype(bf16)
    up_grad = jnp.concatenate([grads[:rank], grads[rank : 2 * rank]], axis=1)
    down_grad = grads[2 * rank : 3 * rank].T
    return (normed_grad, down_grad, up_grad)


def solution(mesh):
    placed = (P("fsdp", "mp"), P("fsdp", "mp"), P(), P(), P("fsdp", "mp"))
    return jax.shard_map(
        body,
        mesh=mesh,
        in_specs=placed,
        out_specs=(P("fsdp", "mp"), P("mp", None), P(None, "mp")),
        check_vma=False,
    )
```

time: 197 us -> 202 us (1.025)
  blocking collectives: 0 us -> 29.4 us
  starting transfers between devices: 69.8 us -> 43.6 us
  waiting for transfers between devices: 69.6 us -> 78.8 us
  other arithmetic: 10.6 us -> 6.21 us
    all_to_all x0 -> x1, blocking collectives: none -> 18 us  [exchange(): return lax.all_to_all(value, axis, 0, 0, tiled=True)]
    all_to_all x3 -> x2, waiting for transfers between devices: 2.51 us -> 19.9 us  [exchange(): return lax.all_to_all(value, axis, 0, 0, tiled=True)]
    all_to_all x3 -> x2, starting transfers between devices: 28.7 us -> 13.9 us  [exchange(): return lax.all_to_all(value, axis, 0, 0, tiled=True)]
    ppermute x9 -> x8, starting transfers between devices: 41.1 us -> 29.7 us  [send(): return lax.ppermute(value, ('fsdp', 'mp'), pairs)]
    all_gather x0 -> x1, blocking collectives: none -> 11.4 us  [body(): lax.all_gather(up_weight, 'fsdp', axis=0, tiled=True, axis_index_groups=P...]
    ppermute x9 -> x8, waiting for transfers between devices: 65.7 us -> 55.4 us  [send(): return lax.ppermute(value, ('fsdp', 'mp'), pairs)]
    all_gather x1, waiting for transfers between devices: 1.31 us -> 3.41 us  [body(): lax.all_gather(both, 'fsdp', axis=0, tiled=True, axis_index_groups=PLANES)]
  transfers between devices with their start and end apart: 13 -> 11, of which waited for: 10 -> 9; matrix products, arithmetic and copies ran while one was open for 7% -> 4% of each run, Pallas kernels for 5% -> 1%
where the time goes in v5:
time: 202 us; the launch traced here: 201 us
  waiting for transfers between devices  78.8 us (39%)
  starting transfers between devices  43.6 us (22%)
  blocking collectives  29.4 us (15%)
  Pallas kernels  22.4 us (11%)
  between operations  14.3 us (7%)
  other arithmetic  6.21 us (3%)
  local copies, waits for them, and re-layouts  4.61 us (2%)
    ppermute x8, waiting for transfers between devices, send(): return lax.ppermute(value, ('fsdp', 'mp'), pairs)  55.4 us
    ppermute x8, starting transfers between devices, send(): return lax.ppermute(value, ('fsdp', 'mp'), pairs)  29.7 us
    all_to_all x2, waiting for transfers between devices, exchange(): return lax.all_to_all(value, axis, 0, 0, tiled=True)  19.9 us
    all_to_all x1, blocking collectives, exchange(): return lax.all_to_all(value, axis, 0, 0, tiled=True)  18 us
    all_to_all x2, starting transfers between devices, exchange(): return lax.all_to_all(value, axis, 0, 0, tiled=True)  13.9 us
    all_gather x1, blocking collectives, body(): lax.all_gather(up_weight, 'fsdp', axis=0, tiled=True, axis_index_groups=P...  11.4 us
    pallas_call x1, Pallas kernels, forward(): pl.pallas_call(main_kernel, out_shape=(jax.ShapeDtypeStruct((rows, hidden...  10.9 us
    pallas_call x1, Pallas kernels, frozen_terms(): pl.pallas_call(frozen_kernel, out_shape=(half, half), in_specs=[SMEM, VME...  8.59 us
  transfers between devices with their start and end apart: 11, of which 9 were waited for; matrix products, arithmetic and copies ran while one was open for 4% of the time, Pallas kernels for 1%

profile of v5, /device:TPU:6, one launch (start us, length us, event | category | flops | bytes accessed | tf_op | source)
XLA Modules:
  0.0 200.5 jit_solution(8274716778540287709)
XLA Ops:
  7.2 11.4 %all_gather.6 = bf16[384,768]{1,0:T(8,128)(2,1)} all-gather(bf16[192,768]{1,0:T(8,128)(2,1)} %param.6), channel_id=1, replica_groups={{0,32},{16,48},{64,96},{80,112},{128,160},{144,176},{192,224},{208,240}..., dimensions={0}, use_global_device_ids=true | all-gather | bytes 884736 | tf_op jit(solution)/shard_map/all_gather | solution.py:210
  18.6 5.3 %collective-permute-start = (bf16[256,384]{1,0:T(8,128)(2,1)}, bf16[256,384]{1,0:T(8,128)(2,1)S(1)}, u32[]{:S(2)}, u32[]{:S(2)}) collective-permute-start(bf16[256,384]{1,0:T(8,128)(2,1)} %param.5), channel_id=1, source_target_pairs={{0,12},{1,13},{2,14},{3,15},{4,8},{5,9},{6,10},{7,11},{8,4},{9,5},... | collective-permute-start | bytes 589832 | tf_op jit(solution)/shard_map/ppermute | solution.py:35
  23.9 5.6 %collective-permute-done = bf16[256,384]{1,0:T(8,128)(2,1)S(1)} collective-permute-done((bf16[256,384]{1,0:T(8,128)(2,1)}, bf16[256,384]{1,0:T(8,128)(2,1)S(1)}, u32[]{:S(2)}, u32[]{:S(2)}) %collective-permute-start) | collective-permute-done | bytes 196640 | tf_op jit(solution)/shard_map/ppermute | solution.py:35
  29.6 5.6 %collective-permute-start.1 = (bf16[256,768]{1,0:T(8,128)(2,1)S(1)}, bf16[256,768]{1,0:T(8,128)(2,1)S(1)}, u32[]{:S(2)}, u32[]{:S(2)}) collective-permute-start(bf16[256,768]{1,0:T(8,128)(2,1)S(1)} %pad_maximum_fusion.1), channel_id=1, source_target_pairs={{0,4},{1,5},{2,6},{3,7},{4,0},{5,1},{6,2},{7,3},{8,12},{9,13},{10,... | collective-permute-start | bytes 1179656 | tf_op jit(solution)/shard_map/ppermute | solution.py:35
  35.1 10.0 %collective-permute-done.1 = bf16[256,768]{1,0:T(8,128)(2,1)S(1)} collective-permute-done((bf16[256,768]{1,0:T(8,128)(2,1)S(1)}, bf16[256,768]{1,0:T(8,128)(2,1)S(1)}, u32[]{:S(2)}, u32[]{:S(2)}) %collective-permute-start.1) | collective-permute-done | bytes 393248 | tf_op jit(solution)/shard_map/ppermute | solution.py:35
  45.2 1.9 collective-permute-start.2
  47.2 13.6 %collective-permute-done.2 = bf16[256,1536]{1,0:T(8,128)(2,1)S(1)} collective-permute-done((bf16[256,1536]{1,0:T(8,128)(2,1)S(1)}, bf16[256,1536]{1,0:T(8,128)(2,1)S(1)}, u32[]{:S(2)}, u32[]{:S(2)}) %collective-permute-start.2) | collective-permute-done | bytes 786464 | tf_op jit(solution)/shard_map/ppermute | solution.py:35
  60.9 1.9 collective-permute-start.3
  65.1 2.9 %near_lowrank.1.low_near = f32[64,256]{1,0:T(8,128)} custom-call(s32[16]{0:T(128)} %stack.124.table, bf16[256,3072]{1,0:T(8,128)(2,1)} %copy-done.1, bf16[64,6144]{1,0:T(8,128)(2,1)} %bitcast.52), custom_call_target="tpu_custom_call" | custom-call | flops 100663296 | bytes 3145728 | tf_op jit(solution)/shard_map/near_lowrank/pallas_call | solution.py:118
  68.0 15.3 %collective-permute-done.3.xb = bf16[256,3072]{1,0:T(8,128)(2,1)} collective-permute-done((bf16[256,3072]{1,0:T(8,128)(2,1)S(1)}, bf16[256,3072]{1,0:T(8,128)(2,1)}, u32[]{:S(2)}, u32[]{:S(2)}) %collective-permute-start.3) | collective-permute-done | bytes 1572896 | tf_op jit(solution)/shard_map/ppermute | solution.py:35
  83.3 3.4 %all-gather.2.cloned.1.call-done.w = bf16[6144,768]{1,0:T(8,128)(2,1)} async-done(((bf16[384,768]{1,0:T(8,128)(2,1)}), bf16[6144,768]{1,0:T(8,128)(2,1)}) %all-gather.2.cloned.1.call-update) | async-done | bytes 9437200 | tf_op jit(solution)/shard_map/all_gather | solution.py:211
  86.8 10.9 %forward.1 = (bf16[256,768]{1,0:T(8,128)(2,1)}, bf16[1024,256]{1,0:T(8,128)(2,1)}, bf16[64,768]{1,0:T(8,128)(2,1)}) custom-call(s32[32]{0:T(128)} %reshape.690.lies, s32[16]{0:T(128)} %stack.124.table, bf16[256,3072]{1,0:T(8,128)(2,1)} %copy-done.1, bf16[256,3072]{1,0:T(8,128)(2,1)} %collective-permute-done.3.xb, ...), custom_call_target="tpu_custom_call" | custom-call | flops 2415919104 | bytes 14680064 | tf_op jit(solution)/shard_map/forward/pallas_call | solution.py:133
  97.6 8.6 %frozen_terms.1 = (bf16[256,3072]{1,0:T(8,128)(2,1)}, bf16[256,3072]{1,0:T(8,128)(2,1)}) custom-call(s32[32]{0:T(128)} %reshape.690.lies, bf16[256,768]{1,0:T(8,128)(2,1)} %get-tuple-element.12.slope, bf16[6144,768]{1,0:T(8,128)(2,1)} %all-gather.2.cloned.1.call-done.w), custom_call_target="tpu_custom_call" | custom-call | flops 2415919104 | bytes 13631488 | tf_op jit(solution)/shard_map/frozen_terms/pallas_call | solution.py:168
  106.2 2.8 %collective-permute-start.4 = (bf16[256,3072]{1,0:T(8,128)(2,1)}, bf16[256,3072]{1,0:T(8,128)(2,1)}, u32[]{:S(2)}, u32[]{:S(2)}) collective-permute-start(bf16[256,3072]{1,0:T(8,128)(2,1)} %get-tuple-element.14), channel_id=1, source_target_pairs={{0,1},{1,0},{2,3},{3,2},{4,5},{5,4},{6,7},{7,6},{8,9},{9,8},{10,11... | collective-permute-start | bytes 4718600 | tf_op jit(solution)/shard_map/ppermute | solution.py:35
  109.0 10.0 %all-to-all-start = ((bf16[16,64,256]{2,1,0:T(8,128)(2,1)}), bf16[16,64,256]{2,1,0:T(8,128)(2,1)S(1)}, u32[]{:S(2)}, u32[]{:S(2)}) async-start(bf16[16,64,256]{2,1,0:T(8,128)(2,1)} %bitcast.33), calls=%async_computation | async-start | bytes 1048576 | tf_op jit(solution)/shard_map/all_to_all | solution.py:187
  119.2 15.4 %all-to-all-done = bf16[16,64,256]{2,1,0:T(8,128)(2,1)S(1)} async-done(((bf16[16,64,256]{2,1,0:T(8,128)(2,1)}), bf16[16,64,256]{2,1,0:T(8,128)(2,1)S(1)}, u32[]{:S(2)}, u32[]{:S(2)}) %all-to-all-start) | async-done | bytes 524320 | tf_op jit(solution)/shard_map/all_to_all | solution.py:187
  136.2 4.0 %collective-permute-start.5 = (bf16[256,1536]{1,0:T(8,128)(2,1)S(1)}, bf16[256,1536]{1,0:T(8,128)(2,1)}, u32[]{:S(2)}, u32[]{:S(2)}) collective-permute-start(bf16[256,1536]{1,0:T(8,128)(2,1)S(1)} %add_convert_fusion), channel_id=1, source_target_pairs={{0,3},{1,2},{2,1},{3,0},{4,7},{5,6},{6,5},{7,4},{8,11},{9,10},{10,... | collective-permute-start | bytes 2359304 | tf_op jit(solution)/shard_map/ppermute | solution.py:35
  140.5 18.0 %all_to_all.30 = bf16[32,8,384]{2,1,0:T(8,128)(2,1)S(1)} all-to-all(bf16[32,8,384]{2,1,0:T(8,128)(2,1)S(1)} %maximum_bitcast_fusion), channel_id=1, replica_groups=mesh['fsdp'=32,'mp'=16] {'fsdp'}, dimensions={0} | all-to-all | bytes 393216 | tf_op jit(solution)/shard_map/all_to_all | solution.py:187
  159.3 3.9 %all-to-all-start.2 = ((bf16[32,8,384]{2,1,0:T(8,128)(2,1)}), bf16[32,8,384]{2,1,0:T(8,128)(2,1)S(1)}, u32[]{:S(2)}, u32[]{:S(2)}) async-start(bf16[32,8,384]{2,1,0:T(8,128)(2,1)} %broadcast_in_dim.10), calls=%async_computation.2 | async-start | bytes 393216 | tf_op jit(solution)/shard_map/all_to_all | solution.py:187
  165.9 3.7 %collective-permute-start.6 = (bf16[256,768]{1,0:T(8,128)(2,1)}, bf16[256,768]{1,0:T(8,128)(2,1)}, u32[]{:S(2)}, u32[]{:S(2)}) collective-permute-start(bf16[256,768]{1,0:T(8,128)(2,1)} %slice.86), channel_id=1, source_target_pairs={{0,4},{1,5},{2,6},{3,7},{4,0},{5,1},{6,2},{7,3},{8,12},{9,13},{10,... | collective-permute-start | bytes 1179656 | tf_op jit(solution)/shard_map/ppermute | solution.py:35
  169.6 4.5 %all-to-all-done.2 = bf16[32,8,384]{2,1,0:T(8,128)(2,1)S(1)} async-done(((bf16[32,8,384]{2,1,0:T(8,128)(2,1)}), bf16[32,8,384]{2,1,0:T(8,128)(2,1)S(1)}, u32[]{:S(2)}, u32[]{:S(2)}) %all-to-all-start.2) | async-done | bytes 196640 | tf_op jit(solution)/shard_map/all_to_all | solution.py:187
  175.4 4.8 %collective-permute-done.6 = bf16[256,768]{1,0:T(8,128)(2,1)} collective-permute-done((bf16[256,768]{1,0:T(8,128)(2,1)}, bf16[256,768]{1,0:T(8,128)(2,1)}, u32[]{:S(2)}, u32[]{:S(2)}) %collective-permute-start.6) | collective-permute-done | bytes 393248 | tf_op jit(solution)/shard_map/ppermute | solution.py:35
  181.3 4.4 %collective-permute-start.7 = (bf16[256,384]{1,0:T(8,128)(2,1)S(1)}, bf16[256,384]{1,0:T(8,128)(2,1)S(1)}, u32[]{:S(2)}, u32[]{:S(2)}) collective-permute-start(bf16[256,384]{1,0:T(8,128)(2,1)S(1)} %slice.87), channel_id=1, source_target_pairs={{0,12},{1,13},{2,14},{3,15},{4,8},{5,9},{6,10},{7,11},{8,4},{9,5},... | collective-permute-start | bytes 589832 | tf_op jit(solution)/shard_map/ppermute | solution.py:35
  186.8 6.2 %collective-permute-done.7 = bf16[256,384]{1,0:T(8,128)(2,1)S(1)} collective-permute-done((bf16[256,384]{1,0:T(8,128)(2,1)S(1)}, bf16[256,384]{1,0:T(8,128)(2,1)S(1)}, u32[]{:S(2)}, u32[]{:S(2)}) %collective-permute-start.7) | collective-permute-done | bytes 196640 | tf_op jit(solution)/shard_map/ppermute | solution.py:35
  (42 shorter events, 12.1 us)
Async XLA Ops:
  7.2 57.3 %copy-start = (bf16[64,12288]{1,0:T(8,128)(2,1)S(1)}, bf16[64,12288]{1,0:T(8,128)(2,1)}, u32[]{:S(2)}) copy-start(bf16[64,12288]{1,0:T(8,128)(2,1)} %param.8) | copy-start | bytes 4718596
  7.2 22.3 %copy-start.2 = (bf16[256,384]{1,0:T(8,128)(2,1)S(1)}, bf16[256,384]{1,0:T(8,128)(2,1)}, u32[]{:S(2)}) copy-start(bf16[256,384]{1,0:T(8,128)(2,1)} %param.5) | copy-start | bytes 589828
  7.2 79.6 %all-gather.2.cloned.1.call-start = ((), (), s32[]{:S(2)}) async-start(), calls=%async_computation.3 | async-start | bytes 10027008 | tf_op jit(solution)/shard_map/all_gather | solution.py:211
  18.6 10.9 %collective-permute-start = (bf16[256,384]{1,0:T(8,128)(2,1)}, bf16[256,384]{1,0:T(8,128)(2,1)S(1)}, u32[]{:S(2)}, u32[]{:S(2)}) collective-permute-start(bf16[256,384]{1,0:T(8,128)(2,1)} %param.5), channel_id=1, source_target_pairs={{0,12},{1,13},{2,14},{3,15},{4,8},{5,9},{6,10},{7,11},{8,4},{9,5},... | collective-permute-start | bytes 589832 | tf_op jit(solution)/shard_map/ppermute | solution.py:35
  29.6 15.5 %collective-permute-start.1 = (bf16[256,768]{1,0:T(8,128)(2,1)S(1)}, bf16[256,768]{1,0:T(8,128)(2,1)S(1)}, u32[]{:S(2)}, u32[]{:S(2)}) collective-permute-start(bf16[256,768]{1,0:T(8,128)(2,1)S(1)} %pad_maximum_fusion.1), channel_id=1, source_target_pairs={{0,4},{1,5},{2,6},{3,7},{4,0},{5,1},{6,2},{7,3},{8,12},{9,13},{10,... | collective-permute-start | bytes 1179656 | tf_op jit(solution)/shard_map/ppermute | solution.py:35
  45.2 15.6 %collective-permute-start.2 = (bf16[256,1536]{1,0:T(8,128)(2,1)S(1)}, bf16[256,1536]{1,0:T(8,128)(2,1)S(1)}, u32[]{:S(2)}, u32[]{:S(2)}) collective-permute-start(bf16[256,1536]{1,0:T(8,128)(2,1)S(1)} %pad_maximum_fusion), channel_id=1, source_target_pairs={{0,3},{1,2},{2,1},{3,0},{4,7},{5,6},{6,5},{7,4},{8,11},{9,10},{10,... | collective-permute-start | bytes 2359304 | tf_op jit(solution)/shard_map/ppermute | solution.py:35
  60.9 4.2 %copy-start.1 = (bf16[256,3072]{1,0:T(8,128)(2,1)}, bf16[256,3072]{1,0:T(8,128)(2,1)S(1)}, u32[]{:S(2)}) copy-start(bf16[256,3072]{1,0:T(8,128)(2,1)S(1)} %constant_dynamic-update-slice_fusion.xa) | copy-start | bytes 4718596
  60.9 22.4 %collective-permute-start.3 = (bf16[256,3072]{1,0:T(8,128)(2,1)S(1)}, bf16[256,3072]{1,0:T(8,128)(2,1)}, u32[]{:S(2)}, u32[]{:S(2)}) collective-permute-start(bf16[256,3072]{1,0:T(8,128)(2,1)S(1)} %constant_dynamic-update-slice_fusion.xa), channel_id=1, source_target_pairs={{0,1},{1,0},{2,3},{3,2},{4,5},{5,4},{6,7},{7,6},{8,9},{9,8},{10,11... | collective-permute-start | bytes 4718600 | tf_op jit(solution)/shard_map/ppermute | solution.py:35
  97.6 21.5 %copy-start.3 = (bf16[64,768]{1,0:T(8,128)(2,1)S(1)}, bf16[64,768]{1,0:T(8,128)(2,1)}, u32[]{:S(2)}) copy-start(bf16[64,768]{1,0:T(8,128)(2,1)} %get-tuple-element.19) | copy-start | bytes 294916
  106.2 28.4 %collective-permute-start.4 = (bf16[256,3072]{1,0:T(8,128)(2,1)}, bf16[256,3072]{1,0:T(8,128)(2,1)}, u32[]{:S(2)}, u32[]{:S(2)}) collective-permute-start(bf16[256,3072]{1,0:T(8,128)(2,1)} %get-tuple-element.14), channel_id=1, source_target_pairs={{0,1},{1,0},{2,3},{3,2},{4,5},{5,4},{6,7},{7,6},{8,9},{9,8},{10,11... | collective-permute-start | bytes 4718600 | tf_op jit(solution)/shard_map/ppermute | solution.py:35
  109.0 25.5 %all-to-all-start = ((bf16[16,64,256]{2,1,0:T(8,128)(2,1)}), bf16[16,64,256]{2,1,0:T(8,128)(2,1)S(1)}, u32[]{:S(2)}, u32[]{:S(2)}) async-start(bf16[16,64,256]{2,1,0:T(8,128)(2,1)} %bitcast.33), calls=%async_computation | async-start | bytes 1048576 | tf_op jit(solution)/shard_map/all_to_all | solution.py:187
  136.2 27.0 %collective-permute-start.5 = (bf16[256,1536]{1,0:T(8,128)(2,1)S(1)}, bf16[256,1536]{1,0:T(8,128)(2,1)}, u32[]{:S(2)}, u32[]{:S(2)}) collective-permute-start(bf16[256,1536]{1,0:T(8,128)(2,1)S(1)} %add_convert_fusion), channel_id=1, source_target_pairs={{0,3},{1,2},{2,1},{3,0},{4,7},{5,6},{6,5},{7,4},{8,11},{9,10},{10,... | collective-permute-start | bytes 2359304 | tf_op jit(solution)/shard_map/ppermute | solution.py:35
  159.3 14.8 %all-to-all-start.2 = ((bf16[32,8,384]{2,1,0:T(8,128)(2,1)}), bf16[32,8,384]{2,1,0:T(8,128)(2,1)S(1)}, u32[]{:S(2)}, u32[]{:S(2)}) async-start(bf16[32,8,384]{2,1,0:T(8,128)(2,1)} %broadcast_in_dim.10), calls=%async_computation.2 | async-start | bytes 393216 | tf_op jit(solution)/shard_map/all_to_all | solution.py:187
  165.9 14.3 %collective-permute-start.6 = (bf16[256,768]{1,0:T(8,128)(2,1)}, bf16[256,768]{1,0:T(8,128)(2,1)}, u32[]{:S(2)}, u32[]{:S(2)}) collective-permute-start(bf16[256,768]{1,0:T(8,128)(2,1)} %slice.86), channel_id=1, source_target_pairs={{0,4},{1,5},{2,6},{3,7},{4,0},{5,1},{6,2},{7,3},{8,12},{9,13},{10,... | collective-permute-start | bytes 1179656 | tf_op jit(solution)/shard_map/ppermute | solution.py:35
  181.3 11.7 %collective-permute-start.7 = (bf16[256,384]{1,0:T(8,128)(2,1)S(1)}, bf16[256,384]{1,0:T(8,128)(2,1)S(1)}, u32[]{:S(2)}, u32[]{:S(2)}) collective-permute-start(bf16[256,384]{1,0:T(8,128)(2,1)S(1)} %slice.87), channel_id=1, source_target_pairs={{0,12},{1,13},{2,14},{3,15},{4,8},{5,9},{6,10},{7,11},{8,4},{9,5},... | collective-permute-start | bytes 589832 | tf_op jit(solution)/shard_map/ppermute | solution.py:35
Sparse Core Ops, SparseCore 0:
  18.7 67.9 all-gather.1

commit v6 on v5

--- a/solution.py
+++ b/solution.py
@@ -86,7 +86,7 @@
     low_out[...] = lowrank_sum(table, xa, down_t, 0, jnp.zeros(low_out.shape, f32))
 
 
-def main_kernel(lies, table, xa, xb, w, low_near, down_t, up, act, slope_out, rank_out, up_out, held, acc, sems):
+def main_kernel(lies, table, xa, xb, w, low_near, down_t, up, act, slope_out, rank_out, up_out, away, held, acc, sems):
     rank = up.shape[0]
     wide = w.shape[0] // 8
     start_blocks(lies, w, held, sems, 16)
@@ -106,6 +106,10 @@
     for copy in range(YH * X):
         rank_out[copy * rank : (copy + 1) * rank] = part
     up_out[...] = (adapter_scale * jnp.dot(lowrank_t, slope, preferred_element_type=f32)).astype(bf16)
+
+    for k in range(4):
+        rows = held[(4 + k) * wide : (5 + k) * wide]
+        away[:, k * wide : (k + 1) * wide] = contract(slope, rows, 1, 1).astype(bf16)
 
 
 VMEM = pl.BlockSpec(memory_space=pltpu.VMEM)
@@ -136,9 +140,10 @@
             jax.ShapeDtypeStruct((rows, hidden), bf16),
             jax.ShapeDtypeStruct((YH * X * rank, rows), bf16),
             jax.ShapeDtypeStruct((rank, hidden), bf16),
+            jax.ShapeDtypeStruct(xa.shape, bf16),
         ),
         in_specs=[SMEM, SMEM, VMEM, VMEM, HBM, VMEM, VMEM, VMEM, VMEM],
-        out_specs=(VMEM, VMEM, VMEM),
+        out_specs=(VMEM, VMEM, VMEM, VMEM),
         scratch_shapes=[
             pltpu.VMEM(w.shape, bf16),
             pltpu.VMEM((rows, hidden), f32),
@@ -146,36 +151,35 @@
         ],
         compiler_params=pltpu.CompilerParams(vmem_limit_bytes=56 * 2**20),
         cost_estimate=pl.CostEstimate(
-            flops=2 * rows * w.shape[0] * hidden, bytes_accessed=14 * 2**20, transcendentals=0
+            flops=3 * rows * w.shape[0] * hidden, bytes_accessed=14 * 2**20, transcendentals=0
         ),
         name="forward",
     )(lies, table, xa, xb, w, low_near, down_t, up, act)
 
 
-def frozen_kernel(lies, slope, w, kept, away, held, sems):
+def kept_kernel(lies, slope, w, out, held, sems):
     wide = w.shape[0] // 8
-    start_blocks(lies, w, held, sems, 16)
-    for k in range(8):
+    start_blocks(lies, w, held, sems, 8)
+    for k in range(4):
         await_blocks(lies, w, held, sems, 2 * k)
-        out = kept if k < 4 else away
-        product = contract(slope[...], held[k * wide : (k + 1) * wide], 1, 1)
-        out[:, k % 4 * wide : (k % 4 + 1) * wide] = product.astype(bf16)
-
-
-def frozen_terms(lies, slope, w):
+        rows = held[k * wide : (k + 1) * wide]
+        out[:, k * wide : (k + 1) * wide] = contract(slope[...], rows, 1, 1).astype(bf16)
+
+
+def kept_half(lies, slope, w):
     rows, hidden = slope.shape
-    half = jax.ShapeDtypeStruct((rows, w.shape[0] // 2), bf16)
+    half = w.shape[0] // 2
     return pl.pallas_call(
-        frozen_kernel,
-        out_shape=(half, half),
+        kept_kernel,
+        out_shape=jax.ShapeDtypeStruct((rows, half), bf16),
         in_specs=[SMEM, VMEM, HBM],
-        out_specs=(VMEM, VMEM),
-        scratch_shapes=[pltpu.VMEM(w.shape, bf16), pltpu.SemaphoreType.DMA((32,))],
+        out_specs=VMEM,
+        scratch_shapes=[pltpu.VMEM((half, hidden), bf16), pltpu.SemaphoreType.DMA((16,))],
         compiler_params=pltpu.CompilerParams(vmem_limit_bytes=56 * 2**20),
         cost_estimate=pl.CostEstimate(
-            flops=2 * rows * w.shape[0] * hidden, bytes_accessed=13 * 2**20, transcendentals=0
-        ),
-        name="frozen_terms",
+            flops=2 * rows * half * hidden, bytes_accessed=7 * 2**20, transcendentals=0
+        ),
+        name="kept_half",
     )(lies, slope, w)
 
 
@@ -219,14 +223,18 @@
     low_near = near_lowrank(table, near, down_t)
 
     up_columns = lax.dynamic_slice_in_dim(adapter_up, model_index * hidden, hidden, 1)
-    slope_grad, rank_shares, up_local = forward(
+    slope_grad, rank_shares, up_local, away = forward(
         lies, table, near, far, gathered, low_near, down_t, up_columns, act_grad
     )
 
+    over_x = x_second(away)
     rank_parts = exchange(rank_shares, "mp")
-    kept, away = frozen_terms(lies, slope_grad, gathered)
-    over_x = x_second(away)
-    rank_parts, _ = lax.optimization_barrier((rank_parts, away))
+    kept = kept_half(lies, slope_grad, gathered)
+    half = 4 * width
+    to_next = (widen(kept[:, half:]) + widen(over_x[:, half:])).astype(bf16)
+    over_next = x_first(to_next)
+
+    rank_parts, _ = lax.optimization_barrier((rank_parts, to_next))
     rank_grad = add_parts(rank_parts, YH * X)
     rank = rank_grad.shape[0]
     down_local = jnp.dot(rank_grad, normed_tokens, preferred_element_type=f32).astype(bf16)
@@ -235,23 +243,19 @@
     )
     shares = exchange(shares, "fsdp")
 
-    half = 4 * width
-    to_next = (widen(kept[:, half:]) + widen(over_x[:, half:])).astype(bf16)
-    over_next = x_first(to_next)
-    shares, _ = lax.optimization_barrier((shares, to_next))
-    members = Z * YL * C
-    grads = gather_small(add_parts(shares, members), "fsdp", members)
-
     own = widen(kept[:, :half]) + widen(over_x[:, :half]) + widen(over_next)
     own, to_y = own[:, : 2 * width], own[:, 2 * width :].astype(bf16)
     over_y = y_second(to_y)
+    shares, _ = lax.optimization_barrier((shares, to_y))
+    members = Z * YL * C
+    grads = gather_small(add_parts(shares, members), "fsdp", members)
 
     own = own + widen(over_y)
     own, to_y = own[:, :width], own[:, width:].astype(bf16)
     over_last = y_first(to_y)
     down_rows = lax.dynamic_slice_in_dim(adapter_down, model_index * width, width, 0)
     own = own + contract(rank_grad, down_rows, 0, 1)
-    own, over_last = lax.optimization_barrier((own, over_last))
+    own, over_last, grads = lax.optimization_barrier((own, over_last, grads))
     normed_grad = (own + widen(over_last)).astype(bf16)
     up_grad = jnp.concatenate([grads[:rank], grads[rank : 2 * rank]], axis=1)
     down_grad = grads[2 * rank : 3 * rank].T

time: 202 us -> 186 us (0.921)
  blocking collectives: 29.4 us -> 11.3 us
  waiting for transfers between devices: 78.8 us -> 66 us
  starting transfers between devices: 43.6 us -> 54.3 us
  other arithmetic: 6.21 us -> 8.73 us
    all_to_all x1 -> x0, blocking collectives: 18 us -> none  [exchange(): return lax.all_to_all(value, axis, 0, 0, tiled=True)]
    all_to_all x2 -> x3, waiting for transfers between devices: 19.9 us -> 2.29 us  [exchange(): return lax.all_to_all(value, axis, 0, 0, tiled=True)]
    all_to_all x2 -> x3, starting transfers between devices: 13.9 us -> 24.2 us  [exchange(): return lax.all_to_all(value, axis, 0, 0, tiled=True)]
    ppermute x8, waiting for transfers between devices: 55.4 us -> 60.3 us  [send(): return lax.ppermute(value, ('fsdp', 'mp'), pairs)]
    pallas_call x1, Pallas kernels: 10.9 us -> 13.9 us  [forward(): pl.pallas_call(main_kernel, out_shape=(jax.ShapeDtypeStruct((rows, hidden...]
    pallas_call x1, Pallas kernels: 8.59 us -> 5.97 us  [kept_half(): pl.pallas_call(kept_kernel, out_shape=jax.ShapeDtypeStruct((rows, half),...]
  transfers between devices with their start and end apart: 11 -> 12, of which waited for: 9 -> 11; matrix products, arithmetic and copies ran while one was open for 4% -> 6% of each run, Pallas kernels for 1% -> 5%
where the time goes in v6:
time: 186 us; the launch traced here: 184 us
  waiting for transfers between devices  66 us (35%)
  starting transfers between devices  54.3 us (29%)
  Pallas kernels  22.8 us (12%)
  between operations  14.3 us (8%)
  blocking collectives  11.3 us (6%)
  other arithmetic  8.73 us (5%)
  local copies, waits for them, and re-layouts  4.94 us (3%)
    ppermute x8, waiting for transfers between devices, send(): return lax.ppermute(value, ('fsdp', 'mp'), pairs)  60.3 us
    ppermute x8, starting transfers between devices, send(): return lax.ppermute(value, ('fsdp', 'mp'), pairs)  30.1 us
    all_to_all x3, starting transfers between devices, exchange(): return lax.all_to_all(value, axis, 0, 0, tiled=True)  24.2 us
    pallas_call x1, Pallas kernels, forward(): pl.pallas_call(main_kernel, out_shape=(jax.ShapeDtypeStruct((rows, hidden...  13.9 us
    all_gather x1, blocking collectives, body(): lax.all_gather(up_weight, 'fsdp', axis=0, tiled=True, axis_index_groups=P...  11.3 us
    pallas_call x1, Pallas kernels, kept_half(): pl.pallas_call(kept_kernel, out_shape=jax.ShapeDtypeStruct((rows, half),...  5.97 us
  transfers between devices with their start and end apart: 12, of which 11 were waited for; matrix products, arithmetic and copies ran while one was open for 6% of the time, Pallas kernels for 5%

profile of v6, /device:TPU:6, one launch (start us, length us, event | category | flops | bytes accessed | tf_op | source)
XLA Modules:
  0.0 183.7 jit_solution(2417855373896201930)
XLA Ops:
  7.2 11.3 %all_gather.6 = bf16[384,768]{1,0:T(8,128)(2,1)} all-gather(bf16[192,768]{1,0:T(8,128)(2,1)} %param.6), channel_id=1, replica_groups={{0,32},{16,48},{64,96},{80,112},{128,160},{144,176},{192,224},{208,240}..., dimensions={0}, use_global_device_ids=true | all-gather | bytes 884736 | tf_op jit(solution)/shard_map/all_gather | solution.py:214
  18.6 5.3 %collective-permute-start = (bf16[256,384]{1,0:T(8,128)(2,1)}, bf16[256,384]{1,0:T(8,128)(2,1)S(1)}, u32[]{:S(2)}, u32[]{:S(2)}) collective-permute-start(bf16[256,384]{1,0:T(8,128)(2,1)} %param.5), channel_id=1, source_target_pairs={{0,12},{1,13},{2,14},{3,15},{4,8},{5,9},{6,10},{7,11},{8,4},{9,5},... | collective-permute-start | bytes 589832 | tf_op jit(solution)/shard_map/ppermute | solution.py:35
  23.9 5.6 %collective-permute-done = bf16[256,384]{1,0:T(8,128)(2,1)S(1)} collective-permute-done((bf16[256,384]{1,0:T(8,128)(2,1)}, bf16[256,384]{1,0:T(8,128)(2,1)S(1)}, u32[]{:S(2)}, u32[]{:S(2)}) %collective-permute-start) | collective-permute-done | bytes 196640 | tf_op jit(solution)/shard_map/ppermute | solution.py:35
  29.5 5.6 %collective-permute-start.1 = (bf16[256,768]{1,0:T(8,128)(2,1)S(1)}, bf16[256,768]{1,0:T(8,128)(2,1)S(1)}, u32[]{:S(2)}, u32[]{:S(2)}) collective-permute-start(bf16[256,768]{1,0:T(8,128)(2,1)S(1)} %pad_maximum_fusion.1), channel_id=1, source_target_pairs={{0,4},{1,5},{2,6},{3,7},{4,0},{5,1},{6,2},{7,3},{8,12},{9,13},{10,... | collective-permute-start | bytes 1179656 | tf_op jit(solution)/shard_map/ppermute | solution.py:35
  35.1 10.0 %collective-permute-done.1 = bf16[256,768]{1,0:T(8,128)(2,1)S(1)} collective-permute-done((bf16[256,768]{1,0:T(8,128)(2,1)S(1)}, bf16[256,768]{1,0:T(8,128)(2,1)S(1)}, u32[]{:S(2)}, u32[]{:S(2)}) %collective-permute-start.1) | collective-permute-done | bytes 393248 | tf_op jit(solution)/shard_map/ppermute | solution.py:35
  45.2 1.9 %collective-permute-start.2 = (bf16[256,1536]{1,0:T(8,128)(2,1)S(1)}, bf16[256,1536]{1,0:T(8,128)(2,1)S(1)}, u32[]{:S(2)}, u32[]{:S(2)}) collective-permute-start(bf16[256,1536]{1,0:T(8,128)(2,1)S(1)} %pad_maximum_fusion), channel_id=1, source_target_pairs={{0,3},{1,2},{2,1},{3,0},{4,7},{5,6},{6,5},{7,4},{8,11},{9,10},{10,... | collective-permute-start | bytes 2359304 | tf_op jit(solution)/shard_map/ppermute | solution.py:35
  47.2 13.6 %collective-permute-done.2 = bf16[256,1536]{1,0:T(8,128)(2,1)S(1)} collective-permute-done((bf16[256,1536]{1,0:T(8,128)(2,1)S(1)}, bf16[256,1536]{1,0:T(8,128)(2,1)S(1)}, u32[]{:S(2)}, u32[]{:S(2)}) %collective-permute-start.2) | collective-permute-done | bytes 786464 | tf_op jit(solution)/shard_map/ppermute | solution.py:35
  60.9 1.9 %collective-permute-start.3 = (bf16[256,3072]{1,0:T(8,128)(2,1)S(1)}, bf16[256,3072]{1,0:T(8,128)(2,1)}, u32[]{:S(2)}, u32[]{:S(2)}) collective-permute-start(bf16[256,3072]{1,0:T(8,128)(2,1)S(1)} %constant_dynamic-update-slice_fusion.xa), channel_id=1, source_target_pairs={{0,1},{1,0},{2,3},{3,2},{4,5},{5,4},{6,7},{7,6},{8,9},{9,8},{10,11... | collective-permute-start | bytes 4718600 | tf_op jit(solution)/shard_map/ppermute | solution.py:35
  65.0 2.9 %near_lowrank.1.low_near = f32[64,256]{1,0:T(8,128)} custom-call(s32[16]{0:T(128)} %stack.124.table, bf16[256,3072]{1,0:T(8,128)(2,1)} %copy-done.1, bf16[64,6144]{1,0:T(8,128)(2,1)} %bitcast.47), custom_call_target="tpu_custom_call" | custom-call | flops 100663296 | bytes 3145728 | tf_op jit(solution)/shard_map/near_lowrank/pallas_call | solution.py:122
  67.9 15.4 %collective-permute-done.3.xb = bf16[256,3072]{1,0:T(8,128)(2,1)} collective-permute-done((bf16[256,3072]{1,0:T(8,128)(2,1)S(1)}, bf16[256,3072]{1,0:T(8,128)(2,1)}, u32[]{:S(2)}, u32[]{:S(2)}) %collective-permute-start.3) | collective-permute-done | bytes 1572896 | tf_op jit(solution)/shard_map/ppermute | solution.py:35
  83.3 3.4 %all-gather.2.cloned.1.call-done.w = bf16[6144,768]{1,0:T(8,128)(2,1)} async-done(((bf16[384,768]{1,0:T(8,128)(2,1)}), bf16[6144,768]{1,0:T(8,128)(2,1)}) %all-gather.2.cloned.1.call-update) | async-done | bytes 9437200 | tf_op jit(solution)/shard_map/all_gather | solution.py:215
  86.7 13.9 %forward.1 = (bf16[256,768]{1,0:T(8,128)(2,1)}, bf16[1024,256]{1,0:T(8,128)(2,1)}, bf16[64,768]{1,0:T(8,128)(2,1)}, bf16[256,3072]{1,0:T(8,128)(2,1)}) custom-call(s32[32]{0:T(128)} %reshape.687.lies, s32[16]{0:T(128)} %stack.124.table, bf16[256,3072]{1,0:T(8,128)(2,1)} %copy-done.1, bf16[256,3072]{1,0:T(8,128)(2,1)} %collective-permute-done.3.xb, ...), custom_call_target="tpu_custom_call" | custom-call | flops 3623878656 | bytes 14680064 | tf_op jit(solution)/shard_map/forward/pallas_call | solution.py:137
  100.6 2.8 %collective-permute-start.4 = (bf16[256,3072]{1,0:T(8,128)(2,1)}, bf16[256,3072]{1,0:T(8,128)(2,1)}, u32[]{:S(2)}, u32[]{:S(2)}) collective-permute-start(bf16[256,3072]{1,0:T(8,128)(2,1)} %get-tuple-element.13), channel_id=1, source_target_pairs={{0,1},{1,0},{2,3},{3,2},{4,5},{5,4},{6,7},{7,6},{8,9},{9,8},{10,11... | collective-permute-start | bytes 4718600 | tf_op jit(solution)/shard_map/ppermute | solution.py:35
  103.4 10.0 %all-to-all-start = ((bf16[16,64,256]{2,1,0:T(8,128)(2,1)}), bf16[16,64,256]{2,1,0:T(8,128)(2,1)}, u32[]{:S(2)}, u32[]{:S(2)}) async-start(bf16[16,64,256]{2,1,0:T(8,128)(2,1)} %bitcast.51), calls=%async_computation | async-start | bytes 1048576 | tf_op jit(solution)/shard_map/all_to_all | solution.py:191
  113.5 6.0 %kept_half.1 = bf16[256,3072]{1,0:T(8,128)(2,1)} custom-call(s32[32]{0:T(128)} %reshape.687.lies, bf16[256,768]{1,0:T(8,128)(2,1)} %get-tuple-element.12.slope, bf16[6144,768]{1,0:T(8,128)(2,1)} %all-gather.2.cloned.1.call-done.w), custom_call_target="tpu_custom_call" | custom-call | flops 1207959552 | bytes 7340032 | tf_op jit(solution)/shard_map/kept_half/pallas_call | solution.py:172
  119.5 8.1 %collective-permute-done.4 = bf16[256,3072]{1,0:T(8,128)(2,1)} collective-permute-done((bf16[256,3072]{1,0:T(8,128)(2,1)}, bf16[256,3072]{1,0:T(8,128)(2,1)}, u32[]{:S(2)}, u32[]{:S(2)}) %collective-permute-start.4) | collective-permute-done | bytes 1572896 | tf_op jit(solution)/shard_map/ppermute | solution.py:35
  127.6 2.5 %add_convert_fusion = bf16[256,1536]{1,0:T(8,128)(2,1)} fusion(bf16[256,3072]{1,0:T(8,128)(2,1)} %collective-permute-done.4, bf16[256,3072]{1,0:T(8,128)(2,1)} %kept_half.1), kind=kLoop, calls=%fused_computation.1 | loop fusion | flops 1572864 | bytes 2359296 | tf_op jit(solution)/shard_map/convert_element_type | solution.py:234
  130.1 2.7 %collective-permute-start.5 = (bf16[256,1536]{1,0:T(8,128)(2,1)}, bf16[256,1536]{1,0:T(8,128)(2,1)}, u32[]{:S(2)}, u32[]{:S(2)}) collective-permute-start(bf16[256,1536]{1,0:T(8,128)(2,1)} %add_convert_fusion), channel_id=1, source_target_pairs={{0,3},{1,2},{2,1},{3,0},{4,7},{5,6},{6,5},{7,4},{8,11},{9,10},{10,... | collective-permute-start | bytes 2359304 | tf_op jit(solution)/shard_map/ppermute | solution.py:35
  135.0 7.6 %all-to-all-start.1 = ((bf16[32,8,384]{2,1,0:T(8,128)(2,1)}), bf16[32,8,384]{2,1,0:T(8,128)(2,1)S(1)}, u32[]{:S(2)}, u32[]{:S(2)}) async-start(bf16[32,8,384]{2,1,0:T(8,128)(2,1)} %maximum_bitcast_fusion), calls=%async_computation.1 | async-start | bytes 393216 | tf_op jit(solution)/shard_map/all_to_all | solution.py:191
  142.6 2.9 %collective-permute-done.5 = bf16[256,1536]{1,0:T(8,128)(2,1)} collective-permute-done((bf16[256,1536]{1,0:T(8,128)(2,1)}, bf16[256,1536]{1,0:T(8,128)(2,1)}, u32[]{:S(2)}, u32[]{:S(2)}) %collective-permute-start.5) | collective-permute-done | bytes 786464 | tf_op jit(solution)/shard_map/ppermute | solution.py:35
  148.3 3.9 %collective-permute-start.6 = (bf16[256,768]{1,0:T(8,128)(2,1)S(1)}, bf16[256,768]{1,0:T(8,128)(2,1)S(1)}, u32[]{:S(2)}, u32[]{:S(2)}) collective-permute-start(bf16[256,768]{1,0:T(8,128)(2,1)S(1)} %slice.71), channel_id=1, source_target_pairs={{0,4},{1,5},{2,6},{3,7},{4,0},{5,1},{6,2},{7,3},{8,12},{9,13},{10,... | collective-permute-start | bytes 1179656 | tf_op jit(solution)/shard_map/ppermute | solution.py:35
  154.2 6.6 %all-to-all-start.2 = ((bf16[32,8,384]{2,1,0:T(8,128)(2,1)}), bf16[32,8,384]{2,1,0:T(8,128)(2,1)S(1)}, u32[]{:S(2)}, u32[]{:S(2)}) async-start(bf16[32,8,384]{2,1,0:T(8,128)(2,1)} %broadcast_in_dim.10), calls=%async_computation.2 | async-start | bytes 393216 | tf_op jit(solution)/shard_map/all_to_all | solution.py:191
  163.5 6.0 %collective-permute-start.7 = (bf16[256,384]{1,0:T(8,128)(2,1)S(1)}, bf16[256,384]{1,0:T(8,128)(2,1)S(1)}, u32[]{:S(2)}, u32[]{:S(2)}) collective-permute-start(bf16[256,384]{1,0:T(8,128)(2,1)S(1)} %slice.72), channel_id=1, source_target_pairs={{0,12},{1,13},{2,14},{3,15},{4,8},{5,9},{6,10},{7,11},{8,4},{9,5},... | collective-permute-start | bytes 589832 | tf_op jit(solution)/shard_map/ppermute | solution.py:35
  171.6 3.2 %collective-permute-done.7 = bf16[256,384]{1,0:T(8,128)(2,1)S(1)} collective-permute-done((bf16[256,384]{1,0:T(8,128)(2,1)S(1)}, bf16[256,384]{1,0:T(8,128)(2,1)S(1)}, u32[]{:S(2)}, u32[]{:S(2)}) %collective-permute-start.7) | collective-permute-done | bytes 196640 | tf_op jit(solution)/shard_map/ppermute | solution.py:35
  (47 shorter events, 16.3 us)
Async XLA Ops:
  7.2 57.2 %copy-start = (bf16[64,12288]{1,0:T(8,128)(2,1)S(1)}, bf16[64,12288]{1,0:T(8,128)(2,1)}, u32[]{:S(2)}) copy-start(bf16[64,12288]{1,0:T(8,128)(2,1)} %param.8) | copy-start | bytes 4718596
  7.2 22.3 %copy-start.4 = (bf16[256,384]{1,0:T(8,128)(2,1)S(1)}, bf16[256,384]{1,0:T(8,128)(2,1)}, u32[]{:S(2)}) copy-start(bf16[256,384]{1,0:T(8,128)(2,1)} %param.5) | copy-start | bytes 589828
  7.2 79.5 %all-gather.2.cloned.1.call-start = ((), (), s32[]{:S(2)}) async-start(), calls=%async_computation.3 | async-start | bytes 10027008 | tf_op jit(solution)/shard_map/all_gather | solution.py:215
  18.6 10.9 %collective-permute-start = (bf16[256,384]{1,0:T(8,128)(2,1)}, bf16[256,384]{1,0:T(8,128)(2,1)S(1)}, u32[]{:S(2)}, u32[]{:S(2)}) collective-permute-start(bf16[256,384]{1,0:T(8,128)(2,1)} %param.5), channel_id=1, source_target_pairs={{0,12},{1,13},{2,14},{3,15},{4,8},{5,9},{6,10},{7,11},{8,4},{9,5},... | collective-permute-start | bytes 589832 | tf_op jit(solution)/shard_map/ppermute | solution.py:35
  29.5 15.6 %collective-permute-start.1 = (bf16[256,768]{1,0:T(8,128)(2,1)S(1)}, bf16[256,768]{1,0:T(8,128)(2,1)S(1)}, u32[]{:S(2)}, u32[]{:S(2)}) collective-permute-start(bf16[256,768]{1,0:T(8,128)(2,1)S(1)} %pad_maximum_fusion.1), channel_id=1, source_target_pairs={{0,4},{1,5},{2,6},{3,7},{4,0},{5,1},{6,2},{7,3},{8,12},{9,13},{10,... | collective-permute-start | bytes 1179656 | tf_op jit(solution)/shard_map/ppermute | solution.py:35
  45.2 15.7 %collective-permute-start.2 = (bf16[256,1536]{1,0:T(8,128)(2,1)S(1)}, bf16[256,1536]{1,0:T(8,128)(2,1)S(1)}, u32[]{:S(2)}, u32[]{:S(2)}) collective-permute-start(bf16[256,1536]{1,0:T(8,128)(2,1)S(1)} %pad_maximum_fusion), channel_id=1, source_target_pairs={{0,3},{1,2},{2,1},{3,0},{4,7},{5,6},{6,5},{7,4},{8,11},{9,10},{10,... | collective-permute-start | bytes 2359304 | tf_op jit(solution)/shard_map/ppermute | solution.py:35
  60.9 4.1 %copy-start.1 = (bf16[256,3072]{1,0:T(8,128)(2,1)}, bf16[256,3072]{1,0:T(8,128)(2,1)S(1)}, u32[]{:S(2)}) copy-start(bf16[256,3072]{1,0:T(8,128)(2,1)S(1)} %constant_dynamic-update-slice_fusion.xa) | copy-start | bytes 4718596
  60.9 22.4 %collective-permute-start.3 = (bf16[256,3072]{1,0:T(8,128)(2,1)S(1)}, bf16[256,3072]{1,0:T(8,128)(2,1)}, u32[]{:S(2)}, u32[]{:S(2)}) collective-permute-start(bf16[256,3072]{1,0:T(8,128)(2,1)S(1)} %constant_dynamic-update-slice_fusion.xa), channel_id=1, source_target_pairs={{0,1},{1,0},{2,3},{3,2},{4,5},{5,4},{6,7},{7,6},{8,9},{9,8},{10,11... | collective-permute-start | bytes 4718600 | tf_op jit(solution)/shard_map/ppermute | solution.py:35
  100.6 26.9 %collective-permute-start.4 = (bf16[256,3072]{1,0:T(8,128)(2,1)}, bf16[256,3072]{1,0:T(8,128)(2,1)}, u32[]{:S(2)}, u32[]{:S(2)}) collective-permute-start(bf16[256,3072]{1,0:T(8,128)(2,1)} %get-tuple-element.13), channel_id=1, source_target_pairs={{0,1},{1,0},{2,3},{3,2},{4,5},{5,4},{6,7},{7,6},{8,9},{9,8},{10,11... | collective-permute-start | bytes 4718600 | tf_op jit(solution)/shard_map/ppermute | solution.py:35
  103.4 29.5 %all-to-all-start = ((bf16[16,64,256]{2,1,0:T(8,128)(2,1)}), bf16[16,64,256]{2,1,0:T(8,128)(2,1)}, u32[]{:S(2)}, u32[]{:S(2)}) async-start(bf16[16,64,256]{2,1,0:T(8,128)(2,1)} %bitcast.51), calls=%async_computation | async-start | bytes 1048576 | tf_op jit(solution)/shard_map/all_to_all | solution.py:191
  119.5 13.4 %copy-start.5 = (bf16[64,768]{1,0:T(8,128)(2,1)S(1)}, bf16[64,768]{1,0:T(8,128)(2,1)}, u32[]{:S(2)}) copy-start(bf16[64,768]{1,0:T(8,128)(2,1)} %get-tuple-element.16) | copy-start | bytes 294916
  119.5 26.0 %copy-start.2 = (bf16[256,3072]{1,0:T(8,128)(2,1)S(1)}, bf16[256,3072]{1,0:T(8,128)(2,1)}, u32[]{:S(2)}) copy-start(bf16[256,3072]{1,0:T(8,128)(2,1)} %kept_half.1) | copy-start | bytes 4718596
  130.1 15.4 %collective-permute-start.5 = (bf16[256,1536]{1,0:T(8,128)(2,1)}, bf16[256,1536]{1,0:T(8,128)(2,1)}, u32[]{:S(2)}, u32[]{:S(2)}) collective-permute-start(bf16[256,1536]{1,0:T(8,128)(2,1)} %add_convert_fusion), channel_id=1, source_target_pairs={{0,3},{1,2},{2,1},{3,0},{4,7},{5,6},{6,5},{7,4},{8,11},{9,10},{10,... | collective-permute-start | bytes 2359304 | tf_op jit(solution)/shard_map/ppermute | solution.py:35
  135.0 18.5 %all-to-all-start.1 = ((bf16[32,8,384]{2,1,0:T(8,128)(2,1)}), bf16[32,8,384]{2,1,0:T(8,128)(2,1)S(1)}, u32[]{:S(2)}, u32[]{:S(2)}) async-start(bf16[32,8,384]{2,1,0:T(8,128)(2,1)} %maximum_bitcast_fusion), calls=%async_computation.1 | async-start | bytes 393216 | tf_op jit(solution)/shard_map/all_to_all | solution.py:191
  147.1 1.2 copy-start.3
  148.3 14.0 %collective-permute-start.6 = (bf16[256,768]{1,0:T(8,128)(2,1)S(1)}, bf16[256,768]{1,0:T(8,128)(2,1)S(1)}, u32[]{:S(2)}, u32[]{:S(2)}) collective-permute-start(bf16[256,768]{1,0:T(8,128)(2,1)S(1)} %slice.71), channel_id=1, source_target_pairs={{0,4},{1,5},{2,6},{3,7},{4,0},{5,1},{6,2},{7,3},{8,12},{9,13},{10,... | collective-permute-start | bytes 1179656 | tf_op jit(solution)/shard_map/ppermute | solution.py:35
  154.2 17.4 %all-to-all-start.2 = ((bf16[32,8,384]{2,1,0:T(8,128)(2,1)}), bf16[32,8,384]{2,1,0:T(8,128)(2,1)S(1)}, u32[]{:S(2)}, u32[]{:S(2)}) async-start(bf16[32,8,384]{2,1,0:T(8,128)(2,1)} %broadcast_in_dim.10), calls=%async_computation.2 | async-start | bytes 393216 | tf_op jit(solution)/shard_map/all_to_all | solution.py:191
  163.5 11.3 %collective-permute-start.7 = (bf16[256,384]{1,0:T(8,128)(2,1)S(1)}, bf16[256,384]{1,0:T(8,128)(2,1)S(1)}, u32[]{:S(2)}, u32[]{:S(2)}) collective-permute-start(bf16[256,384]{1,0:T(8,128)(2,1)S(1)} %slice.72), channel_id=1, source_target_pairs={{0,12},{1,13},{2,14},{3,15},{4,8},{5,9},{6,10},{7,11},{8,4},{9,5},... | collective-permute-start | bytes 589832 | tf_op jit(solution)/shard_map/ppermute | solution.py:35
Sparse Core Ops, SparseCore 0:
  18.7 67.9 all-gather.1

commit v7 on v6

--- a/solution.py
+++ b/solution.py
@@ -86,14 +86,19 @@
     low_out[...] = lowrank_sum(table, xa, down_t, 0, jnp.zeros(low_out.shape, f32))
 
 
-def main_kernel(lies, table, xa, xb, w, low_near, down_t, up, act, slope_out, rank_out, up_out, away, held, acc, sems):
+def far_kernel(table, xb, down_t, low_near, up, low_out, term_out):
+    low_t = lowrank_sum(table, xb, down_t, 8, low_near[...])
+    low_out[...] = low_t.astype(bf16)
+    lowrank = low_t.T.astype(bf16)
+    term_out[...] = adapter_scale * jnp.dot(lowrank, up[...], preferred_element_type=f32)
+
+
+def main_kernel(lies, xa, xb, w, low_t, term, up, act, slope_out, rank_out, up_out, away, held, acc, sems):
     rank = up.shape[0]
     wide = w.shape[0] // 8
     start_blocks(lies, w, held, sems, 16)
 
-    low_t = lowrank_sum(table, xb, down_t, 8, low_near[...])
-    lowrank_t, lowrank = low_t.astype(bf16), low_t.T.astype(bf16)
-    acc[...] = adapter_scale * jnp.dot(lowrank, up[...], preferred_element_type=f32)
+    acc[...] = term[...]
     for k in range(8):
         await_blocks(lies, w, held, sems, 2 * k)
         x_ref = xa if k < 4 else xb
@@ -105,7 +110,7 @@
     part = (adapter_scale * contract(up[...], slope, 1, 1)).astype(bf16)
     for copy in range(YH * X):
         rank_out[copy * rank : (copy + 1) * rank] = part
-    up_out[...] = (adapter_scale * jnp.dot(lowrank_t, slope, preferred_element_type=f32)).astype(bf16)
+    up_out[...] = (adapter_scale * jnp.dot(low_t[...], slope, preferred_element_type=f32)).astype(bf16)
 
     for k in range(4):
         rows = held[(4 + k) * wide : (5 + k) * wide]
@@ -124,7 +129,7 @@
         out_shape=jax.ShapeDtypeStruct((rank, rows), f32),
         in_specs=[SMEM, VMEM, VMEM],
         out_specs=VMEM,
-        compiler_params=pltpu.CompilerParams(vmem_limit_bytes=56 * 2**20),
+        compiler_params=pltpu.CompilerParams(vmem_limit_bytes=8 * 2**20),
         cost_estimate=pl.CostEstimate(
             flops=2 * rows * rank * xa.shape[1], bytes_accessed=3 * 2**20, transcendentals=0
         ),
@@ -132,7 +137,22 @@
     )(table, xa, down_t)
 
 
-def forward(lies, table, xa, xb, w, low_near, down_t, up, act):
+def far_lowrank(table, xb, down_t, low_near, up):
+    rows, rank, hidden = xb.shape[0], up.shape[0], up.shape[1]
+    return pl.pallas_call(
+        far_kernel,
+        out_shape=(jax.ShapeDtypeStruct((rank, rows), bf16), jax.ShapeDtypeStruct((rows, hidden), f32)),
+        in_specs=[SMEM, VMEM, VMEM, VMEM, VMEM],
+        out_specs=(VMEM, VMEM),
+        compiler_params=pltpu.CompilerParams(vmem_limit_bytes=8 * 2**20),
+        cost_estimate=pl.CostEstimate(
+            flops=2 * rows * rank * (xb.shape[1] + hidden), bytes_accessed=4 * 2**20, transcendentals=0
+        ),
+        name="far_lowrank",
+    )(table, xb, down_t, low_near, up)
+
+
+def forward(lies, xa, xb, w, low_t, term, up, act):
     rows, rank, hidden = xa.shape[0], up.shape[0], w.shape[1]
     return pl.pallas_call(
         main_kernel,
@@ -142,7 +162,7 @@
             jax.ShapeDtypeStruct((rank, hidden), bf16),
             jax.ShapeDtypeStruct(xa.shape, bf16),
         ),
-        in_specs=[SMEM, SMEM, VMEM, VMEM, HBM, VMEM, VMEM, VMEM, VMEM],
+        in_specs=[SMEM, VMEM, VMEM, HBM, VMEM, VMEM, VMEM, VMEM],
         out_specs=(VMEM, VMEM, VMEM, VMEM),
         scratch_shapes=[
             pltpu.VMEM(w.shape, bf16),
@@ -154,7 +174,7 @@
             flops=3 * rows * w.shape[0] * hidden, bytes_accessed=14 * 2**20, transcendentals=0
         ),
         name="forward",
-    )(lies, table, xa, xb, w, low_near, down_t, up, act)
+    )(lies, xa, xb, w, low_t, term, up, act)
 
 
 def kept_kernel(lies, slope, w, out, held, sems):
@@ -175,7 +195,7 @@
         in_specs=[SMEM, VMEM, HBM],
         out_specs=VMEM,
         scratch_shapes=[pltpu.VMEM((half, hidden), bf16), pltpu.SemaphoreType.DMA((16,))],
-        compiler_params=pltpu.CompilerParams(vmem_limit_bytes=56 * 2**20),
+        compiler_params=pltpu.CompilerParams(vmem_limit_bytes=16 * 2**20),
         cost_estimate=pl.CostEstimate(
             flops=2 * rows * half * hidden, bytes_accessed=7 * 2**20, transcendentals=0
         ),
@@ -223,8 +243,9 @@
     low_near = near_lowrank(table, near, down_t)
 
     up_columns = lax.dynamic_slice_in_dim(adapter_up, model_index * hidden, hidden, 1)
+    low_t, low_term = far_lowrank(table, far, down_t, low_near, up_columns)
     slope_grad, rank_shares, up_local, away = forward(
-        lies, table, near, far, gathered, low_near, down_t, up_columns, act_grad
+        lies, near, far, gathered, low_t, low_term, up_columns, act_grad
     )
 
     over_x = x_second(away)
@@ -255,7 +276,8 @@
     over_last = y_first(to_y)
     down_rows = lax.dynamic_slice_in_dim(adapter_down, model_index * width, width, 0)
     own = own + contract(rank_grad, down_rows, 0, 1)
-    own, over_last, grads = lax.optimization_barrier((own, over_last, grads))
+    own, grads = lax.optimization_barrier((own, grads))
+    own, over_last = lax.optimization_barrier((own, over_last))
     normed_grad = (own + widen(over_last)).astype(bf16)
     up_grad = jnp.concatenate([grads[:rank], grads[rank : 2 * rank]], axis=1)
     down_grad = grads[2 * rank : 3 * rank].T

time: 186 us -> 195 us (1.048)
  local copies, waits for them, and re-layouts: 4.94 us -> 11.2 us
  waiting for transfers between devices: 66 us -> 71.6 us
  Pallas kernels: 22.8 us -> 18.8 us
  starting transfers between devices: 54.3 us -> 56.3 us
    all_to_all x3, waiting for transfers between devices: 2.29 us -> 12.9 us  [exchange(): return lax.all_to_all(value, axis, 0, 0, tiled=True)]
    unnamed x15 -> x27, local copies, waits for them, and re-layouts: 1.3 us -> 8.65 us
    all_to_all x3, starting transfers between devices: 24.2 us -> 29.7 us  [exchange(): return lax.all_to_all(value, axis, 0, 0, tiled=True)]
    ppermute x8, starting transfers between devices: 30.1 us -> 26.6 us  [send(): return lax.ppermute(value, ('fsdp', 'mp'), pairs)]
    all_gather x1, waiting for transfers between devices: 3.4 us -> 0.01 us  [body(): lax.all_gather(both, 'fsdp', axis=0, tiled=True, axis_index_groups=PLANES)]
    pallas_call x1, Pallas kernels: 13.9 us -> 11.1 us  [forward(): pl.pallas_call(main_kernel, out_shape=(jax.ShapeDtypeStruct((rows, hidden...]
    pallas_call x0 -> x1, Pallas kernels: none -> 2.48 us  [far_lowrank(): pl.pallas_call(far_kernel, out_shape=(jax.ShapeDtypeStruct((rank, rows),...]
  transfers between devices with their start and end apart: 12 -> 12, of which waited for: 11 -> 8; matrix products, arithmetic and copies ran while one was open for 6% -> 6% of each run, Pallas kernels for 5% -> 4%
where the time goes in v7:
time: 195 us; the launch traced here: 193 us
  waiting for transfers between devices  71.6 us (37%)
  starting transfers between devices  56.3 us (29%)
  Pallas kernels  18.8 us (10%)
  between operations  14.4 us (7%)
  blocking collectives  11.3 us (6%)
  local copies, waits for them, and re-layouts  11.2 us (6%)
  other arithmetic  8.55 us (4%)
    ppermute x8, waiting for transfers between devices, send(): return lax.ppermute(value, ('fsdp', 'mp'), pairs)  58.7 us
    all_to_all x3, starting transfers between devices, exchange(): return lax.all_to_all(value, axis, 0, 0, tiled=True)  29.7 us
    ppermute x8, starting transfers between devices, send(): return lax.ppermute(value, ('fsdp', 'mp'), pairs)  26.6 us
    all_to_all x3, waiting for transfers between devices, exchange(): return lax.all_to_all(value, axis, 0, 0, tiled=True)  12.9 us
    all_gather x1, blocking collectives, body(): lax.all_gather(up_weight, 'fsdp', axis=0, tiled=True, axis_index_groups=P...  11.3 us
    pallas_call x1, Pallas kernels, forward(): pl.pallas_call(main_kernel, out_shape=(jax.ShapeDtypeStruct((rows, hidden...  11.1 us
    unnamed x27, local copies, waits for them, and re-layouts  8.65 us
    pallas_call x1, Pallas kernels, kept_half(): pl.pallas_call(kept_kernel, out_shape=jax.ShapeDtypeStruct((rows, half),...  4.14 us
  transfers between devices with their start and end apart: 12, of which 8 were waited for; matrix products, arithmetic and copies ran while one was open for 6% of the time, Pallas kernels for 4%

profile of v7, /device:TPU:6, one launch (start us, length us, event | category | flops | bytes accessed | tf_op | source)
XLA Modules:
  0.0 193.5 jit_solution(11539931036792804919)
XLA Ops:
  7.2 11.3 %all_gather.6 = bf16[384,768]{1,0:T(8,128)(2,1)} all-gather(bf16[192,768]{1,0:T(8,128)(2,1)} %param.6), channel_id=1, replica_groups={{0,32},{16,48},{64,96},{80,112},{128,160},{144,176},{192,224},{208,240}..., dimensions={0}, use_global_device_ids=true | all-gather | bytes 884736 | tf_op jit(solution)/shard_map/all_gather | solution.py:234
  18.6 5.3 %collective-permute-start = (bf16[256,384]{1,0:T(8,128)(2,1)}, bf16[256,384]{1,0:T(8,128)(2,1)S(1)}, u32[]{:S(2)}, u32[]{:S(2)}) collective-permute-start(bf16[256,384]{1,0:T(8,128)(2,1)} %param.5), channel_id=1, source_target_pairs={{0,12},{1,13},{2,14},{3,15},{4,8},{5,9},{6,10},{7,11},{8,4},{9,5},... | collective-permute-start | bytes 589832 | tf_op jit(solution)/shard_map/ppermute | solution.py:35
  23.9 5.6 %collective-permute-done = bf16[256,384]{1,0:T(8,128)(2,1)S(1)} collective-permute-done((bf16[256,384]{1,0:T(8,128)(2,1)}, bf16[256,384]{1,0:T(8,128)(2,1)S(1)}, u32[]{:S(2)}, u32[]{:S(2)}) %collective-permute-start) | collective-permute-done | bytes 196640 | tf_op jit(solution)/shard_map/ppermute | solution.py:35
  29.5 5.6 %collective-permute-start.1 = (bf16[256,768]{1,0:T(8,128)(2,1)S(1)}, bf16[256,768]{1,0:T(8,128)(2,1)S(1)}, u32[]{:S(2)}, u32[]{:S(2)}) collective-permute-start(bf16[256,768]{1,0:T(8,128)(2,1)S(1)} %pad_maximum_fusion.1), channel_id=1, source_target_pairs={{0,4},{1,5},{2,6},{3,7},{4,0},{5,1},{6,2},{7,3},{8,12},{9,13},{10,... | collective-permute-start | bytes 1179656 | tf_op jit(solution)/shard_map/ppermute | solution.py:35
  35.1 10.0 %collective-permute-done.1 = bf16[256,768]{1,0:T(8,128)(2,1)S(1)} collective-permute-done((bf16[256,768]{1,0:T(8,128)(2,1)S(1)}, bf16[256,768]{1,0:T(8,128)(2,1)S(1)}, u32[]{:S(2)}, u32[]{:S(2)}) %collective-permute-start.1) | collective-permute-done | bytes 393248 | tf_op jit(solution)/shard_map/ppermute | solution.py:35
  45.1 1.9 collective-permute-start.2
  47.2 13.6 %collective-permute-done.2 = bf16[256,1536]{1,0:T(8,128)(2,1)S(1)} collective-permute-done((bf16[256,1536]{1,0:T(8,128)(2,1)S(1)}, bf16[256,1536]{1,0:T(8,128)(2,1)S(1)}, u32[]{:S(2)}, u32[]{:S(2)}) %collective-permute-start.2) | collective-permute-done | bytes 786464 | tf_op jit(solution)/shard_map/ppermute | solution.py:35
  60.9 1.9 collective-permute-start.3
  66.3 17.1 %collective-permute-done.3.xb = bf16[256,3072]{1,0:T(8,128)(2,1)} collective-permute-done((bf16[256,3072]{1,0:T(8,128)(2,1)S(1)}, bf16[256,3072]{1,0:T(8,128)(2,1)}, u32[]{:S(2)}, u32[]{:S(2)}) %collective-permute-start.3) | collective-permute-done | bytes 1572896 | tf_op jit(solution)/shard_map/ppermute | solution.py:35
  83.3 2.5 %far_lowrank.1 = (bf16[64,256]{1,0:T(8,128)(2,1)S(1)}, f32[256,768]{1,0:T(8,128)S(1)}) custom-call(s32[16]{0:T(128)S(1)} %stack.124.table, bf16[256,3072]{1,0:T(8,128)(2,1)} %collective-permute-done.3.xb, bf16[64,6144]{1,0:T(8,128)(2,1)S(1)} %bitcast.48, f32[64,256]{1,0:T(8,128)S(1)} %near_lowrank.1.low_near, bf16[64,768]{1,0:T(8,128)(2,1)S(1)} %constant_dynamic-slice_fusion.up), custom_call_target="tpu_custom_call" | custom-call | flops 125829120 | bytes 4194304 | tf_op jit(solution)/shard_map/far_lowrank/pallas_call | solution.py:142
  87.3 11.1 %forward.1 = (bf16[256,768]{1,0:T(8,128)(2,1)}, bf16[1024,256]{1,0:T(8,128)(2,1)}, bf16[64,768]{1,0:T(8,128)(2,1)}, bf16[256,3072]{1,0:T(8,128)(2,1)}) custom-call(s32[32]{0:T(128)} %reshape.687.lies, bf16[256,3072]{1,0:T(8,128)(2,1)} %copy-done.2, bf16[256,3072]{1,0:T(8,128)(2,1)} %collective-permute-done.3.xb, ...), custom_call_target="tpu_custom_call" | custom-call | flops 3623878656 | bytes 14680064 | tf_op jit(solution)/shard_map/forward/pallas_call | solution.py:157
  98.4 2.1 %collective-permute-start.4 = (bf16[256,3072]{1,0:T(8,128)(2,1)}, bf16[256,3072]{1,0:T(8,128)(2,1)}, u32[]{:S(2)}, u32[]{:S(2)}) collective-permute-start(bf16[256,3072]{1,0:T(8,128)(2,1)} %get-tuple-element.18), channel_id=1, source_target_pairs={{0,1},{1,0},{2,3},{3,2},{4,5},{5,4},{6,7},{7,6},{8,9},{9,8},{10,11... | collective-permute-start | bytes 4718600 | tf_op jit(solution)/shard_map/ppermute | solution.py:35
  100.6 10.1 %all-to-all-start = ((bf16[16,64,256]{2,1,0:T(8,128)(2,1)}), bf16[16,64,256]{2,1,0:T(8,128)(2,1)}, u32[]{:S(2)}, u32[]{:S(2)}) async-start(bf16[16,64,256]{2,1,0:T(8,128)(2,1)} %bitcast.51), calls=%async_computation | async-start | bytes 1048576 | tf_op jit(solution)/shard_map/all_to_all | solution.py:211
  110.6 3.7 %copy-done.1 = bf16[6144,768]{1,0:T(8,128)(2,1)S(1)} copy-done((bf16[6144,768]{1,0:T(8,128)(2,1)S(1)}, bf16[6144,768]{1,0:T(8,128)(2,1)}, u32[]{:S(2)}) %copy-start.1) | copy-done | bytes 9437208
  115.3 4.1 %kept_half.1 = bf16[256,3072]{1,0:T(8,128)(2,1)S(1)} custom-call(s32[32]{0:T(128)S(1)} %copy-done.8, bf16[256,768]{1,0:T(8,128)(2,1)S(1)} %copy-done.6, bf16[6144,768]{1,0:T(8,128)(2,1)S(1)} %copy-done.1), custom_call_target="tpu_custom_call" | custom-call | flops 1207959552 | bytes 7340032 | tf_op jit(solution)/shard_map/kept_half/pallas_call | solution.py:192
  119.5 6.1 %collective-permute-done.4 = bf16[256,3072]{1,0:T(8,128)(2,1)} collective-permute-done((bf16[256,3072]{1,0:T(8,128)(2,1)}, bf16[256,3072]{1,0:T(8,128)(2,1)}, u32[]{:S(2)}, u32[]{:S(2)}) %collective-permute-start.4) | collective-permute-done | bytes 1572896 | tf_op jit(solution)/shard_map/ppermute | solution.py:35
  125.6 2.3 %add_convert_fusion = bf16[256,1536]{1,0:T(8,128)(2,1)} fusion(bf16[256,3072]{1,0:T(8,128)(2,1)} %collective-permute-done.4, bf16[256,3072]{1,0:T(8,128)(2,1)S(1)} %kept_half.1), kind=kLoop, calls=%fused_computation.1 | loop fusion | flops 1572864 | bytes 2359296 | tf_op jit(solution)/shard_map/convert_element_type | solution.py:255
  132.0 11.5 %all-to-all-start.1 = ((bf16[32,8,384]{2,1,0:T(8,128)(2,1)}), bf16[32,8,384]{2,1,0:T(8,128)(2,1)S(1)}, u32[]{:S(2)}, u32[]{:S(2)}) async-start(bf16[32,8,384]{2,1,0:T(8,128)(2,1)} %maximum_bitcast_fusion), calls=%async_computation.1 | async-start | bytes 393216 | tf_op jit(solution)/shard_map/all_to_all | solution.py:211
  146.4 3.7 %collective-permute-start.6 = (bf16[256,768]{1,0:T(8,128)(2,1)S(1)}, bf16[256,768]{1,0:T(8,128)(2,1)S(1)}, u32[]{:S(2)}, u32[]{:S(2)}) collective-permute-start(bf16[256,768]{1,0:T(8,128)(2,1)S(1)} %slice.71), channel_id=1, source_target_pairs={{0,4},{1,5},{2,6},{3,7},{4,0},{5,1},{6,2},{7,3},{8,12},{9,13},{10,... | collective-permute-start | bytes 1179656 | tf_op jit(solution)/shard_map/ppermute | solution.py:35
  150.1 4.3 %all-to-all-done.1 = bf16[32,8,384]{2,1,0:T(8,128)(2,1)S(1)} async-done(((bf16[32,8,384]{2,1,0:T(8,128)(2,1)}), bf16[32,8,384]{2,1,0:T(8,128)(2,1)S(1)}, u32[]{:S(2)}, u32[]{:S(2)}) %all-to-all-start.1) | async-done | bytes 196640 | tf_op jit(solution)/shard_map/all_to_all | solution.py:211
  155.1 8.1 %all-to-all-start.2 = ((bf16[32,8,384]{2,1,0:T(8,128)(2,1)}), bf16[32,8,384]{2,1,0:T(8,128)(2,1)S(1)}, u32[]{:S(2)}, u32[]{:S(2)}) async-start(bf16[32,8,384]{2,1,0:T(8,128)(2,1)} %broadcast_in_dim.10), calls=%async_computation.2 | async-start | bytes 393216 | tf_op jit(solution)/shard_map/all_to_all | solution.py:211
  165.5 8.6 %all-to-all-done.2 = bf16[32,8,384]{2,1,0:T(8,128)(2,1)S(1)} async-done(((bf16[32,8,384]{2,1,0:T(8,128)(2,1)}), bf16[32,8,384]{2,1,0:T(8,128)(2,1)S(1)}, u32[]{:S(2)}, u32[]{:S(2)}) %all-to-all-start.2) | async-done | bytes 196640 | tf_op jit(solution)/shard_map/all_to_all | solution.py:211
  174.1 4.1 %collective-permute-start.7 = (bf16[256,384]{1,0:T(8,128)(2,1)S(1)}, bf16[256,384]{1,0:T(8,128)(2,1)S(1)}, u32[]{:S(2)}, u32[]{:S(2)}) collective-permute-start(bf16[256,384]{1,0:T(8,128)(2,1)S(1)} %slice.72), channel_id=1, source_target_pairs={{0,12},{1,13},{2,14},{3,15},{4,8},{5,9},{6,10},{7,11},{8,4},{9,5},... | collective-permute-start | bytes 589832 | tf_op jit(solution)/shard_map/ppermute | solution.py:35
  179.6 6.3 %collective-permute-done.7 = bf16[256,384]{1,0:T(8,128)(2,1)S(1)} collective-permute-done((bf16[256,384]{1,0:T(8,128)(2,1)S(1)}, bf16[256,384]{1,0:T(8,128)(2,1)S(1)}, u32[]{:S(2)}, u32[]{:S(2)}) %collective-permute-start.7) | collective-permute-done | bytes 196640 | tf_op jit(solution)/shard_map/ppermute | solution.py:35
  (60 shorter events, 18.1 us)
Async XLA Ops:
  7.2 56.7 %copy-start = (bf16[64,12288]{1,0:T(8,128)(2,1)S(1)}, bf16[64,12288]{1,0:T(8,128)(2,1)}, u32[]{:S(2)}) copy-start(bf16[64,12288]{1,0:T(8,128)(2,1)} %param.8) | copy-start | bytes 4718596
  7.2 22.3 %copy-start.10 = (bf16[256,384]{1,0:T(8,128)(2,1)S(1)}, bf16[256,384]{1,0:T(8,128)(2,1)}, u32[]{:S(2)}) copy-start(bf16[256,384]{1,0:T(8,128)(2,1)} %param.5) | copy-start | bytes 589828
  7.2 80.1 %all-gather.2.cloned.1.call-start = ((), (), s32[]{:S(2)}) async-start(), calls=%async_computation.3 | async-start | bytes 10027008 | tf_op jit(solution)/shard_map/all_gather | solution.py:235
  18.6 10.9 %collective-permute-start = (bf16[256,384]{1,0:T(8,128)(2,1)}, bf16[256,384]{1,0:T(8,128)(2,1)S(1)}, u32[]{:S(2)}, u32[]{:S(2)}) collective-permute-start(bf16[256,384]{1,0:T(8,128)(2,1)} %param.5), channel_id=1, source_target_pairs={{0,12},{1,13},{2,14},{3,15},{4,8},{5,9},{6,10},{7,11},{8,4},{9,5},... | collective-permute-start | bytes 589832 | tf_op jit(solution)/shard_map/ppermute | solution.py:35
  29.5 15.6 %collective-permute-start.1 = (bf16[256,768]{1,0:T(8,128)(2,1)S(1)}, bf16[256,768]{1,0:T(8,128)(2,1)S(1)}, u32[]{:S(2)}, u32[]{:S(2)}) collective-permute-start(bf16[256,768]{1,0:T(8,128)(2,1)S(1)} %pad_maximum_fusion.1), channel_id=1, source_target_pairs={{0,4},{1,5},{2,6},{3,7},{4,0},{5,1},{6,2},{7,3},{8,12},{9,13},{10,... | collective-permute-start | bytes 1179656 | tf_op jit(solution)/shard_map/ppermute | solution.py:35
  45.1 15.7 %collective-permute-start.2 = (bf16[256,1536]{1,0:T(8,128)(2,1)S(1)}, bf16[256,1536]{1,0:T(8,128)(2,1)S(1)}, u32[]{:S(2)}, u32[]{:S(2)}) collective-permute-start(bf16[256,1536]{1,0:T(8,128)(2,1)S(1)} %pad_maximum_fusion), channel_id=1, source_target_pairs={{0,3},{1,2},{2,1},{3,0},{4,7},{5,6},{6,5},{7,4},{8,11},{9,10},{10,... | collective-permute-start | bytes 2359304 | tf_op jit(solution)/shard_map/ppermute | solution.py:35
  60.9 24.9 %copy-start.2 = (bf16[256,3072]{1,0:T(8,128)(2,1)}, bf16[256,3072]{1,0:T(8,128)(2,1)S(1)}, u32[]{:S(2)}) copy-start(bf16[256,3072]{1,0:T(8,128)(2,1)S(1)} %constant_dynamic-update-slice_fusion.xa) | copy-start | bytes 4718596
  60.9 22.4 %collective-permute-start.3 = (bf16[256,3072]{1,0:T(8,128)(2,1)S(1)}, bf16[256,3072]{1,0:T(8,128)(2,1)}, u32[]{:S(2)}, u32[]{:S(2)}) collective-permute-start(bf16[256,3072]{1,0:T(8,128)(2,1)S(1)} %constant_dynamic-update-slice_fusion.xa), channel_id=1, source_target_pairs={{0,1},{1,0},{2,3},{3,2},{4,5},{5,4},{6,7},{7,6},{8,9},{9,8},{10,11... | collective-permute-start | bytes 4718600 | tf_op jit(solution)/shard_map/ppermute | solution.py:35
  63.9 21.9 %copy-start.4 = (bf16[64,768]{1,0:T(8,128)(2,1)}, bf16[64,768]{1,0:T(8,128)(2,1)S(1)}, u32[]{:S(2)}) copy-start(bf16[64,768]{1,0:T(8,128)(2,1)S(1)} %constant_dynamic-slice_fusion.up) | copy-start | bytes 294916
  63.9 1.2 copy-start.3
  85.8 0.9 copy-start.5
  86.7 0.6 copy-start.7
  87.3 23.3 %copy-start.8 = (s32[32]{0:T(128)S(1)}, s32[32]{0:T(128)}, u32[]{:S(2)}) copy-start(s32[32]{0:T(128)} %reshape.687.lies) | copy-start | bytes 388
  98.4 27.2 %collective-permute-start.4 = (bf16[256,3072]{1,0:T(8,128)(2,1)}, bf16[256,3072]{1,0:T(8,128)(2,1)}, u32[]{:S(2)}, u32[]{:S(2)}) collective-permute-start(bf16[256,3072]{1,0:T(8,128)(2,1)} %get-tuple-element.18), channel_id=1, source_target_pairs={{0,1},{1,0},{2,3},{3,2},{4,5},{5,4},{6,7},{7,6},{8,9},{9,8},{10,11... | collective-permute-start | bytes 4718600 | tf_op jit(solution)/shard_map/ppermute | solution.py:35
  100.6 29.3 %all-to-all-start = ((bf16[16,64,256]{2,1,0:T(8,128)(2,1)}), bf16[16,64,256]{2,1,0:T(8,128)(2,1)}, u32[]{:S(2)}, u32[]{:S(2)}) async-start(bf16[16,64,256]{2,1,0:T(8,128)(2,1)} %bitcast.51), calls=%async_computation | async-start | bytes 1048576 | tf_op jit(solution)/shard_map/all_to_all | solution.py:211
  110.6 3.7 %copy-start.1 = (bf16[6144,768]{1,0:T(8,128)(2,1)S(1)}, bf16[6144,768]{1,0:T(8,128)(2,1)}, u32[]{:S(2)}) copy-start(bf16[6144,768]{1,0:T(8,128)(2,1)} %all-gather.2.cloned.1.call-done.w) | copy-start | bytes 28311556
  114.3 1.0 copy-start.6
  119.4 10.4 %copy-start.11 = (bf16[64,768]{1,0:T(8,128)(2,1)S(1)}, bf16[64,768]{1,0:T(8,128)(2,1)}, u32[]{:S(2)}) copy-start(bf16[64,768]{1,0:T(8,128)(2,1)} %get-tuple-element.21) | copy-start | bytes 294916
  127.9 15.6 %collective-permute-start.5 = (bf16[256,1536]{1,0:T(8,128)(2,1)}, bf16[256,1536]{1,0:T(8,128)(2,1)}, u32[]{:S(2)}, u32[]{:S(2)}) collective-permute-start(bf16[256,1536]{1,0:T(8,128)(2,1)} %add_convert_fusion), channel_id=1, source_target_pairs={{0,3},{1,2},{2,1},{3,0},{4,7},{5,6},{6,5},{7,4},{8,11},{9,10},{10,... | collective-permute-start | bytes 2359304 | tf_op jit(solution)/shard_map/ppermute | solution.py:35
  132.0 22.4 %all-to-all-start.1 = ((bf16[32,8,384]{2,1,0:T(8,128)(2,1)}), bf16[32,8,384]{2,1,0:T(8,128)(2,1)S(1)}, u32[]{:S(2)}, u32[]{:S(2)}) async-start(bf16[32,8,384]{2,1,0:T(8,128)(2,1)} %maximum_bitcast_fusion), calls=%async_computation.1 | async-start | bytes 393216 | tf_op jit(solution)/shard_map/all_to_all | solution.py:211
  145.2 1.2 copy-start.9
  146.4 16.8 %collective-permute-start.6 = (bf16[256,768]{1,0:T(8,128)(2,1)S(1)}, bf16[256,768]{1,0:T(8,128)(2,1)S(1)}, u32[]{:S(2)}, u32[]{:S(2)}) collective-permute-start(bf16[256,768]{1,0:T(8,128)(2,1)S(1)} %slice.71), channel_id=1, source_target_pairs={{0,4},{1,5},{2,6},{3,7},{4,0},{5,1},{6,2},{7,3},{8,12},{9,13},{10,... | collective-permute-start | bytes 1179656 | tf_op jit(solution)/shard_map/ppermute | solution.py:35
  155.1 19.0 %all-to-all-start.2 = ((bf16[32,8,384]{2,1,0:T(8,128)(2,1)}), bf16[32,8,384]{2,1,0:T(8,128)(2,1)S(1)}, u32[]{:S(2)}, u32[]{:S(2)}) async-start(bf16[32,8,384]{2,1,0:T(8,128)(2,1)} %broadcast_in_dim.10), calls=%async_computation.2 | async-start | bytes 393216 | tf_op jit(solution)/shard_map/all_to_all | solution.py:211
  174.1 11.8 %collective-permute-start.7 = (bf16[256,384]{1,0:T(8,128)(2,1)S(1)}, bf16[256,384]{1,0:T(8,128)(2,1)S(1)}, u32[]{:S(2)}, u32[]{:S(2)}) collective-permute-start(bf16[256,384]{1,0:T(8,128)(2,1)S(1)} %slice.72), channel_id=1, source_target_pairs={{0,12},{1,13},{2,14},{3,15},{4,8},{5,9},{6,10},{7,11},{8,4},{9,5},... | collective-permute-start | bytes 589832 | tf_op jit(solution)/shard_map/ppermute | solution.py:35
Sparse Core Ops, SparseCore 0:
  18.7 67.9 all-gather.1

commit v8 on v7

--- a/solution.py
+++ b/solution.py
@@ -216,6 +216,10 @@
     return exchange(copies.reshape(-1, value.shape[1]), axis)
 
 
+def total(parts, start, stop):
+    return sum(widen(part[:, start:stop]) for part in parts)
+
+
 def add_parts(parts, count):
     return jnp.sum(widen(parts).reshape(count, -1, parts.shape[1]), axis=0).astype(bf16)
 
@@ -251,8 +255,7 @@
     over_x = x_second(away)
     rank_parts = exchange(rank_shares, "mp")
     kept = kept_half(lies, slope_grad, gathered)
-    half = 4 * width
-    to_next = (widen(kept[:, half:]) + widen(over_x[:, half:])).astype(bf16)
+    to_next = total([kept, over_x], 4 * width, 8 * width).astype(bf16)
     over_next = x_first(to_next)
 
     rank_parts, _ = lax.optimization_barrier((rank_parts, to_next))
@@ -264,20 +267,17 @@
     )
     shares = exchange(shares, "fsdp")
 
-    own = widen(kept[:, :half]) + widen(over_x[:, :half]) + widen(over_next)
-    own, to_y = own[:, : 2 * width], own[:, 2 * width :].astype(bf16)
+    to_y = total([kept, over_x, over_next], 2 * width, 4 * width).astype(bf16)
     over_y = y_second(to_y)
     shares, _ = lax.optimization_barrier((shares, to_y))
     members = Z * YL * C
     grads = gather_small(add_parts(shares, members), "fsdp", members)
 
-    own = own + widen(over_y)
-    own, to_y = own[:, :width], own[:, width:].astype(bf16)
-    over_last = y_first(to_y)
+    to_last = total([kept, over_x, over_next, over_y], width, 2 * width).astype(bf16)
+    over_last = y_first(to_last)
     down_rows = lax.dynamic_slice_in_dim(adapter_down, model_index * width, width, 0)
-    own = own + contract(rank_grad, down_rows, 0, 1)
-    own, grads = lax.optimization_barrier((own, grads))
-    own, over_last = lax.optimization_barrier((own, over_last))
+    own = total([kept, over_x, over_next, over_y], 0, width) + contract(rank_grad, down_rows, 0, 1)
+    own, over_last, grads = lax.optimization_barrier((own, over_last, grads))
     normed_grad = (own + widen(over_last)).astype(bf16)
     up_grad = jnp.concatenate([grads[:rank], grads[rank : 2 * rank]], axis=1)
     down_grad = grads[2 * rank : 3 * rank].T

time: 195 us -> 189 us (0.969)
  waiting for transfers between devices: 71.6 us -> 61.8 us
    all_to_all x3, waiting for transfers between devices: 12.9 us -> 6.27 us  [exchange(): return lax.all_to_all(value, axis, 0, 0, tiled=True)]
    convert_element_type x1 -> x3, other arithmetic: 2.27 us -> 6.19 us  [the longest x1 2.29 us: body(): to_next = total([kept, over_x], 4 * width, 8 * width).astype(bf16)]
    ppermute x8, waiting for transfers between devices: 58.7 us -> 55.5 us  [send(): return lax.ppermute(value, ('fsdp', 'mp'), pairs)]
    add x2 -> x0, other arithmetic: 2.85 us -> none  [the longest x1 1.65 us: body(): own = widen(kept[:, :half]) + widen(over_x[:, :half]) + widen(over_next)]
    ppermute x8, starting transfers between devices: 26.6 us -> 28.9 us  [send(): return lax.ppermute(value, ('fsdp', 'mp'), pairs)]
    unnamed x27 -> x29, local copies, waits for them, and re-layouts: 8.65 us -> 7.49 us
where the time goes in v8:
time: 189 us; the launch traced here: 187 us
  waiting for transfers between devices  61.8 us (33%)
  starting transfers between devices  57.8 us (31%)
  Pallas kernels  18.8 us (10%)
  between operations  14.4 us (8%)
  blocking collectives  11.3 us (6%)
  local copies, waits for them, and re-layouts  10.8 us (6%)
  other arithmetic  10.5 us (6%)
    ppermute x8, waiting for transfers between devices, send(): return lax.ppermute(value, ('fsdp', 'mp'), pairs)  55.5 us
    ppermute x8, starting transfers between devices, send(): return lax.ppermute(value, ('fsdp', 'mp'), pairs)  28.9 us
    all_to_all x3, starting transfers between devices, exchange(): return lax.all_to_all(value, axis, 0, 0, tiled=True)  28.9 us
    all_gather x1, blocking collectives, body(): lax.all_gather(up_weight, 'fsdp', axis=0, tiled=True, axis_index_groups=P...  11.3 us
    pallas_call x1, Pallas kernels, forward(): pl.pallas_call(main_kernel, out_shape=(jax.ShapeDtypeStruct((rows, hidden...  11.1 us
    unnamed x29, local copies, waits for them, and re-layouts  7.49 us
    all_to_all x3, waiting for transfers between devices, exchange(): return lax.all_to_all(value, axis, 0, 0, tiled=True)  6.27 us
    pallas_call x1, Pallas kernels, kept_half(): pl.pallas_call(kept_kernel, out_shape=jax.ShapeDtypeStruct((rows, half),...  4.14 us
  transfers between devices with their start and end apart: 12, of which 8 were waited for; matrix products, arithmetic and copies ran while one was open for 6% of the time, Pallas kernels for 4%

profile of v8, /device:TPU:6, one launch (start us, length us, event | category | flops | bytes accessed | tf_op | source)
XLA Modules:
  0.0 187.0 jit_solution(11518342393279847945)
XLA Ops:
  7.2 11.3 %all_gather.6 = bf16[384,768]{1,0:T(8,128)(2,1)} all-gather(bf16[192,768]{1,0:T(8,128)(2,1)} %param.6), channel_id=1, replica_groups={{0,32},{16,48},{64,96},{80,112},{128,160},{144,176},{192,224},{208,240}..., dimensions={0}, use_global_device_ids=true | all-gather | bytes 884736 | tf_op jit(solution)/shard_map/all_gather | solution.py:238
  18.6 5.3 %collective-permute-start = (bf16[256,384]{1,0:T(8,128)(2,1)}, bf16[256,384]{1,0:T(8,128)(2,1)S(1)}, u32[]{:S(2)}, u32[]{:S(2)}) collective-permute-start(bf16[256,384]{1,0:T(8,128)(2,1)} %param.5), channel_id=1, source_target_pairs={{0,12},{1,13},{2,14},{3,15},{4,8},{5,9},{6,10},{7,11},{8,4},{9,5},... | collective-permute-start | bytes 589832 | tf_op jit(solution)/shard_map/ppermute | solution.py:35
  23.9 5.6 %collective-permute-done = bf16[256,384]{1,0:T(8,128)(2,1)S(1)} collective-permute-done((bf16[256,384]{1,0:T(8,128)(2,1)}, bf16[256,384]{1,0:T(8,128)(2,1)S(1)}, u32[]{:S(2)}, u32[]{:S(2)}) %collective-permute-start) | collective-permute-done | bytes 196640 | tf_op jit(solution)/shard_map/ppermute | solution.py:35
  29.5 5.6 %collective-permute-start.1 = (bf16[256,768]{1,0:T(8,128)(2,1)S(1)}, bf16[256,768]{1,0:T(8,128)(2,1)S(1)}, u32[]{:S(2)}, u32[]{:S(2)}) collective-permute-start(bf16[256,768]{1,0:T(8,128)(2,1)S(1)} %pad_maximum_fusion.1), channel_id=1, source_target_pairs={{0,4},{1,5},{2,6},{3,7},{4,0},{5,1},{6,2},{7,3},{8,12},{9,13},{10,... | collective-permute-start | bytes 1179656 | tf_op jit(solution)/shard_map/ppermute | solution.py:35
  35.1 10.0 %collective-permute-done.1 = bf16[256,768]{1,0:T(8,128)(2,1)S(1)} collective-permute-done((bf16[256,768]{1,0:T(8,128)(2,1)S(1)}, bf16[256,768]{1,0:T(8,128)(2,1)S(1)}, u32[]{:S(2)}, u32[]{:S(2)}) %collective-permute-start.1) | collective-permute-done | bytes 393248 | tf_op jit(solution)/shard_map/ppermute | solution.py:35
  45.1 1.9 %collective-permute-start.2 = (bf16[256,1536]{1,0:T(8,128)(2,1)S(1)}, bf16[256,1536]{1,0:T(8,128)(2,1)S(1)}, u32[]{:S(2)}, u32[]{:S(2)}) collective-permute-start(bf16[256,1536]{1,0:T(8,128)(2,1)S(1)} %pad_maximum_fusion), channel_id=1, source_target_pairs={{0,3},{1,2},{2,1},{3,0},{4,7},{5,6},{6,5},{7,4},{8,11},{9,10},{10,... | collective-permute-start | bytes 2359304 | tf_op jit(solution)/shard_map/ppermute | solution.py:35
  47.2 13.6 %collective-permute-done.2 = bf16[256,1536]{1,0:T(8,128)(2,1)S(1)} collective-permute-done((bf16[256,1536]{1,0:T(8,128)(2,1)S(1)}, bf16[256,1536]{1,0:T(8,128)(2,1)S(1)}, u32[]{:S(2)}, u32[]{:S(2)}) %collective-permute-start.2) | collective-permute-done | bytes 786464 | tf_op jit(solution)/shard_map/ppermute | solution.py:35
  60.9 1.9 %collective-permute-start.3 = (bf16[256,3072]{1,0:T(8,128)(2,1)S(1)}, bf16[256,3072]{1,0:T(8,128)(2,1)}, u32[]{:S(2)}, u32[]{:S(2)}) collective-permute-start(bf16[256,3072]{1,0:T(8,128)(2,1)S(1)} %constant_dynamic-update-slice_fusion.xa), channel_id=1, source_target_pairs={{0,1},{1,0},{2,3},{3,2},{4,5},{5,4},{6,7},{7,6},{8,9},{9,8},{10,11... | collective-permute-start | bytes 4718600 | tf_op jit(solution)/shard_map/ppermute | solution.py:35
  66.2 17.1 %collective-permute-done.3.xb = bf16[256,3072]{1,0:T(8,128)(2,1)} collective-permute-done((bf16[256,3072]{1,0:T(8,128)(2,1)S(1)}, bf16[256,3072]{1,0:T(8,128)(2,1)}, u32[]{:S(2)}, u32[]{:S(2)}) %collective-permute-start.3) | collective-permute-done | bytes 1572896 | tf_op jit(solution)/shard_map/ppermute | solution.py:35
  83.3 2.5 %far_lowrank.1 = (bf16[64,256]{1,0:T(8,128)(2,1)S(1)}, f32[256,768]{1,0:T(8,128)S(1)}) custom-call(s32[16]{0:T(128)S(1)} %stack.124.table, bf16[256,3072]{1,0:T(8,128)(2,1)} %collective-permute-done.3.xb, bf16[64,6144]{1,0:T(8,128)(2,1)S(1)} %bitcast.48, f32[64,256]{1,0:T(8,128)S(1)} %near_lowrank.1.low_near, bf16[64,768]{1,0:T(8,128)(2,1)S(1)} %constant_dynamic-slice_fusion.up), custom_call_target="tpu_custom_call" | custom-call | flops 125829120 | bytes 4194304 | tf_op jit(solution)/shard_map/far_lowrank/pallas_call | solution.py:142
  87.3 11.1 %forward.1 = (bf16[256,768]{1,0:T(8,128)(2,1)}, bf16[1024,256]{1,0:T(8,128)(2,1)}, bf16[64,768]{1,0:T(8,128)(2,1)}, bf16[256,3072]{1,0:T(8,128)(2,1)}) custom-call(s32[32]{0:T(128)} %reshape.687.lies, bf16[256,3072]{1,0:T(8,128)(2,1)} %copy-done.2, bf16[256,3072]{1,0:T(8,128)(2,1)} %collective-permute-done.3.xb, ...), custom_call_target="tpu_custom_call" | custom-call | flops 3623878656 | bytes 14680064 | tf_op jit(solution)/shard_map/forward/pallas_call | solution.py:157
  98.4 2.2 %collective-permute-start.4 = (bf16[256,3072]{1,0:T(8,128)(2,1)}, bf16[256,3072]{1,0:T(8,128)(2,1)}, u32[]{:S(2)}, u32[]{:S(2)}) collective-permute-start(bf16[256,3072]{1,0:T(8,128)(2,1)} %get-tuple-element.17), channel_id=1, source_target_pairs={{0,1},{1,0},{2,3},{3,2},{4,5},{5,4},{6,7},{7,6},{8,9},{9,8},{10,11... | collective-permute-start | bytes 4718600 | tf_op jit(solution)/shard_map/ppermute | solution.py:35
  100.6 10.0 %all-to-all-start = ((bf16[16,64,256]{2,1,0:T(8,128)(2,1)}), bf16[16,64,256]{2,1,0:T(8,128)(2,1)}, u32[]{:S(2)}, u32[]{:S(2)}) async-start(bf16[16,64,256]{2,1,0:T(8,128)(2,1)} %bitcast.50), calls=%async_computation | async-start | bytes 1048576 | tf_op jit(solution)/shard_map/all_to_all | solution.py:211
  110.6 3.7 %copy-done.1 = bf16[6144,768]{1,0:T(8,128)(2,1)S(1)} copy-done((bf16[6144,768]{1,0:T(8,128)(2,1)S(1)}, bf16[6144,768]{1,0:T(8,128)(2,1)}, u32[]{:S(2)}) %copy-start.1) | copy-done | bytes 9437208
  115.3 4.1 %kept_half.1 = bf16[256,3072]{1,0:T(8,128)(2,1)S(1)} custom-call(s32[32]{0:T(128)S(1)} %copy-done.9, bf16[256,768]{1,0:T(8,128)(2,1)S(1)} %copy-done.7, bf16[6144,768]{1,0:T(8,128)(2,1)S(1)} %copy-done.1), custom_call_target="tpu_custom_call" | custom-call | flops 1207959552 | bytes 7340032 | tf_op jit(solution)/shard_map/kept_half/pallas_call | solution.py:192
  119.4 6.1 %collective-permute-done.4 = bf16[256,3072]{1,0:T(8,128)(2,1)} collective-permute-done((bf16[256,3072]{1,0:T(8,128)(2,1)}, bf16[256,3072]{1,0:T(8,128)(2,1)}, u32[]{:S(2)}, u32[]{:S(2)}) %collective-permute-start.4) | collective-permute-done | bytes 1572896 | tf_op jit(solution)/shard_map/ppermute | solution.py:35
  125.6 2.3 %add_convert_fusion = bf16[256,1536]{1,0:T(8,128)(2,1)} fusion(bf16[256,3072]{1,0:T(8,128)(2,1)} %collective-permute-done.4, bf16[256,3072]{1,0:T(8,128)(2,1)S(1)} %kept_half.1), kind=kLoop, calls=%fused_computation | loop fusion | flops 1572864 | bytes 2359296 | tf_op jit(solution)/shard_map/convert_element_type | solution.py:258
  132.0 11.5 %all-to-all-start.1 = ((bf16[32,8,384]{2,1,0:T(8,128)(2,1)}), bf16[32,8,384]{2,1,0:T(8,128)(2,1)S(1)}, u32[]{:S(2)}, u32[]{:S(2)}) async-start(bf16[32,8,384]{2,1,0:T(8,128)(2,1)} %maximum_bitcast_fusion), calls=%async_computation.1 | async-start | bytes 393216 | tf_op jit(solution)/shard_map/all_to_all | solution.py:211
  143.6 2.0 %add_convert_fusion.1 = bf16[256,768]{1,0:T(8,128)(2,1)} fusion(bf16[256,1536]{1,0:T(8,128)(2,1)} %collective-permute-done.5, bf16[256,3072]{1,0:T(8,128)(2,1)} %collective-permute-done.4, bf16[256,3072]{1,0:T(8,128)(2,1)S(1)} %kept_half.1), kind=kLoop, calls=%fused_computation.3 | loop fusion | flops 1179648 | bytes 1572864 | tf_op jit(solution)/shard_map/convert_element_type | solution.py:270
  145.6 3.7 %collective-permute-start.6 = (bf16[256,768]{1,0:T(8,128)(2,1)}, bf16[256,768]{1,0:T(8,128)(2,1)}, u32[]{:S(2)}, u32[]{:S(2)}) collective-permute-start(bf16[256,768]{1,0:T(8,128)(2,1)} %add_convert_fusion.1), channel_id=1, source_target_pairs={{0,4},{1,5},{2,6},{3,7},{4,0},{5,1},{6,2},{7,3},{8,12},{9,13},{10,... | collective-permute-start | bytes 1179656 | tf_op jit(solution)/shard_map/ppermute | solution.py:35
  149.3 5.2 %all-to-all-done.1 = bf16[32,8,384]{2,1,0:T(8,128)(2,1)S(1)} async-done(((bf16[32,8,384]{2,1,0:T(8,128)(2,1)}), bf16[32,8,384]{2,1,0:T(8,128)(2,1)S(1)}, u32[]{:S(2)}, u32[]{:S(2)}) %all-to-all-start.1) | async-done | bytes 196640 | tf_op jit(solution)/shard_map/all_to_all | solution.py:211
  155.2 7.3 %all-to-all-start.2 = ((bf16[32,8,384]{2,1,0:T(8,128)(2,1)}), bf16[32,8,384]{2,1,0:T(8,128)(2,1)}, u32[]{:S(2)}, u32[]{:S(2)}) async-start(bf16[32,8,384]{2,1,0:T(8,128)(2,1)} %broadcast_in_dim.10), calls=%async_computation.2 | async-start | bytes 393216 | tf_op jit(solution)/shard_map/all_to_all | solution.py:211
  164.4 6.5 %collective-permute-start.7 = (bf16[256,384]{1,0:T(8,128)(2,1)}, bf16[256,384]{1,0:T(8,128)(2,1)}, u32[]{:S(2)}, u32[]{:S(2)}) collective-permute-start(bf16[256,384]{1,0:T(8,128)(2,1)} %add_convert_fusion.3), channel_id=1, source_target_pairs={{0,12},{1,13},{2,14},{3,15},{4,8},{5,9},{6,10},{7,11},{8,4},{9,5},... | collective-permute-start | bytes 589832 | tf_op jit(solution)/shard_map/ppermute | solution.py:35
  173.4 3.1 %collective-permute-done.7 = bf16[256,384]{1,0:T(8,128)(2,1)} collective-permute-done((bf16[256,384]{1,0:T(8,128)(2,1)}, bf16[256,384]{1,0:T(8,128)(2,1)}, u32[]{:S(2)}, u32[]{:S(2)}) %collective-permute-start.7) | collective-permute-done | bytes 196640 | tf_op jit(solution)/shard_map/ppermute | solution.py:35
  (60 shorter events, 19.1 us)
Async XLA Ops:
  7.2 56.7 %copy-start = (bf16[64,12288]{1,0:T(8,128)(2,1)S(1)}, bf16[64,12288]{1,0:T(8,128)(2,1)}, u32[]{:S(2)}) copy-start(bf16[64,12288]{1,0:T(8,128)(2,1)} %param.8) | copy-start | bytes 4718596
  7.2 22.3 %copy-start.10 = (bf16[256,384]{1,0:T(8,128)(2,1)S(1)}, bf16[256,384]{1,0:T(8,128)(2,1)}, u32[]{:S(2)}) copy-start(bf16[256,384]{1,0:T(8,128)(2,1)} %param.5) | copy-start | bytes 589828
  7.2 80.1 %all-gather.2.cloned.1.call-start = ((), (), s32[]{:S(2)}) async-start(), calls=%async_computation.3 | async-start | bytes 10027008 | tf_op jit(solution)/shard_map/all_gather | solution.py:239
  18.6 10.9 %collective-permute-start = (bf16[256,384]{1,0:T(8,128)(2,1)}, bf16[256,384]{1,0:T(8,128)(2,1)S(1)}, u32[]{:S(2)}, u32[]{:S(2)}) collective-permute-start(bf16[256,384]{1,0:T(8,128)(2,1)} %param.5), channel_id=1, source_target_pairs={{0,12},{1,13},{2,14},{3,15},{4,8},{5,9},{6,10},{7,11},{8,4},{9,5},... | collective-permute-start | bytes 589832 | tf_op jit(solution)/shard_map/ppermute | solution.py:35
  29.5 15.6 %collective-permute-start.1 = (bf16[256,768]{1,0:T(8,128)(2,1)S(1)}, bf16[256,768]{1,0:T(8,128)(2,1)S(1)}, u32[]{:S(2)}, u32[]{:S(2)}) collective-permute-start(bf16[256,768]{1,0:T(8,128)(2,1)S(1)} %pad_maximum_fusion.1), channel_id=1, source_target_pairs={{0,4},{1,5},{2,6},{3,7},{4,0},{5,1},{6,2},{7,3},{8,12},{9,13},{10,... | collective-permute-start | bytes 1179656 | tf_op jit(solution)/shard_map/ppermute | solution.py:35
  45.1 15.7 %collective-permute-start.2 = (bf16[256,1536]{1,0:T(8,128)(2,1)S(1)}, bf16[256,1536]{1,0:T(8,128)(2,1)S(1)}, u32[]{:S(2)}, u32[]{:S(2)}) collective-permute-start(bf16[256,1536]{1,0:T(8,128)(2,1)S(1)} %pad_maximum_fusion), channel_id=1, source_target_pairs={{0,3},{1,2},{2,1},{3,0},{4,7},{5,6},{6,5},{7,4},{8,11},{9,10},{10,... | collective-permute-start | bytes 2359304 | tf_op jit(solution)/shard_map/ppermute | solution.py:35
  60.9 24.9 %copy-start.2 = (bf16[256,3072]{1,0:T(8,128)(2,1)}, bf16[256,3072]{1,0:T(8,128)(2,1)S(1)}, u32[]{:S(2)}) copy-start(bf16[256,3072]{1,0:T(8,128)(2,1)S(1)} %constant_dynamic-update-slice_fusion.xa) | copy-start | bytes 4718596
  60.9 22.4 %collective-permute-start.3 = (bf16[256,3072]{1,0:T(8,128)(2,1)S(1)}, bf16[256,3072]{1,0:T(8,128)(2,1)}, u32[]{:S(2)}, u32[]{:S(2)}) collective-permute-start(bf16[256,3072]{1,0:T(8,128)(2,1)S(1)} %constant_dynamic-update-slice_fusion.xa), channel_id=1, source_target_pairs={{0,1},{1,0},{2,3},{3,2},{4,5},{5,4},{6,7},{7,6},{8,9},{9,8},{10,11... | collective-permute-start | bytes 4718600 | tf_op jit(solution)/shard_map/ppermute | solution.py:35
  63.9 22.0 %copy-start.5 = (bf16[64,768]{1,0:T(8,128)(2,1)}, bf16[64,768]{1,0:T(8,128)(2,1)S(1)}, u32[]{:S(2)}) copy-start(bf16[64,768]{1,0:T(8,128)(2,1)S(1)} %constant_dynamic-slice_fusion.up) | copy-start | bytes 294916
  63.9 1.2 copy-start.3
  65.1 18.3 %copy-start.4 = (bf16[6144,64]{0,1:T(8,128)(2,1)S(1)}, bf16[6144,64]{0,1:T(8,128)(2,1)}, u32[]{:S(2)}) copy-start(bf16[6144,64]{0,1:T(8,128)(2,1)} %param.7) | copy-start | bytes 2359300
  85.8 0.9 copy-start.6
  87.3 23.3 %copy-start.9 = (s32[32]{0:T(128)S(1)}, s32[32]{0:T(128)}, u32[]{:S(2)}) copy-start(s32[32]{0:T(128)} %reshape.687.lies) | copy-start | bytes 388
  98.4 27.2 %collective-permute-start.4 = (bf16[256,3072]{1,0:T(8,128)(2,1)}, bf16[256,3072]{1,0:T(8,128)(2,1)}, u32[]{:S(2)}, u32[]{:S(2)}) collective-permute-start(bf16[256,3072]{1,0:T(8,128)(2,1)} %get-tuple-element.17), channel_id=1, source_target_pairs={{0,1},{1,0},{2,3},{3,2},{4,5},{5,4},{6,7},{7,6},{8,9},{9,8},{10,11... | collective-permute-start | bytes 4718600 | tf_op jit(solution)/shard_map/ppermute | solution.py:35
  100.6 29.3 %all-to-all-start = ((bf16[16,64,256]{2,1,0:T(8,128)(2,1)}), bf16[16,64,256]{2,1,0:T(8,128)(2,1)}, u32[]{:S(2)}, u32[]{:S(2)}) async-start(bf16[16,64,256]{2,1,0:T(8,128)(2,1)} %bitcast.50), calls=%async_computation | async-start | bytes 1048576 | tf_op jit(solution)/shard_map/all_to_all | solution.py:211
  110.6 3.7 %copy-start.1 = (bf16[6144,768]{1,0:T(8,128)(2,1)S(1)}, bf16[6144,768]{1,0:T(8,128)(2,1)}, u32[]{:S(2)}) copy-start(bf16[6144,768]{1,0:T(8,128)(2,1)} %all-gather.2.cloned.1.call-done.w) | copy-start | bytes 28311556
  114.3 1.0 copy-start.7
  119.4 10.4 %copy-start.12 = (bf16[64,768]{1,0:T(8,128)(2,1)S(1)}, bf16[64,768]{1,0:T(8,128)(2,1)}, u32[]{:S(2)}) copy-start(bf16[64,768]{1,0:T(8,128)(2,1)} %get-tuple-element.20) | copy-start | bytes 294916
  127.9 15.7 %collective-permute-start.5 = (bf16[256,1536]{1,0:T(8,128)(2,1)}, bf16[256,1536]{1,0:T(8,128)(2,1)}, u32[]{:S(2)}, u32[]{:S(2)}) collective-permute-start(bf16[256,1536]{1,0:T(8,128)(2,1)} %add_convert_fusion), channel_id=1, source_target_pairs={{0,3},{1,2},{2,1},{3,0},{4,7},{5,6},{6,5},{7,4},{8,11},{9,10},{10,... | collective-permute-start | bytes 2359304 | tf_op jit(solution)/shard_map/ppermute | solution.py:35
  131.0 1.0 copy-start.11
  132.0 22.4 %all-to-all-start.1 = ((bf16[32,8,384]{2,1,0:T(8,128)(2,1)}), bf16[32,8,384]{2,1,0:T(8,128)(2,1)S(1)}, u32[]{:S(2)}, u32[]{:S(2)}) async-start(bf16[32,8,384]{2,1,0:T(8,128)(2,1)} %maximum_bitcast_fusion), calls=%async_computation.1 | async-start | bytes 393216 | tf_op jit(solution)/shard_map/all_to_all | solution.py:211
  145.6 16.9 %collective-permute-start.6 = (bf16[256,768]{1,0:T(8,128)(2,1)}, bf16[256,768]{1,0:T(8,128)(2,1)}, u32[]{:S(2)}, u32[]{:S(2)}) collective-permute-start(bf16[256,768]{1,0:T(8,128)(2,1)} %add_convert_fusion.1), channel_id=1, source_target_pairs={{0,4},{1,5},{2,6},{3,7},{4,0},{5,1},{6,2},{7,3},{8,12},{9,13},{10,... | collective-permute-start | bytes 1179656 | tf_op jit(solution)/shard_map/ppermute | solution.py:35
  155.2 18.2 %all-to-all-start.2 = ((bf16[32,8,384]{2,1,0:T(8,128)(2,1)}), bf16[32,8,384]{2,1,0:T(8,128)(2,1)}, u32[]{:S(2)}, u32[]{:S(2)}) async-start(bf16[32,8,384]{2,1,0:T(8,128)(2,1)} %broadcast_in_dim.10), calls=%async_computation.2 | async-start | bytes 393216 | tf_op jit(solution)/shard_map/all_to_all | solution.py:211
  164.4 12.1 %collective-permute-start.7 = (bf16[256,384]{1,0:T(8,128)(2,1)}, bf16[256,384]{1,0:T(8,128)(2,1)}, u32[]{:S(2)}, u32[]{:S(2)}) collective-permute-start(bf16[256,384]{1,0:T(8,128)(2,1)} %add_convert_fusion.3), channel_id=1, source_target_pairs={{0,12},{1,13},{2,14},{3,15},{4,8},{5,9},{6,10},{7,11},{8,4},{9,5},... | collective-permute-start | bytes 589832 | tf_op jit(solution)/shard_map/ppermute | solution.py:35
  (1 other events, 0.6 us)
Sparse Core Ops, SparseCore 0:
  18.7 67.9 all-gather.1

commit v9 on v8

--- a/solution.py
+++ b/solution.py
@@ -236,10 +236,11 @@
     table = jnp.stack([((y_hi ^ step[r]) << 2) | (x_at ^ step[q]) for q in range(4) for r in range(4)])
 
     both = lax.all_gather(up_weight, "fsdp", axis=0, tiled=True, axis_index_groups=PAIRS)
+    both, next_y = lax.optimization_barrier((both, y_first(normed_tokens)))
     gathered = lax.all_gather(both, "fsdp", axis=0, tiled=True, axis_index_groups=PLANES)
     lies = jnp.stack([(table >> 1) * 4 + (table & 1) + 2 * c for c in range(C)], axis=1).reshape(-1)
 
-    pair = jnp.concatenate([normed_tokens, y_first(normed_tokens)], axis=1)
+    pair = jnp.concatenate([normed_tokens, next_y], axis=1)
     column = jnp.concatenate([pair, y_second(pair)], axis=1)
     near = jnp.concatenate([column, x_first(column)], axis=1)
     far = x_second(near)
@@ -273,10 +274,11 @@
     members = Z * YL * C
     grads = gather_small(add_parts(shares, members), "fsdp", members)
 
-    to_last = total([kept, over_x, over_next, over_y], width, 2 * width).astype(bf16)
+    own = total([kept, over_x, over_next], 0, 2 * width)
+    to_last = (own[:, width:] + widen(over_y[:, width:])).astype(bf16)
     over_last = y_first(to_last)
     down_rows = lax.dynamic_slice_in_dim(adapter_down, model_index * width, width, 0)
-    own = total([kept, over_x, over_next, over_y], 0, width) + contract(rank_grad, down_rows, 0, 1)
+    own = own[:, :width] + widen(over_y[:, :width]) + contract(rank_grad, down_rows, 0, 1)
     own, over_last, grads = lax.optimization_barrier((own, over_last, grads))
     normed_grad = (own + widen(over_last)).astype(bf16)
     up_grad = jnp.concatenate([grads[:rank], grads[rank : 2 * rank]], axis=1)

time: 189 us -> 190 us (level)
  waiting for transfers between devices: 61.8 us -> 70.8 us
  starting transfers between devices: 57.8 us -> 51.5 us
    all_gather x1, waiting for transfers between devices: 0.01 us -> 11.1 us  [body(): lax.all_gather(both, 'fsdp', axis=0, tiled=True, axis_index_groups=PLANES)]
    all_to_all x3, starting transfers between devices: 28.9 us -> 22.2 us  [exchange(): return lax.all_to_all(value, axis, 0, 0, tiled=True)]
    all_to_all x3, waiting for transfers between devices: 6.27 us -> 0.01 us  [exchange(): return lax.all_to_all(value, axis, 0, 0, tiled=True)]
    ppermute x8, waiting for transfers between devices: 55.5 us -> 59.7 us  [send(): return lax.ppermute(value, ('fsdp', 'mp'), pairs)]
where the time goes in v9:
time: 190 us; the launch traced here: 189 us
  waiting for transfers between devices  70.8 us (37%)
  starting transfers between devices  51.5 us (27%)
  Pallas kernels  18.8 us (10%)
  between operations  14.4 us (8%)
  blocking collectives  11.9 us (6%)
  other arithmetic  10.1 us (5%)
  local copies, waits for them, and re-layouts  9.9 us (5%)
    ppermute x8, waiting for transfers between devices, send(): return lax.ppermute(value, ('fsdp', 'mp'), pairs)  59.7 us
    ppermute x8, starting transfers between devices, send(): return lax.ppermute(value, ('fsdp', 'mp'), pairs)  29.2 us
    all_to_all x3, starting transfers between devices, exchange(): return lax.all_to_all(value, axis, 0, 0, tiled=True)  22.2 us
    all_gather x1, blocking collectives, body(): lax.all_gather(up_weight, 'fsdp', axis=0, tiled=True, axis_index_groups=P...  11.9 us
    all_gather x1, waiting for transfers between devices, body(): lax.all_gather(both, 'fsdp', axis=0, tiled=True, axis_index_groups=PLANES)  11.1 us
    pallas_call x1, Pallas kernels, forward(): pl.pallas_call(main_kernel, out_shape=(jax.ShapeDtypeStruct((rows, hidden...  11.1 us
    unnamed x29, local copies, waits for them, and re-layouts  7.46 us
    pallas_call x1, Pallas kernels, kept_half(): pl.pallas_call(kept_kernel, out_shape=jax.ShapeDtypeStruct((rows, half),...  4.14 us
  transfers between devices with their start and end apart: 12, of which 8 were waited for; matrix products, arithmetic and copies ran while one was open for 6% of the time, Pallas kernels for 4%

profile of v9, /device:TPU:6, one launch (start us, length us, event | category | flops | bytes accessed | tf_op | source)
XLA Modules:
  0.0 188.6 jit_solution(14473127741053193898)
XLA Ops:
  7.2 6.3 %collective-permute-start = (bf16[256,384]{1,0:T(8,128)(2,1)}, bf16[256,384]{1,0:T(8,128)(2,1)S(1)}, u32[]{:S(2)}, u32[]{:S(2)}) collective-permute-start(bf16[256,384]{1,0:T(8,128)(2,1)} %param.5), channel_id=1, source_target_pairs={{0,12},{1,13},{2,14},{3,15},{4,8},{5,9},{6,10},{7,11},{8,4},{9,5},... | collective-permute-start | bytes 589832 | tf_op jit(solution)/shard_map/ppermute | solution.py:35
  13.5 11.9 %all_gather.6 = bf16[384,768]{1,0:T(8,128)(2,1)} all-gather(bf16[192,768]{1,0:T(8,128)(2,1)} %param.6), channel_id=1, replica_groups={{0,32},{16,48},{64,96},{80,112},{128,160},{144,176},{192,224},{208,240}..., dimensions={0}, use_global_device_ids=true | all-gather | bytes 884736 | tf_op jit(solution)/shard_map/all_gather | solution.py:238
  27.5 12.2 %collective-permute-done.1 = bf16[256,768]{1,0:T(8,128)(2,1)S(1)} collective-permute-done((bf16[256,768]{1,0:T(8,128)(2,1)S(1)}, bf16[256,768]{1,0:T(8,128)(2,1)S(1)}, u32[]{:S(2)}, u32[]{:S(2)}) %collective-permute-start.1) | collective-permute-done | bytes 393248 | tf_op jit(solution)/shard_map/ppermute | solution.py:35
  39.7 2.4 %collective-permute-start.2 = (bf16[256,1536]{1,0:T(8,128)(2,1)S(1)}, bf16[256,1536]{1,0:T(8,128)(2,1)S(1)}, u32[]{:S(2)}, u32[]{:S(2)}) collective-permute-start(bf16[256,1536]{1,0:T(8,128)(2,1)S(1)} %pad_maximum_fusion), channel_id=1, source_target_pairs={{0,3},{1,2},{2,1},{3,0},{4,7},{5,6},{6,5},{7,4},{8,11},{9,10},{10,... | collective-permute-start | bytes 2359304 | tf_op jit(solution)/shard_map/ppermute | solution.py:35
  42.3 12.6 %collective-permute-done.2 = bf16[256,1536]{1,0:T(8,128)(2,1)S(1)} collective-permute-done((bf16[256,1536]{1,0:T(8,128)(2,1)S(1)}, bf16[256,1536]{1,0:T(8,128)(2,1)S(1)}, u32[]{:S(2)}, u32[]{:S(2)}) %collective-permute-start.2) | collective-permute-done | bytes 786464 | tf_op jit(solution)/shard_map/ppermute | solution.py:35
  60.2 17.2 %collective-permute-done.3.xb = bf16[256,3072]{1,0:T(8,128)(2,1)} collective-permute-done((bf16[256,3072]{1,0:T(8,128)(2,1)S(1)}, bf16[256,3072]{1,0:T(8,128)(2,1)}, u32[]{:S(2)}, u32[]{:S(2)}) %collective-permute-start.3) | collective-permute-done | bytes 1572896 | tf_op jit(solution)/shard_map/ppermute | solution.py:35
  77.4 2.5 %far_lowrank.1 = (bf16[64,256]{1,0:T(8,128)(2,1)S(1)}, f32[256,768]{1,0:T(8,128)S(1)}) custom-call(s32[16]{0:T(128)S(1)} %stack.124.table, bf16[256,3072]{1,0:T(8,128)(2,1)} %collective-permute-done.3.xb, bf16[64,6144]{1,0:T(8,128)(2,1)S(1)} %bitcast.48, f32[64,256]{1,0:T(8,128)S(1)} %near_lowrank.1.low_near, bf16[64,768]{1,0:T(8,128)(2,1)S(1)} %constant_dynamic-slice_fusion.up), custom_call_target="tpu_custom_call" | custom-call | flops 125829120 | bytes 4194304 | tf_op jit(solution)/shard_map/far_lowrank/pallas_call | solution.py:142
  81.4 11.1 %all-gather.2.cloned.1.call-done.w = bf16[6144,768]{1,0:T(8,128)(2,1)} async-done(((bf16[384,768]{1,0:T(8,128)(2,1)}), bf16[6144,768]{1,0:T(8,128)(2,1)}) %all-gather.2.cloned.1.call-update) | async-done | bytes 9437200 | tf_op jit(solution)/shard_map/all_gather | solution.py:240
  92.5 11.1 %forward.1 = (bf16[256,768]{1,0:T(8,128)(2,1)}, bf16[1024,256]{1,0:T(8,128)(2,1)}, bf16[64,768]{1,0:T(8,128)(2,1)}, bf16[256,3072]{1,0:T(8,128)(2,1)}) custom-call(s32[32]{0:T(128)} %reshape.687.lies, bf16[256,3072]{1,0:T(8,128)(2,1)} %copy-done.2, bf16[256,3072]{1,0:T(8,128)(2,1)} %collective-permute-done.3.xb, ...), custom_call_target="tpu_custom_call" | custom-call | flops 3623878656 | bytes 14680064 | tf_op jit(solution)/shard_map/forward/pallas_call | solution.py:157
  103.6 2.8 %collective-permute-start.4 = (bf16[256,3072]{1,0:T(8,128)(2,1)}, bf16[256,3072]{1,0:T(8,128)(2,1)}, u32[]{:S(2)}, u32[]{:S(2)}) collective-permute-start(bf16[256,3072]{1,0:T(8,128)(2,1)} %get-tuple-element.21), channel_id=1, source_target_pairs={{0,1},{1,0},{2,3},{3,2},{4,5},{5,4},{6,7},{7,6},{8,9},{9,8},{10,11... | collective-permute-start | bytes 4718600 | tf_op jit(solution)/shard_map/ppermute | solution.py:35
  106.3 10.0 %all-to-all-start = ((bf16[16,64,256]{2,1,0:T(8,128)(2,1)}), bf16[16,64,256]{2,1,0:T(8,128)(2,1)}, u32[]{:S(2)}, u32[]{:S(2)}) async-start(bf16[16,64,256]{2,1,0:T(8,128)(2,1)} %bitcast.51), calls=%async_computation | async-start | bytes 1048576 | tf_op jit(solution)/shard_map/all_to_all | solution.py:211
  116.4 3.7 %copy-done.1 = bf16[6144,768]{1,0:T(8,128)(2,1)S(1)} copy-done((bf16[6144,768]{1,0:T(8,128)(2,1)S(1)}, bf16[6144,768]{1,0:T(8,128)(2,1)}, u32[]{:S(2)}) %copy-start.1) | copy-done | bytes 9437208
  121.1 4.1 %kept_half.1 = bf16[256,3072]{1,0:T(8,128)(2,1)S(1)} custom-call(s32[32]{0:T(128)S(1)} %copy-done.8, bf16[256,768]{1,0:T(8,128)(2,1)S(1)} %copy-done.6, bf16[6144,768]{1,0:T(8,128)(2,1)S(1)} %copy-done.1), custom_call_target="tpu_custom_call" | custom-call | flops 1207959552 | bytes 7340032 | tf_op jit(solution)/shard_map/kept_half/pallas_call | solution.py:192
  125.2 5.4 %collective-permute-done.4 = bf16[256,3072]{1,0:T(8,128)(2,1)} collective-permute-done((bf16[256,3072]{1,0:T(8,128)(2,1)}, bf16[256,3072]{1,0:T(8,128)(2,1)}, u32[]{:S(2)}, u32[]{:S(2)}) %collective-permute-start.4) | collective-permute-done | bytes 1572896 | tf_op jit(solution)/shard_map/ppermute | solution.py:35
  130.6 2.3 %add_convert_fusion = bf16[256,1536]{1,0:T(8,128)(2,1)} fusion(bf16[256,3072]{1,0:T(8,128)(2,1)} %collective-permute-done.4, bf16[256,3072]{1,0:T(8,128)(2,1)S(1)} %kept_half.1), kind=kLoop, calls=%fused_computation | loop fusion | flops 1572864 | bytes 2359296 | tf_op jit(solution)/shard_map/convert_element_type | solution.py:259
  132.9 2.6 %collective-permute-start.5 = (bf16[256,1536]{1,0:T(8,128)(2,1)}, bf16[256,1536]{1,0:T(8,128)(2,1)}, u32[]{:S(2)}, u32[]{:S(2)}) collective-permute-start(bf16[256,1536]{1,0:T(8,128)(2,1)} %add_convert_fusion), channel_id=1, source_target_pairs={{0,3},{1,2},{2,1},{3,0},{4,7},{5,6},{6,5},{7,4},{8,11},{9,10},{10,... | collective-permute-start | bytes 2359304 | tf_op jit(solution)/shard_map/ppermute | solution.py:35
  137.7 5.7 %all-to-all-start.1 = ((bf16[32,8,384]{2,1,0:T(8,128)(2,1)}), bf16[32,8,384]{2,1,0:T(8,128)(2,1)S(1)}, u32[]{:S(2)}, u32[]{:S(2)}) async-start(bf16[32,8,384]{2,1,0:T(8,128)(2,1)} %maximum_bitcast_fusion), calls=%async_computation.1 | async-start | bytes 393216 | tf_op jit(solution)/shard_map/all_to_all | solution.py:211
  143.4 4.8 %collective-permute-done.5 = bf16[256,1536]{1,0:T(8,128)(2,1)} collective-permute-done((bf16[256,1536]{1,0:T(8,128)(2,1)}, bf16[256,1536]{1,0:T(8,128)(2,1)}, u32[]{:S(2)}, u32[]{:S(2)}) %collective-permute-start.5) | collective-permute-done | bytes 786464 | tf_op jit(solution)/shard_map/ppermute | solution.py:35
  148.3 2.6 %add_convert_fusion.1 = (bf16[256,768]{1,0:T(8,128)(2,1)}, f32[256,768]{1,0:T(8,128)}) fusion(bf16[256,1536]{1,0:T(8,128)(2,1)} %collective-permute-done.5, bf16[256,3072]{1,0:T(8,128)(2,1)} %collective-permute-done.4, bf16[256,3072]{1,0:T(8,128)(2,1)S(1)} %kept_half.1), kind=kLoop, calls=%fused_computation.3 | loop fusion | flops 2162688 | bytes 3538944 | tf_op jit(solution)/shard_map/convert_element_type | solution.py:271
  150.9 3.9 %collective-permute-start.6 = (bf16[256,768]{1,0:T(8,128)(2,1)}, bf16[256,768]{1,0:T(8,128)(2,1)S(1)}, u32[]{:S(2)}, u32[]{:S(2)}) collective-permute-start(bf16[256,768]{1,0:T(8,128)(2,1)} %get-tuple-element.31), channel_id=1, source_target_pairs={{0,4},{1,5},{2,6},{3,7},{4,0},{5,1},{6,2},{7,3},{8,12},{9,13},{10,... | collective-permute-start | bytes 1179656 | tf_op jit(solution)/shard_map/ppermute | solution.py:35
  155.6 6.4 %all-to-all-start.2 = ((bf16[32,8,384]{2,1,0:T(8,128)(2,1)}), bf16[32,8,384]{2,1,0:T(8,128)(2,1)S(1)}, u32[]{:S(2)}, u32[]{:S(2)}) async-start(bf16[32,8,384]{2,1,0:T(8,128)(2,1)} %broadcast_in_dim.10), calls=%async_computation.2 | async-start | bytes 393216 | tf_op jit(solution)/shard_map/all_to_all | solution.py:211
  162.0 3.2 %collective-permute-done.6 = bf16[256,768]{1,0:T(8,128)(2,1)S(1)} collective-permute-done((bf16[256,768]{1,0:T(8,128)(2,1)}, bf16[256,768]{1,0:T(8,128)(2,1)S(1)}, u32[]{:S(2)}, u32[]{:S(2)}) %collective-permute-start.6) | collective-permute-done | bytes 393248 | tf_op jit(solution)/shard_map/ppermute | solution.py:35
  167.0 7.4 %collective-permute-start.7 = (bf16[256,384]{1,0:T(8,128)(2,1)}, bf16[256,384]{1,0:T(8,128)(2,1)S(1)}, u32[]{:S(2)}, u32[]{:S(2)}) collective-permute-start(bf16[256,384]{1,0:T(8,128)(2,1)} %fusion), channel_id=1, source_target_pairs={{0,12},{1,13},{2,14},{3,15},{4,8},{5,9},{6,10},{7,11},{8,4},{9,5},... | collective-permute-start | bytes 589832 | tf_op jit(solution)/shard_map/ppermute | solution.py:35
  175.5 4.3 %collective-permute-done.7 = bf16[256,384]{1,0:T(8,128)(2,1)S(1)} collective-permute-done((bf16[256,384]{1,0:T(8,128)(2,1)}, bf16[256,384]{1,0:T(8,128)(2,1)S(1)}, u32[]{:S(2)}, u32[]{:S(2)}) %collective-permute-start.7) | collective-permute-done | bytes 196640 | tf_op jit(solution)/shard_map/ppermute | solution.py:35
  (60 shorter events, 17.6 us)
Async XLA Ops:
  7.2 50.7 %copy-start = (bf16[64,12288]{1,0:T(8,128)(2,1)S(1)}, bf16[64,12288]{1,0:T(8,128)(2,1)}, u32[]{:S(2)}) copy-start(bf16[64,12288]{1,0:T(8,128)(2,1)} %param.8) | copy-start | bytes 4718596
  7.2 18.3 %copy-start.10 = (bf16[256,384]{1,0:T(8,128)(2,1)S(1)}, bf16[256,384]{1,0:T(8,128)(2,1)}, u32[]{:S(2)}) copy-start(bf16[256,384]{1,0:T(8,128)(2,1)} %param.5) | copy-start | bytes 589828
  7.2 85.3 %all-gather.2.cloned.1.call-start = ((), (), s32[]{:S(2)}) async-start(), calls=%async_computation.3 | async-start | bytes 10027008 | tf_op jit(solution)/shard_map/all_gather | solution.py:240
  7.2 18.2 %collective-permute-start = (bf16[256,384]{1,0:T(8,128)(2,1)}, bf16[256,384]{1,0:T(8,128)(2,1)S(1)}, u32[]{:S(2)}, u32[]{:S(2)}) collective-permute-start(bf16[256,384]{1,0:T(8,128)(2,1)} %param.5), channel_id=1, source_target_pairs={{0,12},{1,13},{2,14},{3,15},{4,8},{5,9},{6,10},{7,11},{8,4},{9,5},... | collective-permute-start | bytes 589832 | tf_op jit(solution)/shard_map/ppermute | solution.py:35
  25.5 14.1 %collective-permute-start.1 = (bf16[256,768]{1,0:T(8,128)(2,1)S(1)}, bf16[256,768]{1,0:T(8,128)(2,1)S(1)}, u32[]{:S(2)}, u32[]{:S(2)}) collective-permute-start(bf16[256,768]{1,0:T(8,128)(2,1)S(1)} %pad_maximum_fusion.1), channel_id=1, source_target_pairs={{0,4},{1,5},{2,6},{3,7},{4,0},{5,1},{6,2},{7,3},{8,12},{9,13},{10,... | collective-permute-start | bytes 1179656 | tf_op jit(solution)/shard_map/ppermute | solution.py:35
  39.7 15.1 %collective-permute-start.2 = (bf16[256,1536]{1,0:T(8,128)(2,1)S(1)}, bf16[256,1536]{1,0:T(8,128)(2,1)S(1)}, u32[]{:S(2)}, u32[]{:S(2)}) collective-permute-start(bf16[256,1536]{1,0:T(8,128)(2,1)S(1)} %pad_maximum_fusion), channel_id=1, source_target_pairs={{0,3},{1,2},{2,1},{3,0},{4,7},{5,6},{6,5},{7,4},{8,11},{9,10},{10,... | collective-permute-start | bytes 2359304 | tf_op jit(solution)/shard_map/ppermute | solution.py:35
  54.9 25.0 %copy-start.2 = (bf16[256,3072]{1,0:T(8,128)(2,1)}, bf16[256,3072]{1,0:T(8,128)(2,1)S(1)}, u32[]{:S(2)}) copy-start(bf16[256,3072]{1,0:T(8,128)(2,1)S(1)} %constant_dynamic-update-slice_fusion.xa) | copy-start | bytes 4718596
  54.9 22.4 %collective-permute-start.3 = (bf16[256,3072]{1,0:T(8,128)(2,1)S(1)}, bf16[256,3072]{1,0:T(8,128)(2,1)}, u32[]{:S(2)}, u32[]{:S(2)}) collective-permute-start(bf16[256,3072]{1,0:T(8,128)(2,1)S(1)} %constant_dynamic-update-slice_fusion.xa), channel_id=1, source_target_pairs={{0,1},{1,0},{2,3},{3,2},{4,5},{5,4},{6,7},{7,6},{8,9},{9,8},{10,11... | collective-permute-start | bytes 4718600 | tf_op jit(solution)/shard_map/ppermute | solution.py:35
  57.9 22.0 %copy-start.4 = (bf16[64,768]{1,0:T(8,128)(2,1)}, bf16[64,768]{1,0:T(8,128)(2,1)S(1)}, u32[]{:S(2)}) copy-start(bf16[64,768]{1,0:T(8,128)(2,1)S(1)} %constant_dynamic-slice_fusion.up) | copy-start | bytes 294916
  57.9 1.2 copy-start.3
  79.9 0.9 copy-start.5
  92.5 23.9 %copy-start.8 = (s32[32]{0:T(128)S(1)}, s32[32]{0:T(128)}, u32[]{:S(2)}) copy-start(s32[32]{0:T(128)} %reshape.687.lies) | copy-start | bytes 388
  103.6 27.0 %collective-permute-start.4 = (bf16[256,3072]{1,0:T(8,128)(2,1)}, bf16[256,3072]{1,0:T(8,128)(2,1)}, u32[]{:S(2)}, u32[]{:S(2)}) collective-permute-start(bf16[256,3072]{1,0:T(8,128)(2,1)} %get-tuple-element.21), channel_id=1, source_target_pairs={{0,1},{1,0},{2,3},{3,2},{4,5},{5,4},{6,7},{7,6},{8,9},{9,8},{10,11... | collective-permute-start | bytes 4718600 | tf_op jit(solution)/shard_map/ppermute | solution.py:35
  106.3 29.3 %all-to-all-start = ((bf16[16,64,256]{2,1,0:T(8,128)(2,1)}), bf16[16,64,256]{2,1,0:T(8,128)(2,1)}, u32[]{:S(2)}, u32[]{:S(2)}) async-start(bf16[16,64,256]{2,1,0:T(8,128)(2,1)} %bitcast.51), calls=%async_computation | async-start | bytes 1048576 | tf_op jit(solution)/shard_map/all_to_all | solution.py:211
  116.4 3.7 %copy-start.1 = (bf16[6144,768]{1,0:T(8,128)(2,1)S(1)}, bf16[6144,768]{1,0:T(8,128)(2,1)}, u32[]{:S(2)}) copy-start(bf16[6144,768]{1,0:T(8,128)(2,1)} %all-gather.2.cloned.1.call-done.w) | copy-start | bytes 28311556
  120.1 1.0 copy-start.6
  125.2 10.4 %copy-start.12 = (bf16[64,768]{1,0:T(8,128)(2,1)S(1)}, bf16[64,768]{1,0:T(8,128)(2,1)}, u32[]{:S(2)}) copy-start(bf16[64,768]{1,0:T(8,128)(2,1)} %get-tuple-element.24) | copy-start | bytes 294916
  132.9 15.4 %collective-permute-start.5 = (bf16[256,1536]{1,0:T(8,128)(2,1)}, bf16[256,1536]{1,0:T(8,128)(2,1)}, u32[]{:S(2)}, u32[]{:S(2)}) collective-permute-start(bf16[256,1536]{1,0:T(8,128)(2,1)} %add_convert_fusion), channel_id=1, source_target_pairs={{0,3},{1,2},{2,1},{3,0},{4,7},{5,6},{6,5},{7,4},{8,11},{9,10},{10,... | collective-permute-start | bytes 2359304 | tf_op jit(solution)/shard_map/ppermute | solution.py:35
  136.7 1.0 copy-start.11
  137.7 17.1 %all-to-all-start.1 = ((bf16[32,8,384]{2,1,0:T(8,128)(2,1)}), bf16[32,8,384]{2,1,0:T(8,128)(2,1)S(1)}, u32[]{:S(2)}, u32[]{:S(2)}) async-start(bf16[32,8,384]{2,1,0:T(8,128)(2,1)} %maximum_bitcast_fusion), calls=%async_computation.1 | async-start | bytes 393216 | tf_op jit(solution)/shard_map/all_to_all | solution.py:211
  150.9 23.5 %copy-start.9 = (f32[256,768]{1,0:T(8,128)S(1)}, f32[256,768]{1,0:T(8,128)}, u32[]{:S(2)}) copy-start(f32[256,768]{1,0:T(8,128)} %get-tuple-element.32) | copy-start | bytes 2359300
  150.9 14.3 %collective-permute-start.6 = (bf16[256,768]{1,0:T(8,128)(2,1)}, bf16[256,768]{1,0:T(8,128)(2,1)S(1)}, u32[]{:S(2)}, u32[]{:S(2)}) collective-permute-start(bf16[256,768]{1,0:T(8,128)(2,1)} %get-tuple-element.31), channel_id=1, source_target_pairs={{0,4},{1,5},{2,6},{3,7},{4,0},{5,1},{6,2},{7,3},{8,12},{9,13},{10,... | collective-permute-start | bytes 1179656 | tf_op jit(solution)/shard_map/ppermute | solution.py:35
  155.6 19.9 %all-to-all-start.2 = ((bf16[32,8,384]{2,1,0:T(8,128)(2,1)}), bf16[32,8,384]{2,1,0:T(8,128)(2,1)S(1)}, u32[]{:S(2)}, u32[]{:S(2)}) async-start(bf16[32,8,384]{2,1,0:T(8,128)(2,1)} %broadcast_in_dim.10), calls=%async_computation.2 | async-start | bytes 393216 | tf_op jit(solution)/shard_map/all_to_all | solution.py:211
  167.0 12.8 %collective-permute-start.7 = (bf16[256,384]{1,0:T(8,128)(2,1)}, bf16[256,384]{1,0:T(8,128)(2,1)S(1)}, u32[]{:S(2)}, u32[]{:S(2)}) collective-permute-start(bf16[256,384]{1,0:T(8,128)(2,1)} %fusion), channel_id=1, source_target_pairs={{0,12},{1,13},{2,14},{3,15},{4,8},{5,9},{6,10},{7,11},{8,4},{9,5},... | collective-permute-start | bytes 589832 | tf_op jit(solution)/shard_map/ppermute | solution.py:35
  (1 other events, 0.6 us)
Sparse Core Ops, SparseCore 0:
  25.6 66.8 all-gather.1

commit v10 on v9

--- a/solution.py
+++ b/solution.py
@@ -144,7 +144,7 @@
         out_shape=(jax.ShapeDtypeStruct((rank, rows), bf16), jax.ShapeDtypeStruct((rows, hidden), f32)),
         in_specs=[SMEM, VMEM, VMEM, VMEM, VMEM],
         out_specs=(VMEM, VMEM),
-        compiler_params=pltpu.CompilerParams(vmem_limit_bytes=8 * 2**20),
+        compiler_params=pltpu.CompilerParams(vmem_limit_bytes=56 * 2**20),
         cost_estimate=pl.CostEstimate(
             flops=2 * rows * rank * (xb.shape[1] + hidden), bytes_accessed=4 * 2**20, transcendentals=0
         ),
@@ -236,11 +236,10 @@
     table = jnp.stack([((y_hi ^ step[r]) << 2) | (x_at ^ step[q]) for q in range(4) for r in range(4)])
 
     both = lax.all_gather(up_weight, "fsdp", axis=0, tiled=True, axis_index_groups=PAIRS)
-    both, next_y = lax.optimization_barrier((both, y_first(normed_tokens)))
     gathered = lax.all_gather(both, "fsdp", axis=0, tiled=True, axis_index_groups=PLANES)
     lies = jnp.stack([(table >> 1) * 4 + (table & 1) + 2 * c for c in range(C)], axis=1).reshape(-1)
 
-    pair = jnp.concatenate([normed_tokens, next_y], axis=1)
+    pair = jnp.concatenate([normed_tokens, y_first(normed_tokens)], axis=1)
     column = jnp.concatenate([pair, y_second(pair)], axis=1)
     near = jnp.concatenate([column, x_first(column)], axis=1)
     far = x_second(near)

time: 190 us -> 188 us (0.989)
  waiting for transfers between devices: 70.8 us -> 59.8 us
  starting transfers between devices: 51.5 us -> 59 us
    all_gather x1, waiting for transfers between devices: 11.1 us -> 0.01 us  [body(): lax.all_gather(both, 'fsdp', axis=0, tiled=True, axis_index_groups=PLANES)]
    all_to_all x3, starting transfers between devices: 22.2 us -> 29.3 us  [exchange(): return lax.all_to_all(value, axis, 0, 0, tiled=True)]
    all_to_all x3, waiting for transfers between devices: 0.01 us -> 6.01 us  [exchange(): return lax.all_to_all(value, axis, 0, 0, tiled=True)]
    ppermute x8, waiting for transfers between devices: 59.7 us -> 53.8 us  [send(): return lax.ppermute(value, ('fsdp', 'mp'), pairs)]
    unnamed x29 -> x27, local copies, waits for them, and re-layouts: 7.46 us -> 6.57 us
  transfers between devices with their start and end apart: 12 -> 12, of which waited for: 8 -> 8; matrix products, arithmetic and copies ran while one was open for 6% -> 7% of each run, Pallas kernels for 4% -> 5%
where the time goes in v10:
time: 188 us; the launch traced here: 186 us
  waiting for transfers between devices  59.8 us (32%)
  starting transfers between devices  59 us (31%)
  Pallas kernels  20 us (11%)
  between operations  14.4 us (8%)
  blocking collectives  11.3 us (6%)
  other arithmetic  10.1 us (5%)
  local copies, waits for them, and re-layouts  9.67 us (5%)
    ppermute x8, waiting for transfers between devices, send(): return lax.ppermute(value, ('fsdp', 'mp'), pairs)  53.8 us
    ppermute x8, starting transfers between devices, send(): return lax.ppermute(value, ('fsdp', 'mp'), pairs)  29.7 us
    all_to_all x3, starting transfers between devices, exchange(): return lax.all_to_all(value, axis, 0, 0, tiled=True)  29.3 us
    all_gather x1, blocking collectives, body(): lax.all_gather(up_weight, 'fsdp', axis=0, tiled=True, axis_index_groups=P...  11.3 us
    pallas_call x1, Pallas kernels, forward(): pl.pallas_call(main_kernel, out_shape=(jax.ShapeDtypeStruct((rows, hidden...  11.1 us
    unnamed x27, local copies, waits for them, and re-layouts  6.57 us
    all_to_all x3, waiting for transfers between devices, exchange(): return lax.all_to_all(value, axis, 0, 0, tiled=True)  6.01 us
    pallas_call x1, Pallas kernels, kept_half(): pl.pallas_call(kept_kernel, out_shape=jax.ShapeDtypeStruct((rows, half),...  4.14 us
  transfers between devices with their start and end apart: 12, of which 8 were waited for; matrix products, arithmetic and copies ran while one was open for 7% of the time, Pallas kernels for 5%

profile of v10, /device:TPU:6, one launch (start us, length us, event | category | flops | bytes accessed | tf_op | source)
XLA Modules:
  0.0 185.5 jit_solution(8997562344968201157)
XLA Ops:
  7.2 11.3 %all_gather.6 = bf16[384,768]{1,0:T(8,128)(2,1)} all-gather(bf16[192,768]{1,0:T(8,128)(2,1)} %param.6), channel_id=1, replica_groups={{0,32},{16,48},{64,96},{80,112},{128,160},{144,176},{192,224},{208,240}..., dimensions={0}, use_global_device_ids=true | all-gather | bytes 884736 | tf_op jit(solution)/shard_map/all_gather | solution.py:238
  18.6 5.3 %collective-permute-start = (bf16[256,384]{1,0:T(8,128)(2,1)}, bf16[256,384]{1,0:T(8,128)(2,1)S(1)}, u32[]{:S(2)}, u32[]{:S(2)}) collective-permute-start(bf16[256,384]{1,0:T(8,128)(2,1)} %param.5), channel_id=1, source_target_pairs={{0,12},{1,13},{2,14},{3,15},{4,8},{5,9},{6,10},{7,11},{8,4},{9,5},... | collective-permute-start | bytes 589832 | tf_op jit(solution)/shard_map/ppermute | solution.py:35
  23.9 5.6 %collective-permute-done = bf16[256,384]{1,0:T(8,128)(2,1)S(1)} collective-permute-done((bf16[256,384]{1,0:T(8,128)(2,1)}, bf16[256,384]{1,0:T(8,128)(2,1)S(1)}, u32[]{:S(2)}, u32[]{:S(2)}) %collective-permute-start) | collective-permute-done | bytes 196640 | tf_op jit(solution)/shard_map/ppermute | solution.py:35
  29.5 5.6 %collective-permute-start.1 = (bf16[256,768]{1,0:T(8,128)(2,1)S(1)}, bf16[256,768]{1,0:T(8,128)(2,1)S(1)}, u32[]{:S(2)}, u32[]{:S(2)}) collective-permute-start(bf16[256,768]{1,0:T(8,128)(2,1)S(1)} %pad_maximum_fusion.1), channel_id=1, source_target_pairs={{0,4},{1,5},{2,6},{3,7},{4,0},{5,1},{6,2},{7,3},{8,12},{9,13},{10,... | collective-permute-start | bytes 1179656 | tf_op jit(solution)/shard_map/ppermute | solution.py:35
  35.1 10.0 %collective-permute-done.1 = bf16[256,768]{1,0:T(8,128)(2,1)S(1)} collective-permute-done((bf16[256,768]{1,0:T(8,128)(2,1)S(1)}, bf16[256,768]{1,0:T(8,128)(2,1)S(1)}, u32[]{:S(2)}, u32[]{:S(2)}) %collective-permute-start.1) | collective-permute-done | bytes 393248 | tf_op jit(solution)/shard_map/ppermute | solution.py:35
  47.2 13.6 %collective-permute-done.2 = bf16[256,1536]{1,0:T(8,128)(2,1)S(1)} collective-permute-done((bf16[256,1536]{1,0:T(8,128)(2,1)S(1)}, bf16[256,1536]{1,0:T(8,128)(2,1)S(1)}, u32[]{:S(2)}, u32[]{:S(2)}) %collective-permute-start.2) | collective-permute-done | bytes 786464 | tf_op jit(solution)/shard_map/ppermute | solution.py:35
  60.9 1.9 %collective-permute-start.3 = (bf16[256,3072]{1,0:T(8,128)(2,1)S(1)}, bf16[256,3072]{1,0:T(8,128)(2,1)}, u32[]{:S(2)}, u32[]{:S(2)}) collective-permute-start(bf16[256,3072]{1,0:T(8,128)(2,1)S(1)} %constant_dynamic-update-slice_fusion.xa), channel_id=1, source_target_pairs={{0,1},{1,0},{2,3},{3,2},{4,5},{5,4},{6,7},{7,6},{8,9},{9,8},{10,11... | collective-permute-start | bytes 4718600 | tf_op jit(solution)/shard_map/ppermute | solution.py:35
  67.4 15.9 %collective-permute-done.3.xb = bf16[256,3072]{1,0:T(8,128)(2,1)} collective-permute-done((bf16[256,3072]{1,0:T(8,128)(2,1)S(1)}, bf16[256,3072]{1,0:T(8,128)(2,1)}, u32[]{:S(2)}, u32[]{:S(2)}) %collective-permute-start.3) | collective-permute-done | bytes 1572896 | tf_op jit(solution)/shard_map/ppermute | solution.py:35
  83.3 3.6 %far_lowrank.1 = (bf16[64,256]{1,0:T(8,128)(2,1)}, f32[256,768]{1,0:T(8,128)}) custom-call(s32[16]{0:T(128)} %copy-done.7, bf16[256,3072]{1,0:T(8,128)(2,1)} %collective-permute-done.3.xb, bf16[64,6144]{1,0:T(8,128)(2,1)} %bitcast.47, f32[64,256]{1,0:T(8,128)} %copy-done.5, bf16[64,768]{1,0:T(8,128)(2,1)} %constant_dynamic-slice_fusion.up), custom_call_target="tpu_custom_call" | custom-call | flops 125829120 | bytes 4194304 | tf_op jit(solution)/shard_map/far_lowrank/pallas_call | solution.py:142
  86.9 11.1 %forward.1 = (bf16[256,768]{1,0:T(8,128)(2,1)}, bf16[1024,256]{1,0:T(8,128)(2,1)}, bf16[64,768]{1,0:T(8,128)(2,1)}, bf16[256,3072]{1,0:T(8,128)(2,1)}) custom-call(s32[32]{0:T(128)} %reshape.687.lies, bf16[256,3072]{1,0:T(8,128)(2,1)} %copy-done.2, bf16[256,3072]{1,0:T(8,128)(2,1)} %collective-permute-done.3.xb, ...), custom_call_target="tpu_custom_call" | custom-call | flops 3623878656 | bytes 14680064 | tf_op jit(solution)/shard_map/forward/pallas_call | solution.py:157
  98.0 2.5 %collective-permute-start.4 = (bf16[256,3072]{1,0:T(8,128)(2,1)}, bf16[256,3072]{1,0:T(8,128)(2,1)}, u32[]{:S(2)}, u32[]{:S(2)}) collective-permute-start(bf16[256,3072]{1,0:T(8,128)(2,1)} %get-tuple-element.17), channel_id=1, source_target_pairs={{0,1},{1,0},{2,3},{3,2},{4,5},{5,4},{6,7},{7,6},{8,9},{9,8},{10,11... | collective-permute-start | bytes 4718600 | tf_op jit(solution)/shard_map/ppermute | solution.py:35
  100.6 10.0 %all-to-all-start = ((bf16[16,64,256]{2,1,0:T(8,128)(2,1)}), bf16[16,64,256]{2,1,0:T(8,128)(2,1)}, u32[]{:S(2)}, u32[]{:S(2)}) async-start(bf16[16,64,256]{2,1,0:T(8,128)(2,1)} %bitcast.51), calls=%async_computation | async-start | bytes 1048576 | tf_op jit(solution)/shard_map/all_to_all | solution.py:211
  110.6 3.7 %copy-done.1 = bf16[6144,768]{1,0:T(8,128)(2,1)S(1)} copy-done((bf16[6144,768]{1,0:T(8,128)(2,1)S(1)}, bf16[6144,768]{1,0:T(8,128)(2,1)}, u32[]{:S(2)}) %copy-start.1) | copy-done | bytes 9437208
  115.3 4.1 %kept_half.1 = bf16[256,3072]{1,0:T(8,128)(2,1)S(1)} custom-call(s32[32]{0:T(128)S(1)} %copy-done.6, bf16[256,768]{1,0:T(8,128)(2,1)S(1)} %copy-done.4, bf16[6144,768]{1,0:T(8,128)(2,1)S(1)} %copy-done.1), custom_call_target="tpu_custom_call" | custom-call | flops 1207959552 | bytes 7340032 | tf_op jit(solution)/shard_map/kept_half/pallas_call | solution.py:192
  119.4 5.8 %collective-permute-done.4 = bf16[256,3072]{1,0:T(8,128)(2,1)} collective-permute-done((bf16[256,3072]{1,0:T(8,128)(2,1)}, bf16[256,3072]{1,0:T(8,128)(2,1)}, u32[]{:S(2)}, u32[]{:S(2)}) %collective-permute-start.4) | collective-permute-done | bytes 1572896 | tf_op jit(solution)/shard_map/ppermute | solution.py:35
  125.2 2.3 %add_convert_fusion = bf16[256,1536]{1,0:T(8,128)(2,1)} fusion(bf16[256,3072]{1,0:T(8,128)(2,1)} %collective-permute-done.4, bf16[256,3072]{1,0:T(8,128)(2,1)S(1)} %kept_half.1), kind=kLoop, calls=%fused_computation | loop fusion | flops 1572864 | bytes 2359296 | tf_op jit(solution)/shard_map/convert_element_type | solution.py:258
  127.5 2.2 %collective-permute-start.5 = (bf16[256,1536]{1,0:T(8,128)(2,1)}, bf16[256,1536]{1,0:T(8,128)(2,1)}, u32[]{:S(2)}, u32[]{:S(2)}) collective-permute-start(bf16[256,1536]{1,0:T(8,128)(2,1)} %add_convert_fusion), channel_id=1, source_target_pairs={{0,3},{1,2},{2,1},{3,0},{4,7},{5,6},{6,5},{7,4},{8,11},{9,10},{10,... | collective-permute-start | bytes 2359304 | tf_op jit(solution)/shard_map/ppermute | solution.py:35
  131.9 11.2 %all-to-all-start.1 = ((bf16[32,8,384]{2,1,0:T(8,128)(2,1)}), bf16[32,8,384]{2,1,0:T(8,128)(2,1)S(1)}, u32[]{:S(2)}, u32[]{:S(2)}) async-start(bf16[32,8,384]{2,1,0:T(8,128)(2,1)} %maximum_bitcast_fusion), calls=%async_computation.1 | async-start | bytes 393216 | tf_op jit(solution)/shard_map/all_to_all | solution.py:211
  143.2 2.7 %add_convert_fusion.1 = (bf16[256,768]{1,0:T(8,128)(2,1)}, f32[256,768]{1,0:T(8,128)}) fusion(bf16[256,1536]{1,0:T(8,128)(2,1)} %collective-permute-done.5, bf16[256,3072]{1,0:T(8,128)(2,1)} %collective-permute-done.4, bf16[256,3072]{1,0:T(8,128)(2,1)S(1)} %kept_half.1), kind=kLoop, calls=%fused_computation.3 | loop fusion | flops 2162688 | bytes 3538944 | tf_op jit(solution)/shard_map/convert_element_type | solution.py:270
  145.8 3.8 %collective-permute-start.6 = (bf16[256,768]{1,0:T(8,128)(2,1)}, bf16[256,768]{1,0:T(8,128)(2,1)S(1)}, u32[]{:S(2)}, u32[]{:S(2)}) collective-permute-start(bf16[256,768]{1,0:T(8,128)(2,1)} %get-tuple-element.27), channel_id=1, source_target_pairs={{0,4},{1,5},{2,6},{3,7},{4,0},{5,1},{6,2},{7,3},{8,12},{9,13},{10,... | collective-permute-start | bytes 1179656 | tf_op jit(solution)/shard_map/ppermute | solution.py:35
  149.7 4.4 %all-to-all-done.1 = bf16[32,8,384]{2,1,0:T(8,128)(2,1)S(1)} async-done(((bf16[32,8,384]{2,1,0:T(8,128)(2,1)}), bf16[32,8,384]{2,1,0:T(8,128)(2,1)S(1)}, u32[]{:S(2)}, u32[]{:S(2)}) %all-to-all-start.1) | async-done | bytes 196640 | tf_op jit(solution)/shard_map/all_to_all | solution.py:211
  154.8 8.0 %all-to-all-start.2 = ((bf16[32,8,384]{2,1,0:T(8,128)(2,1)}), bf16[32,8,384]{2,1,0:T(8,128)(2,1)S(1)}, u32[]{:S(2)}, u32[]{:S(2)}) async-start(bf16[32,8,384]{2,1,0:T(8,128)(2,1)} %broadcast_in_dim.10), calls=%async_computation.2 | async-start | bytes 393216 | tf_op jit(solution)/shard_map/all_to_all | solution.py:211
  164.5 6.5 %collective-permute-start.7 = (bf16[256,384]{1,0:T(8,128)(2,1)}, bf16[256,384]{1,0:T(8,128)(2,1)S(1)}, u32[]{:S(2)}, u32[]{:S(2)}) collective-permute-start(bf16[256,384]{1,0:T(8,128)(2,1)} %fusion), channel_id=1, source_target_pairs={{0,12},{1,13},{2,14},{3,15},{4,8},{5,9},{6,10},{7,11},{8,4},{9,5},... | collective-permute-start | bytes 589832 | tf_op jit(solution)/shard_map/ppermute | solution.py:35
  173.7 3.0 %collective-permute-done.7 = bf16[256,384]{1,0:T(8,128)(2,1)S(1)} collective-permute-done((bf16[256,384]{1,0:T(8,128)(2,1)}, bf16[256,384]{1,0:T(8,128)(2,1)S(1)}, u32[]{:S(2)}, u32[]{:S(2)}) %collective-permute-start.7) | collective-permute-done | bytes 196640 | tf_op jit(solution)/shard_map/ppermute | solution.py:35
  (58 shorter events, 17.1 us)
Async XLA Ops:
  7.2 56.7 %copy-start = (bf16[64,12288]{1,0:T(8,128)(2,1)S(1)}, bf16[64,12288]{1,0:T(8,128)(2,1)}, u32[]{:S(2)}) copy-start(bf16[64,12288]{1,0:T(8,128)(2,1)} %param.8) | copy-start | bytes 4718596
  7.2 22.3 %copy-start.9 = (bf16[256,384]{1,0:T(8,128)(2,1)S(1)}, bf16[256,384]{1,0:T(8,128)(2,1)}, u32[]{:S(2)}) copy-start(bf16[256,384]{1,0:T(8,128)(2,1)} %param.5) | copy-start | bytes 589828
  7.2 79.8 %all-gather.2.cloned.1.call-start = ((), (), s32[]{:S(2)}) async-start(), calls=%async_computation.3 | async-start | bytes 10027008 | tf_op jit(solution)/shard_map/all_gather | solution.py:239
  18.6 10.9 %collective-permute-start = (bf16[256,384]{1,0:T(8,128)(2,1)}, bf16[256,384]{1,0:T(8,128)(2,1)S(1)}, u32[]{:S(2)}, u32[]{:S(2)}) collective-permute-start(bf16[256,384]{1,0:T(8,128)(2,1)} %param.5), channel_id=1, source_target_pairs={{0,12},{1,13},{2,14},{3,15},{4,8},{5,9},{6,10},{7,11},{8,4},{9,5},... | collective-permute-start | bytes 589832 | tf_op jit(solution)/shard_map/ppermute | solution.py:35
  29.5 15.6 %collective-permute-start.1 = (bf16[256,768]{1,0:T(8,128)(2,1)S(1)}, bf16[256,768]{1,0:T(8,128)(2,1)S(1)}, u32[]{:S(2)}, u32[]{:S(2)}) collective-permute-start(bf16[256,768]{1,0:T(8,128)(2,1)S(1)} %pad_maximum_fusion.1), channel_id=1, source_target_pairs={{0,4},{1,5},{2,6},{3,7},{4,0},{5,1},{6,2},{7,3},{8,12},{9,13},{10,... | collective-permute-start | bytes 1179656 | tf_op jit(solution)/shard_map/ppermute | solution.py:35
  45.1 15.7 %collective-permute-start.2 = (bf16[256,1536]{1,0:T(8,128)(2,1)S(1)}, bf16[256,1536]{1,0:T(8,128)(2,1)S(1)}, u32[]{:S(2)}, u32[]{:S(2)}) collective-permute-start(bf16[256,1536]{1,0:T(8,128)(2,1)S(1)} %pad_maximum_fusion), channel_id=1, source_target_pairs={{0,3},{1,2},{2,1},{3,0},{4,7},{5,6},{6,5},{7,4},{8,11},{9,10},{10,... | collective-permute-start | bytes 2359304 | tf_op jit(solution)/shard_map/ppermute | solution.py:35
  60.9 26.0 %copy-start.2 = (bf16[256,3072]{1,0:T(8,128)(2,1)}, bf16[256,3072]{1,0:T(8,128)(2,1)S(1)}, u32[]{:S(2)}) copy-start(bf16[256,3072]{1,0:T(8,128)(2,1)S(1)} %constant_dynamic-update-slice_fusion.xa) | copy-start | bytes 4718596
  60.9 22.4 %collective-permute-start.3 = (bf16[256,3072]{1,0:T(8,128)(2,1)S(1)}, bf16[256,3072]{1,0:T(8,128)(2,1)}, u32[]{:S(2)}, u32[]{:S(2)}) collective-permute-start(bf16[256,3072]{1,0:T(8,128)(2,1)S(1)} %constant_dynamic-update-slice_fusion.xa), channel_id=1, source_target_pairs={{0,1},{1,0},{2,3},{3,2},{4,5},{5,4},{6,7},{7,6},{8,9},{9,8},{10,11... | collective-permute-start | bytes 4718600 | tf_op jit(solution)/shard_map/ppermute | solution.py:35
  63.8 19.5 %copy-start.7 = (s32[16]{0:T(128)}, s32[16]{0:T(128)S(1)}, u32[]{:S(2)}) copy-start(s32[16]{0:T(128)S(1)} %stack.124.table) | copy-start | bytes 196
  64.5 1.1 copy-start.3
  66.8 0.6 copy-start.5
  86.9 23.7 %copy-start.6 = (s32[32]{0:T(128)S(1)}, s32[32]{0:T(128)}, u32[]{:S(2)}) copy-start(s32[32]{0:T(128)} %reshape.687.lies) | copy-start | bytes 388
  98.0 27.2 %collective-permute-start.4 = (bf16[256,3072]{1,0:T(8,128)(2,1)}, bf16[256,3072]{1,0:T(8,128)(2,1)}, u32[]{:S(2)}, u32[]{:S(2)}) collective-permute-start(bf16[256,3072]{1,0:T(8,128)(2,1)} %get-tuple-element.17), channel_id=1, source_target_pairs={{0,1},{1,0},{2,3},{3,2},{4,5},{5,4},{6,7},{7,6},{8,9},{9,8},{10,11... | collective-permute-start | bytes 4718600 | tf_op jit(solution)/shard_map/ppermute | solution.py:35
  100.6 29.3 %all-to-all-start = ((bf16[16,64,256]{2,1,0:T(8,128)(2,1)}), bf16[16,64,256]{2,1,0:T(8,128)(2,1)}, u32[]{:S(2)}, u32[]{:S(2)}) async-start(bf16[16,64,256]{2,1,0:T(8,128)(2,1)} %bitcast.51), calls=%async_computation | async-start | bytes 1048576 | tf_op jit(solution)/shard_map/all_to_all | solution.py:211
  110.6 3.7 %copy-start.1 = (bf16[6144,768]{1,0:T(8,128)(2,1)S(1)}, bf16[6144,768]{1,0:T(8,128)(2,1)}, u32[]{:S(2)}) copy-start(bf16[6144,768]{1,0:T(8,128)(2,1)} %all-gather.2.cloned.1.call-done.w) | copy-start | bytes 28311556
  114.3 1.0 copy-start.4
  119.4 10.4 %copy-start.11 = (bf16[64,768]{1,0:T(8,128)(2,1)S(1)}, bf16[64,768]{1,0:T(8,128)(2,1)}, u32[]{:S(2)}) copy-start(bf16[64,768]{1,0:T(8,128)(2,1)} %get-tuple-element.20) | copy-start | bytes 294916
  127.5 15.7 %collective-permute-start.5 = (bf16[256,1536]{1,0:T(8,128)(2,1)}, bf16[256,1536]{1,0:T(8,128)(2,1)}, u32[]{:S(2)}, u32[]{:S(2)}) collective-permute-start(bf16[256,1536]{1,0:T(8,128)(2,1)} %add_convert_fusion), channel_id=1, source_target_pairs={{0,3},{1,2},{2,1},{3,0},{4,7},{5,6},{6,5},{7,4},{8,11},{9,10},{10,... | collective-permute-start | bytes 2359304 | tf_op jit(solution)/shard_map/ppermute | solution.py:35
  131.0 1.0 copy-start.10
  131.9 22.1 %all-to-all-start.1 = ((bf16[32,8,384]{2,1,0:T(8,128)(2,1)}), bf16[32,8,384]{2,1,0:T(8,128)(2,1)S(1)}, u32[]{:S(2)}, u32[]{:S(2)}) async-start(bf16[32,8,384]{2,1,0:T(8,128)(2,1)} %maximum_bitcast_fusion), calls=%async_computation.1 | async-start | bytes 393216 | tf_op jit(solution)/shard_map/all_to_all | solution.py:211
  145.8 25.2 %copy-start.8 = (f32[256,768]{1,0:T(8,128)S(1)}, f32[256,768]{1,0:T(8,128)}, u32[]{:S(2)}) copy-start(f32[256,768]{1,0:T(8,128)} %get-tuple-element.28) | copy-start | bytes 2359300
  145.8 17.0 %collective-permute-start.6 = (bf16[256,768]{1,0:T(8,128)(2,1)}, bf16[256,768]{1,0:T(8,128)(2,1)S(1)}, u32[]{:S(2)}, u32[]{:S(2)}) collective-permute-start(bf16[256,768]{1,0:T(8,128)(2,1)} %get-tuple-element.27), channel_id=1, source_target_pairs={{0,4},{1,5},{2,6},{3,7},{4,0},{5,1},{6,2},{7,3},{8,12},{9,13},{10,... | collective-permute-start | bytes 1179656 | tf_op jit(solution)/shard_map/ppermute | solution.py:35
  154.8 18.9 %all-to-all-start.2 = ((bf16[32,8,384]{2,1,0:T(8,128)(2,1)}), bf16[32,8,384]{2,1,0:T(8,128)(2,1)S(1)}, u32[]{:S(2)}, u32[]{:S(2)}) async-start(bf16[32,8,384]{2,1,0:T(8,128)(2,1)} %broadcast_in_dim.10), calls=%async_computation.2 | async-start | bytes 393216 | tf_op jit(solution)/shard_map/all_to_all | solution.py:211
  164.5 12.1 %collective-permute-start.7 = (bf16[256,384]{1,0:T(8,128)(2,1)}, bf16[256,384]{1,0:T(8,128)(2,1)S(1)}, u32[]{:S(2)}, u32[]{:S(2)}) collective-permute-start(bf16[256,384]{1,0:T(8,128)(2,1)} %fusion), channel_id=1, source_target_pairs={{0,12},{1,13},{2,14},{3,15},{4,8},{5,9},{6,10},{7,11},{8,4},{9,5},... | collective-permute-start | bytes 589832 | tf_op jit(solution)/shard_map/ppermute | solution.py:35
Sparse Core Ops, SparseCore 0:
  18.7 67.9 all-gather.1

commit v11 on v7

--- a/solution.py
+++ b/solution.py
@@ -144,7 +144,7 @@
         out_shape=(jax.ShapeDtypeStruct((rank, rows), bf16), jax.ShapeDtypeStruct((rows, hidden), f32)),
         in_specs=[SMEM, VMEM, VMEM, VMEM, VMEM],
         out_specs=(VMEM, VMEM),
-        compiler_params=pltpu.CompilerParams(vmem_limit_bytes=8 * 2**20),
+        compiler_params=pltpu.CompilerParams(vmem_limit_bytes=56 * 2**20),
         cost_estimate=pl.CostEstimate(
             flops=2 * rows * rank * (xb.shape[1] + hidden), bytes_accessed=4 * 2**20, transcendentals=0
         ),
@@ -195,7 +195,7 @@
         in_specs=[SMEM, VMEM, HBM],
         out_specs=VMEM,
         scratch_shapes=[pltpu.VMEM((half, hidden), bf16), pltpu.SemaphoreType.DMA((16,))],
-        compiler_params=pltpu.CompilerParams(vmem_limit_bytes=16 * 2**20),
+        compiler_params=pltpu.CompilerParams(vmem_limit_bytes=56 * 2**20),
         cost_estimate=pl.CostEstimate(
             flops=2 * rows * half * hidden, bytes_accessed=7 * 2**20, transcendentals=0
         ),
@@ -276,8 +276,7 @@
     over_last = y_first(to_y)
     down_rows = lax.dynamic_slice_in_dim(adapter_down, model_index * width, width, 0)
     own = own + contract(rank_grad, down_rows, 0, 1)
-    own, grads = lax.optimization_barrier((own, grads))
-    own, over_last = lax.optimization_barrier((own, over_last))
+    own, over_last, grads = lax.optimization_barrier((own, over_last, grads))
     normed_grad = (own + widen(over_last)).astype(bf16)
     up_grad = jnp.concatenate([grads[:rank], grads[rank : 2 * rank]], axis=1)
     down_grad = grads[2 * rank : 3 * rank].T

time: 195 us -> 188 us (0.964); the launches traced: 193 us -> 184 us
  waiting for transfers between devices: 71.6 us -> 62.1 us
  local copies, waits for them, and re-layouts: 11.2 us -> 6.22 us
  Pallas kernels: 18.8 us -> 21.8 us
  starting transfers between devices: 56.3 us -> 58.6 us
    all_to_all x3, waiting for transfers between devices: 12.9 us -> 6.6 us  [exchange(): return lax.all_to_all(value, axis, 0, 0, tiled=True)]
    unnamed x27 -> x21, local copies, waits for them, and re-layouts: 8.65 us -> 3.06 us
    ppermute x8, waiting for transfers between devices: 58.7 us -> 55.5 us  [send(): return lax.ppermute(value, ('fsdp', 'mp'), pairs)]
    ppermute x8, starting transfers between devices: 26.6 us -> 29.4 us  [send(): return lax.ppermute(value, ('fsdp', 'mp'), pairs)]
  transfers between devices with their start and end apart: 12 -> 12, of which waited for: 8 -> 8; matrix products, arithmetic and copies ran while one was open for 6% -> 6% of each run, Pallas kernels for 4% -> 6%
where the time goes in v11:
time: 188 us; the launch traced here: 184 us
  waiting for transfers between devices  62.1 us (33%)
  starting transfers between devices  58.6 us (31%)
  Pallas kernels  21.8 us (12%)
  between operations  14.4 us (8%)
  blocking collectives  11.3 us (6%)
  other arithmetic  8.75 us (5%)
  local copies, waits for them, and re-layouts  6.22 us (3%)
    ppermute x8, waiting for transfers between devices, send(): return lax.ppermute(value, ('fsdp', 'mp'), pairs)  55.5 us
    ppermute x8, starting transfers between devices, send(): return lax.ppermute(value, ('fsdp', 'mp'), pairs)  29.4 us
    all_to_all x3, starting transfers between devices, exchange(): return lax.all_to_all(value, axis, 0, 0, tiled=True)  29.2 us
    all_gather x1, blocking collectives, body(): lax.all_gather(up_weight, 'fsdp', axis=0, tiled=True, axis_index_groups=P...  11.3 us
    pallas_call x1, Pallas kernels, forward(): pl.pallas_call(main_kernel, out_shape=(jax.ShapeDtypeStruct((rows, hidden...  11.1 us
    all_to_all x3, waiting for transfers between devices, exchange(): return lax.all_to_all(value, axis, 0, 0, tiled=True)  6.6 us
    pallas_call x1, Pallas kernels, kept_half(): pl.pallas_call(kept_kernel, out_shape=jax.ShapeDtypeStruct((rows, half),...  6 us
  transfers between devices with their start and end apart: 12, of which 8 were waited for; matrix products, arithmetic and copies ran while one was open for 6% of the time, Pallas kernels for 6%

profile of v11, /device:TPU:6, one launch (start us, length us, event | category | flops | bytes accessed | tf_op | source)
XLA Modules:
  0.0 184.5 jit_solution(10167131026293222176)
XLA Ops:
  7.2 11.3 %all_gather.6 = bf16[384,768]{1,0:T(8,128)(2,1)} all-gather(bf16[192,768]{1,0:T(8,128)(2,1)} %param.6), channel_id=1, replica_groups={{0,32},{16,48},{64,96},{80,112},{128,160},{144,176},{192,224},{208,240}..., dimensions={0}, use_global_device_ids=true | all-gather | bytes 884736 | tf_op jit(solution)/shard_map/all_gather | solution.py:234
  18.6 5.3 %collective-permute-start = (bf16[256,384]{1,0:T(8,128)(2,1)}, bf16[256,384]{1,0:T(8,128)(2,1)S(1)}, u32[]{:S(2)}, u32[]{:S(2)}) collective-permute-start(bf16[256,384]{1,0:T(8,128)(2,1)} %param.5), channel_id=1, source_target_pairs={{0,12},{1,13},{2,14},{3,15},{4,8},{5,9},{6,10},{7,11},{8,4},{9,5},... | collective-permute-start | bytes 589832 | tf_op jit(solution)/shard_map/ppermute | solution.py:35
  23.9 5.6 %collective-permute-done = bf16[256,384]{1,0:T(8,128)(2,1)S(1)} collective-permute-done((bf16[256,384]{1,0:T(8,128)(2,1)}, bf16[256,384]{1,0:T(8,128)(2,1)S(1)}, u32[]{:S(2)}, u32[]{:S(2)}) %collective-permute-start) | collective-permute-done | bytes 196640 | tf_op jit(solution)/shard_map/ppermute | solution.py:35
  29.5 5.6 %collective-permute-start.1 = (bf16[256,768]{1,0:T(8,128)(2,1)S(1)}, bf16[256,768]{1,0:T(8,128)(2,1)S(1)}, u32[]{:S(2)}, u32[]{:S(2)}) collective-permute-start(bf16[256,768]{1,0:T(8,128)(2,1)S(1)} %pad_maximum_fusion.1), channel_id=1, source_target_pairs={{0,4},{1,5},{2,6},{3,7},{4,0},{5,1},{6,2},{7,3},{8,12},{9,13},{10,... | collective-permute-start | bytes 1179656 | tf_op jit(solution)/shard_map/ppermute | solution.py:35
  35.1 10.0 %collective-permute-done.1 = bf16[256,768]{1,0:T(8,128)(2,1)S(1)} collective-permute-done((bf16[256,768]{1,0:T(8,128)(2,1)S(1)}, bf16[256,768]{1,0:T(8,128)(2,1)S(1)}, u32[]{:S(2)}, u32[]{:S(2)}) %collective-permute-start.1) | collective-permute-done | bytes 393248 | tf_op jit(solution)/shard_map/ppermute | solution.py:35
  45.1 1.9 %collective-permute-start.2 = (bf16[256,1536]{1,0:T(8,128)(2,1)S(1)}, bf16[256,1536]{1,0:T(8,128)(2,1)S(1)}, u32[]{:S(2)}, u32[]{:S(2)}) collective-permute-start(bf16[256,1536]{1,0:T(8,128)(2,1)S(1)} %pad_maximum_fusion), channel_id=1, source_target_pairs={{0,3},{1,2},{2,1},{3,0},{4,7},{5,6},{6,5},{7,4},{8,11},{9,10},{10,... | collective-permute-start | bytes 2359304 | tf_op jit(solution)/shard_map/ppermute | solution.py:35
  47.2 13.6 %collective-permute-done.2 = bf16[256,1536]{1,0:T(8,128)(2,1)S(1)} collective-permute-done((bf16[256,1536]{1,0:T(8,128)(2,1)S(1)}, bf16[256,1536]{1,0:T(8,128)(2,1)S(1)}, u32[]{:S(2)}, u32[]{:S(2)}) %collective-permute-start.2) | collective-permute-done | bytes 786464 | tf_op jit(solution)/shard_map/ppermute | solution.py:35
  60.9 1.9 %collective-permute-start.3 = (bf16[256,3072]{1,0:T(8,128)(2,1)S(1)}, bf16[256,3072]{1,0:T(8,128)(2,1)}, u32[]{:S(2)}, u32[]{:S(2)}) collective-permute-start(bf16[256,3072]{1,0:T(8,128)(2,1)S(1)} %constant_dynamic-update-slice_fusion.xa), channel_id=1, source_target_pairs={{0,1},{1,0},{2,3},{3,2},{4,5},{5,4},{6,7},{7,6},{8,9},{9,8},{10,11... | collective-permute-start | bytes 4718600 | tf_op jit(solution)/shard_map/ppermute | solution.py:35
  67.4 15.9 %collective-permute-done.3.xb = bf16[256,3072]{1,0:T(8,128)(2,1)} collective-permute-done((bf16[256,3072]{1,0:T(8,128)(2,1)S(1)}, bf16[256,3072]{1,0:T(8,128)(2,1)}, u32[]{:S(2)}, u32[]{:S(2)}) %collective-permute-start.3) | collective-permute-done | bytes 1572896 | tf_op jit(solution)/shard_map/ppermute | solution.py:35
  83.3 3.6 %far_lowrank.1 = (bf16[64,256]{1,0:T(8,128)(2,1)}, f32[256,768]{1,0:T(8,128)}) custom-call(s32[16]{0:T(128)} %copy-done.4, bf16[256,3072]{1,0:T(8,128)(2,1)} %collective-permute-done.3.xb, bf16[64,6144]{1,0:T(8,128)(2,1)} %bitcast.47, f32[64,256]{1,0:T(8,128)} %copy-done.3, bf16[64,768]{1,0:T(8,128)(2,1)} %constant_dynamic-slice_fusion.up), custom_call_target="tpu_custom_call" | custom-call | flops 125829120 | bytes 4194304 | tf_op jit(solution)/shard_map/far_lowrank/pallas_call | solution.py:142
  87.0 11.1 %forward.1 = (bf16[256,768]{1,0:T(8,128)(2,1)}, bf16[1024,256]{1,0:T(8,128)(2,1)}, bf16[64,768]{1,0:T(8,128)(2,1)}, bf16[256,3072]{1,0:T(8,128)(2,1)}) custom-call(s32[32]{0:T(128)} %reshape.687.lies, bf16[256,3072]{1,0:T(8,128)(2,1)} %copy-done.1, bf16[256,3072]{1,0:T(8,128)(2,1)} %collective-permute-done.3.xb, ...), custom_call_target="tpu_custom_call" | custom-call | flops 3623878656 | bytes 14680064 | tf_op jit(solution)/shard_map/forward/pallas_call | solution.py:157
  98.0 2.5 %collective-permute-start.4 = (bf16[256,3072]{1,0:T(8,128)(2,1)}, bf16[256,3072]{1,0:T(8,128)(2,1)}, u32[]{:S(2)}, u32[]{:S(2)}) collective-permute-start(bf16[256,3072]{1,0:T(8,128)(2,1)} %get-tuple-element.17), channel_id=1, source_target_pairs={{0,1},{1,0},{2,3},{3,2},{4,5},{5,4},{6,7},{7,6},{8,9},{9,8},{10,11... | collective-permute-start | bytes 4718600 | tf_op jit(solution)/shard_map/ppermute | solution.py:35
  100.6 10.0 %all-to-all-start = ((bf16[16,64,256]{2,1,0:T(8,128)(2,1)}), bf16[16,64,256]{2,1,0:T(8,128)(2,1)}, u32[]{:S(2)}, u32[]{:S(2)}) async-start(bf16[16,64,256]{2,1,0:T(8,128)(2,1)} %bitcast.51), calls=%async_computation | async-start | bytes 1048576 | tf_op jit(solution)/shard_map/all_to_all | solution.py:211
  110.6 6.0 %kept_half.1 = bf16[256,3072]{1,0:T(8,128)(2,1)} custom-call(s32[32]{0:T(128)} %reshape.687.lies, bf16[256,768]{1,0:T(8,128)(2,1)} %get-tuple-element.16.slope, bf16[6144,768]{1,0:T(8,128)(2,1)} %all-gather.2.cloned.1.call-done.w), custom_call_target="tpu_custom_call" | custom-call | flops 1207959552 | bytes 7340032 | tf_op jit(solution)/shard_map/kept_half/pallas_call | solution.py:192
  116.6 8.6 %collective-permute-done.4 = bf16[256,3072]{1,0:T(8,128)(2,1)} collective-permute-done((bf16[256,3072]{1,0:T(8,128)(2,1)}, bf16[256,3072]{1,0:T(8,128)(2,1)}, u32[]{:S(2)}, u32[]{:S(2)}) %collective-permute-start.4) | collective-permute-done | bytes 1572896 | tf_op jit(solution)/shard_map/ppermute | solution.py:35
  125.2 2.5 %add_convert_fusion = bf16[256,1536]{1,0:T(8,128)(2,1)} fusion(bf16[256,3072]{1,0:T(8,128)(2,1)} %collective-permute-done.4, bf16[256,3072]{1,0:T(8,128)(2,1)} %kept_half.1), kind=kLoop, calls=%fused_computation.1 | loop fusion | flops 1572864 | bytes 2359296 | tf_op jit(solution)/shard_map/convert_element_type | solution.py:255
  127.7 2.2 %collective-permute-start.5 = (bf16[256,1536]{1,0:T(8,128)(2,1)}, bf16[256,1536]{1,0:T(8,128)(2,1)}, u32[]{:S(2)}, u32[]{:S(2)}) collective-permute-start(bf16[256,1536]{1,0:T(8,128)(2,1)} %add_convert_fusion), channel_id=1, source_target_pairs={{0,3},{1,2},{2,1},{3,0},{4,7},{5,6},{6,5},{7,4},{8,11},{9,10},{10,... | collective-permute-start | bytes 2359304 | tf_op jit(solution)/shard_map/ppermute | solution.py:35
  132.1 11.2 %all-to-all-start.1 = ((bf16[32,8,384]{2,1,0:T(8,128)(2,1)}), bf16[32,8,384]{2,1,0:T(8,128)(2,1)S(1)}, u32[]{:S(2)}, u32[]{:S(2)}) async-start(bf16[32,8,384]{2,1,0:T(8,128)(2,1)} %maximum_bitcast_fusion), calls=%async_computation.1 | async-start | bytes 393216 | tf_op jit(solution)/shard_map/all_to_all | solution.py:211
  146.3 3.7 %collective-permute-start.6 = (bf16[256,768]{1,0:T(8,128)(2,1)S(1)}, bf16[256,768]{1,0:T(8,128)(2,1)S(1)}, u32[]{:S(2)}, u32[]{:S(2)}) collective-permute-start(bf16[256,768]{1,0:T(8,128)(2,1)S(1)} %slice.71), channel_id=1, source_target_pairs={{0,4},{1,5},{2,6},{3,7},{4,0},{5,1},{6,2},{7,3},{8,12},{9,13},{10,... | collective-permute-start | bytes 1179656 | tf_op jit(solution)/shard_map/ppermute | solution.py:35
  150.0 4.3 %all-to-all-done.1 = bf16[32,8,384]{2,1,0:T(8,128)(2,1)S(1)} async-done(((bf16[32,8,384]{2,1,0:T(8,128)(2,1)}), bf16[32,8,384]{2,1,0:T(8,128)(2,1)S(1)}, u32[]{:S(2)}, u32[]{:S(2)}) %all-to-all-start.1) | async-done | bytes 196640 | tf_op jit(solution)/shard_map/all_to_all | solution.py:211
  155.0 7.9 %all-to-all-start.2 = ((bf16[32,8,384]{2,1,0:T(8,128)(2,1)}), bf16[32,8,384]{2,1,0:T(8,128)(2,1)S(1)}, u32[]{:S(2)}, u32[]{:S(2)}) async-start(bf16[32,8,384]{2,1,0:T(8,128)(2,1)} %broadcast_in_dim.10), calls=%async_computation.2 | async-start | bytes 393216 | tf_op jit(solution)/shard_map/all_to_all | solution.py:211
  164.1 6.3 %collective-permute-start.7 = (bf16[256,384]{1,0:T(8,128)(2,1)S(1)}, bf16[256,384]{1,0:T(8,128)(2,1)S(1)}, u32[]{:S(2)}, u32[]{:S(2)}) collective-permute-start(bf16[256,384]{1,0:T(8,128)(2,1)S(1)} %slice.72), channel_id=1, source_target_pairs={{0,12},{1,13},{2,14},{3,15},{4,8},{5,9},{6,10},{7,11},{8,4},{9,5},... | collective-permute-start | bytes 589832 | tf_op jit(solution)/shard_map/ppermute | solution.py:35
  171.5 2.3 %all-to-all-done.2 = bf16[32,8,384]{2,1,0:T(8,128)(2,1)S(1)} async-done(((bf16[32,8,384]{2,1,0:T(8,128)(2,1)}), bf16[32,8,384]{2,1,0:T(8,128)(2,1)S(1)}, u32[]{:S(2)}, u32[]{:S(2)}) %all-to-all-start.2) | async-done | bytes 196640 | tf_op jit(solution)/shard_map/all_to_all | solution.py:211
  173.8 1.8 collective-permute-done.7
  (54 shorter events, 14.9 us)
Async XLA Ops:
  7.2 56.6 %copy-start = (bf16[64,12288]{1,0:T(8,128)(2,1)S(1)}, bf16[64,12288]{1,0:T(8,128)(2,1)}, u32[]{:S(2)}) copy-start(bf16[64,12288]{1,0:T(8,128)(2,1)} %param.8) | copy-start | bytes 4718596
  7.2 22.3 %copy-start.7 = (bf16[256,384]{1,0:T(8,128)(2,1)S(1)}, bf16[256,384]{1,0:T(8,128)(2,1)}, u32[]{:S(2)}) copy-start(bf16[256,384]{1,0:T(8,128)(2,1)} %param.5) | copy-start | bytes 589828
  7.2 79.8 %all-gather.2.cloned.1.call-start = ((), (), s32[]{:S(2)}) async-start(), calls=%async_computation.3 | async-start | bytes 10027008 | tf_op jit(solution)/shard_map/all_gather | solution.py:235
  18.6 10.9 %collective-permute-start = (bf16[256,384]{1,0:T(8,128)(2,1)}, bf16[256,384]{1,0:T(8,128)(2,1)S(1)}, u32[]{:S(2)}, u32[]{:S(2)}) collective-permute-start(bf16[256,384]{1,0:T(8,128)(2,1)} %param.5), channel_id=1, source_target_pairs={{0,12},{1,13},{2,14},{3,15},{4,8},{5,9},{6,10},{7,11},{8,4},{9,5},... | collective-permute-start | bytes 589832 | tf_op jit(solution)/shard_map/ppermute | solution.py:35
  29.5 15.5 %collective-permute-start.1 = (bf16[256,768]{1,0:T(8,128)(2,1)S(1)}, bf16[256,768]{1,0:T(8,128)(2,1)S(1)}, u32[]{:S(2)}, u32[]{:S(2)}) collective-permute-start(bf16[256,768]{1,0:T(8,128)(2,1)S(1)} %pad_maximum_fusion.1), channel_id=1, source_target_pairs={{0,4},{1,5},{2,6},{3,7},{4,0},{5,1},{6,2},{7,3},{8,12},{9,13},{10,... | collective-permute-start | bytes 1179656 | tf_op jit(solution)/shard_map/ppermute | solution.py:35
  45.1 15.6 %collective-permute-start.2 = (bf16[256,1536]{1,0:T(8,128)(2,1)S(1)}, bf16[256,1536]{1,0:T(8,128)(2,1)S(1)}, u32[]{:S(2)}, u32[]{:S(2)}) collective-permute-start(bf16[256,1536]{1,0:T(8,128)(2,1)S(1)} %pad_maximum_fusion), channel_id=1, source_target_pairs={{0,3},{1,2},{2,1},{3,0},{4,7},{5,6},{6,5},{7,4},{8,11},{9,10},{10,... | collective-permute-start | bytes 2359304 | tf_op jit(solution)/shard_map/ppermute | solution.py:35
  60.9 26.1 %copy-start.1 = (bf16[256,3072]{1,0:T(8,128)(2,1)}, bf16[256,3072]{1,0:T(8,128)(2,1)S(1)}, u32[]{:S(2)}) copy-start(bf16[256,3072]{1,0:T(8,128)(2,1)S(1)} %constant_dynamic-update-slice_fusion.xa) | copy-start | bytes 4718596
  60.9 22.4 %collective-permute-start.3 = (bf16[256,3072]{1,0:T(8,128)(2,1)S(1)}, bf16[256,3072]{1,0:T(8,128)(2,1)}, u32[]{:S(2)}, u32[]{:S(2)}) collective-permute-start(bf16[256,3072]{1,0:T(8,128)(2,1)S(1)} %constant_dynamic-update-slice_fusion.xa), channel_id=1, source_target_pairs={{0,1},{1,0},{2,3},{3,2},{4,5},{5,4},{6,7},{7,6},{8,9},{9,8},{10,11... | collective-permute-start | bytes 4718600 | tf_op jit(solution)/shard_map/ppermute | solution.py:35
  63.8 19.5 %copy-start.4 = (s32[16]{0:T(128)}, s32[16]{0:T(128)S(1)}, u32[]{:S(2)}) copy-start(s32[16]{0:T(128)S(1)} %stack.124.table) | copy-start | bytes 196
  64.5 1.1 copy-start.2
  66.8 0.6 copy-start.3
  98.0 27.2 %collective-permute-start.4 = (bf16[256,3072]{1,0:T(8,128)(2,1)}, bf16[256,3072]{1,0:T(8,128)(2,1)}, u32[]{:S(2)}, u32[]{:S(2)}) collective-permute-start(bf16[256,3072]{1,0:T(8,128)(2,1)} %get-tuple-element.17), channel_id=1, source_target_pairs={{0,1},{1,0},{2,3},{3,2},{4,5},{5,4},{6,7},{7,6},{8,9},{9,8},{10,11... | collective-permute-start | bytes 4718600 | tf_op jit(solution)/shard_map/ppermute | solution.py:35
  100.6 29.5 %all-to-all-start = ((bf16[16,64,256]{2,1,0:T(8,128)(2,1)}), bf16[16,64,256]{2,1,0:T(8,128)(2,1)}, u32[]{:S(2)}, u32[]{:S(2)}) async-start(bf16[16,64,256]{2,1,0:T(8,128)(2,1)} %bitcast.51), calls=%async_computation | async-start | bytes 1048576 | tf_op jit(solution)/shard_map/all_to_all | solution.py:211
  116.6 13.4 %copy-start.8 = (bf16[64,768]{1,0:T(8,128)(2,1)S(1)}, bf16[64,768]{1,0:T(8,128)(2,1)}, u32[]{:S(2)}) copy-start(bf16[64,768]{1,0:T(8,128)(2,1)} %get-tuple-element.20) | copy-start | bytes 294916
  116.6 26.7 %copy-start.5 = (bf16[256,3072]{1,0:T(8,128)(2,1)S(1)}, bf16[256,3072]{1,0:T(8,128)(2,1)}, u32[]{:S(2)}) copy-start(bf16[256,3072]{1,0:T(8,128)(2,1)} %kept_half.1) | copy-start | bytes 4718596
  127.7 15.6 %collective-permute-start.5 = (bf16[256,1536]{1,0:T(8,128)(2,1)}, bf16[256,1536]{1,0:T(8,128)(2,1)}, u32[]{:S(2)}, u32[]{:S(2)}) collective-permute-start(bf16[256,1536]{1,0:T(8,128)(2,1)} %add_convert_fusion), channel_id=1, source_target_pairs={{0,3},{1,2},{2,1},{3,0},{4,7},{5,6},{6,5},{7,4},{8,11},{9,10},{10,... | collective-permute-start | bytes 2359304 | tf_op jit(solution)/shard_map/ppermute | solution.py:35
  132.1 22.1 %all-to-all-start.1 = ((bf16[32,8,384]{2,1,0:T(8,128)(2,1)}), bf16[32,8,384]{2,1,0:T(8,128)(2,1)S(1)}, u32[]{:S(2)}, u32[]{:S(2)}) async-start(bf16[32,8,384]{2,1,0:T(8,128)(2,1)} %maximum_bitcast_fusion), calls=%async_computation.1 | async-start | bytes 393216 | tf_op jit(solution)/shard_map/all_to_all | solution.py:211
  145.0 1.2 copy-start.6
  146.3 16.6 %collective-permute-start.6 = (bf16[256,768]{1,0:T(8,128)(2,1)S(1)}, bf16[256,768]{1,0:T(8,128)(2,1)S(1)}, u32[]{:S(2)}, u32[]{:S(2)}) collective-permute-start(bf16[256,768]{1,0:T(8,128)(2,1)S(1)} %slice.71), channel_id=1, source_target_pairs={{0,4},{1,5},{2,6},{3,7},{4,0},{5,1},{6,2},{7,3},{8,12},{9,13},{10,... | collective-permute-start | bytes 1179656 | tf_op jit(solution)/shard_map/ppermute | solution.py:35
  155.0 18.8 %all-to-all-start.2 = ((bf16[32,8,384]{2,1,0:T(8,128)(2,1)}), bf16[32,8,384]{2,1,0:T(8,128)(2,1)S(1)}, u32[]{:S(2)}, u32[]{:S(2)}) async-start(bf16[32,8,384]{2,1,0:T(8,128)(2,1)} %broadcast_in_dim.10), calls=%async_computation.2 | async-start | bytes 393216 | tf_op jit(solution)/shard_map/all_to_all | solution.py:211
  164.1 11.5 %collective-permute-start.7 = (bf16[256,384]{1,0:T(8,128)(2,1)S(1)}, bf16[256,384]{1,0:T(8,128)(2,1)S(1)}, u32[]{:S(2)}, u32[]{:S(2)}) collective-permute-start(bf16[256,384]{1,0:T(8,128)(2,1)S(1)} %slice.72), channel_id=1, source_target_pairs={{0,12},{1,13},{2,14},{3,15},{4,8},{5,9},{6,10},{7,11},{8,4},{9,5},... | collective-permute-start | bytes 589832 | tf_op jit(solution)/shard_map/ppermute | solution.py:35
Sparse Core Ops, SparseCore 0:
  18.7 67.9 all-gather.1
